TPU v7x, 256 devices: a whole 4x4x8 slice. The times are simulated.
256 devices in a mesh: ctx: 32 (over y, z_hi, x), head: 8 (over z_lo, core).
Axes of the slice: x: 4, y: 4, z: 8 (z_hi: 2, z_lo: 4; z = z_hi * 4 + z_lo), core: 2. Of those that a mesh axis runs over, the one named last changes fastest.
Arguments:
- queries: bfloat16 [8192, 1024], P('ctx', 'head'), may hold values from -10 to 10
- keys: bfloat16 [8192, 128], P('ctx'), may hold values from -6 to 6
- values: bfloat16 [8192, 128], P('ctx'), may hold values from -6 to 6
- doc_lengths: int32 [4], replicated, may hold values from 1 to 6144, 8192 in all
Outputs:
- attn_rows: bfloat16 [8192, 1024], P('ctx', 'head')
- col_scores: float32 [8192], P(('ctx', 'head'))
Inputs may be any that keep to these rules, and one draw needn't show every extreme that they name: `doc_lengths`: the 4 lengths sum to 8192 and the longest is exactly 6144.
All inputs are finite; a program needn't handle non-finite values.
Results may differ from a plain program's by a relative error of at most 0.0075.
Values may be sent and summed in bfloat16 or wider, within the bound.
No kernel may reach another device: no remote copies, remote signals or barrier semaphores. Data moves between devices by JAX's collectives and lax.ppermute only.
A program may use at most 64 MiB of HBM per device.

v0:
```python
import math

import jax
import jax.numpy as jnp
from jax import lax
from jax.sharding import PartitionSpec as P

HD = 128
HEADS = 8


def doc_index(doc_lengths, positions):
    doc_ends = jnp.cumsum(doc_lengths)
    return jnp.sum((positions[:, None] >= doc_ends[None, :]).astype(jnp.int32), axis=1)


def body(queries, keys, values, doc_lengths):
    tok_rows = queries.shape[0]
    head_count = queries.shape[1] // HD
    inv_root = 1.0 / math.sqrt(HD)
    ctx_size = lax.axis_size("ctx")
    all_tokens = tok_rows * ctx_size
    ctx_index = lax.axis_index("ctx")
    q_pos = ctx_index * tok_rows + jnp.arange(tok_rows, dtype=jnp.int32)
    q_docs = doc_index(doc_lengths, q_pos)
    q_three = queries.reshape(tok_rows, head_count, HD)

    def allowed_for(count):
        k_pos = jnp.arange(count, dtype=jnp.int32)
        same_doc = doc_index(doc_lengths, k_pos)[None, :] == q_docs[:, None]
        return same_doc & (k_pos[None, :] <= q_pos[:, None]) & (k_pos[None, :] >= 0)

    def masked_logits(portion, allowed):
        raw = (
            jnp.einsum("qhd,kd->hqk", q_three, portion, preferred_element_type=jnp.float32)
            * inv_root
        )
        return jnp.where(allowed[None], raw, -jnp.inf)

    init_stats = (
        jnp.full((head_count, tok_rows), -1e30, jnp.float32),
        jnp.zeros((head_count, tok_rows), jnp.float32),
    )
    init_rows = (
        jnp.zeros((tok_rows, head_count, HD), jnp.float32),
        jnp.zeros((all_tokens,), jnp.float32),
    )
    portion = lax.all_gather(keys, "ctx", axis=0, tiled=True)
    allowed = allowed_for(portion.shape[0])

    def compute(state):
        row_max, row_sum = state
        logits = masked_logits(portion, allowed)
        new_max = jnp.maximum(row_max, jnp.max(logits, axis=2))
        row_sum = jnp.sum(jnp.exp(logits - new_max[..., None]), axis=2)
        return (new_max, row_sum)

    row_max, row_sum = lax.cond(jnp.any(allowed), compute, lambda state: state, init_stats)
    log_norm = row_max + jnp.log(row_sum)
    key_part = lax.all_gather(keys, "ctx", axis=0, tiled=True)
    value_part = lax.all_gather(values, "ctx", axis=0, tiled=True)
    add_allowed = allowed_for(key_part.shape[0])

    def compute(state):
        probs = jnp.exp(masked_logits(key_part, add_allowed) - log_norm[..., None])
        weighted = jnp.einsum(
            "hqk,kd->qhd",
            probs.astype(jnp.bfloat16),
            value_part,
            preferred_element_type=jnp.float32,
        )
        col_sums = jnp.sum(probs, axis=(0, 1))
        return (weighted, col_sums)

    weighted, col_sums = lax.cond(jnp.any(add_allowed), compute, lambda state: state, init_rows)
    attn_rows = weighted.reshape(tok_rows, head_count * HD).astype(jnp.bfloat16)
    totals = lax.psum_scatter(col_sums, ("ctx", "head"), scatter_dimension=0, tiled=True)
    return (attn_rows, totals / HEADS)


def solution(mesh):
    placed = (P("ctx", "head"), P("ctx", None), P("ctx", None), P())
    return jax.shard_map(
        body,
        mesh=mesh,
        in_specs=placed,
        out_specs=(P("ctx", "head"), P(("ctx", "head"))),
        check_vma=False,
    )
```

profile of v0, /device:TPU:1, one launch (start us, length us, event | category | flops | bytes accessed | tf_op | source)
XLA Modules:
  0.0 282.1 jit_solution(1776633712790259538)
XLA Ops:
  7.2 0.0 all-gather.3.cloned.1.call-start
  7.2 0.7 all-gather.3.cloned.1.call-update
  7.9 0.0 all-gather.5.cloned.1.call-start
  7.9 0.7 all-gather.5.cloned.1.call-update
  8.7 0.8 reduce-window.8
  9.5 0.1 convert_reduce_fusion.1
  9.6 0.2 convert_reduce_fusion
  9.7 3.8 %fusion.14 = (pred[256,8192]{1,0:T(32,128)(4,1)S(1)}, pred[]{:T(512)}) fusion(s32[256]{0:T(256)S(1)} %iota_add_fusion, s32[8192]{0:T(1024)S(1)} %convert_reduce_fusion, s32[256]{0:T(256)S(1)} %convert_reduce_fusion.1), kind=kLoop, calls=%fused_computation.17 | loop fusion | flops 8388607 | bytes 2131969 | tf_op jit(solution)/shard_map/and | solution.py:31
  14.2 91.3 %all-gather.3.cloned.1.call-done = bf16[8192,128]{1,0:T(8,128)(2,1)} async-done(((bf16[256,128]{1,0:T(8,128)(2,1)}), bf16[8192,128]{1,0:T(8,128)(2,1)}) %all-gather.3.cloned.1.call-update) | async-done | bytes 2097168 | tf_op jit(solution)/shard_map/all_gather | solution.py:60
  105.6 8.6 %conditional.2 = (f32[1,256]{1,0:T(1,128)}, f32[1,256]{1,0:T(1,128)S(1)}) conditional(s32[]{:T(128)} %convert_element_type.22, () %tuple.29, (pred[256,8192]{1,0:T(32,128)(4,1)S(1)}, bf16[256,1,128]{2,0,1:T(8,128)(2,1)}, bf16[8192,128]{1,0:T(8,128)(2,1)}) %tuple.49), branch_computations={%region_4.5_spmd, %region_5.8_spmd} | conditional | flops 547356416 | bytes 33889352 | solution.py:58
  105.6 4.4 %copy.9 = pred[256,8192]{0,1:T(32,128)(4,1)S(1)} copy(pred[256,8192]{1,0:T(32,128)(4,1)S(1)} %get-tuple-element.49) | data formatting | bytes 4194304 | tf_op jit(solution)/shard_map
  110.0 0.0 copy-done
  110.0 0.0 copy-done.2
  110.0 1.8 fusion.16
  111.8 0.6 broadcast_maximum_fusion
  112.3 1.9 exponential_reduce_fusion
  114.2 80.5 %all-gather.5.cloned.1.call-done = bf16[8192,128]{1,0:T(8,128)(2,1)} async-done(((bf16[256,128]{1,0:T(8,128)(2,1)}), bf16[8192,128]{1,0:T(8,128)(2,1)}) %all-gather.5.cloned.1.call-update) | async-done | bytes 2097168 | tf_op jit(solution)/shard_map/all_gather | solution.py:61
  194.7 6.5 %conditional.3 = (f32[8192]{0:T(1024)S(1)}, bf16[256,128]{1,0:T(8,128)(2,1)S(1)}) conditional(s32[]{:T(128)} %convert_element_type.22, () %tuple.28, (pred[256,8192]{1,0:T(32,128)(4,1)S(1)}, bf16[256,1,128]{2,0,1:T(8,128)(2,1)}, bf16[8192,128]{1,0:T(8,128)(2,1)}, f32[1,256]{1,0:T(1,128)}, f32[1,256]{1,0:T(1,128)S(1)}, ...), branch_computations={%region_8.9_spmd, %region_9.11_spmd} | conditional | flops 1084252416 | bytes 23236652 | solution.py:75
  194.7 0.7 add.13
  195.4 4.6 %fusion.17 = (f32[8192]{0:T(1024)S(1)}, bf16[1,256,8192]{2,1,0:T(8,128)(2,1)S(1)}) fusion(f32[256]{0:T(256)S(1)} %bitcast.49, bf16[8192,128]{1,0:T(8,128)(2,1)} %get-tuple-element.25, bf16[256,1,128]{2,0,1:T(8,128)(2,1)} %get-tuple-element.26, pred[256,8192]{1,0:T(32,128)(4,1)S(1)} %get-tuple-element.24), kind=kOutput, calls=%fused_computation.25 | convolution fusion | flops 547348480 | bytes 8487936 | tf_op jit(solution)/shard_map/cond/branch_1_fun/qhd,kd->hqk/dot_general | solution.py:35
  200.0 1.2 fusion.10
  201.3 0.0 copy-start.3
  201.3 73.4 %all-reduce = f32[8192]{0:T(1024)S(1)} all-reduce(f32[8192]{0:T(1024)S(1)} %get-tuple-element.39), channel_id=2, replica_groups=mesh['ctx'=32,'head'=8] {'ctx','head'}, use_global_device_ids=true, to_apply=%region_11.12.clone | all-reduce | flops 8192 | bytes 65536
  274.7 0.6 dynamic-slice_multiply_fusion
  (7 shorter events, 0.0 us)
Async XLA Ops:
  7.2 98.4 %all-gather.3.cloned.1.call-start = ((), (), s32[]{:S(2)}) async-start(), calls=%async_computation | async-start | bytes 2162688 | tf_op jit(solution)/shard_map/all_gather | solution.py:60
  7.9 186.8 %all-gather.5.cloned.1.call-start = ((), (), s32[]{:S(2)}) async-start(), calls=%async_computation.1 | async-start | bytes 2162688 | tf_op jit(solution)/shard_map/all_gather | solution.py:61
  105.6 4.4 %copy-start = (bf16[8192,128]{1,0:T(8,128)(2,1)S(1)}, bf16[8192,128]{1,0:T(8,128)(2,1)}, u32[]{:S(2)}) copy-start(bf16[8192,128]{1,0:T(8,128)(2,1)} %get-tuple-element.22) | copy-start | bytes 6291460 | tf_op jit(solution)/shard_map/cond
  105.6 4.4 %copy-start.2 = (bf16[256,1,128]{2,0,1:T(8,128)(2,1)S(1)}, bf16[256,1,128]{2,0,1:T(8,128)(2,1)}, u32[]{:S(2)}) copy-start(bf16[256,1,128]{2,0,1:T(8,128)(2,1)} %get-tuple-element.23) | copy-start | bytes 196612 | tf_op jit(solution)/shard_map/cond
  195.4 4.6 %copy-start.1 = (bf16[8192,128]{1,0:T(8,128)(2,1)S(1)}, bf16[8192,128]{1,0:T(8,128)(2,1)}, u32[]{:S(2)}) copy-start(bf16[8192,128]{1,0:T(8,128)(2,1)} %get-tuple-element.29) | copy-start | bytes 6291460 | tf_op jit(solution)/shard_map/cond
  201.3 74.0 %copy-start.3 = (bf16[256,128]{1,0:T(8,128)(2,1)}, bf16[256,128]{1,0:T(8,128)(2,1)S(1)}, u32[]{:S(2)}) copy-start(bf16[256,128]{1,0:T(8,128)(2,1)S(1)} %get-tuple-element.34) | copy-start | bytes 196612
Sparse Core Ops, SparseCore 0:
  11.5 94.0 all-gather.2
  109.1 85.6 all-gather.4
where the time goes:
time: 282 us
  waiting for transfers between devices  173 us (61%)
  blocking collectives  73.4 us (26%)
  between operations  14.7 us (5%)
  other arithmetic  8.58 us (3%)
  matrix products  7.59 us (3%)
  local copies, waits for them, and re-layouts  4.43 us (2%)
    all_gather x1, waiting for transfers between devices, body(): key_part = lax.all_gather(keys, 'ctx', axis=0, tiled=True)  91.3 us
    all_gather x1, waiting for transfers between devices, body(): value_part = lax.all_gather(values, 'ctx', axis=0, tiled=True)  80.5 us
    unnamed x1, blocking collectives  73.4 us
    dot_general x2, matrix products, masked_logits(): jnp.einsum('qhd,kd->hqk', q_three, portion, preferred_element_type=jnp.fl...  6.35 us
  transfers between devices with their start and end apart: 2, of which 2 were waited for; matrix products, arithmetic and copies ran while one was open for 5% of the time, Pallas kernels for 0%

commit v1 on v0

v1 whole, which is shorter than its diff:
```python
import functools
import math

import jax
import jax.numpy as jnp
from jax import lax
from jax.experimental import pallas as pl
from jax.experimental.pallas import tpu as pltpu
from jax.sharding import Mesh, PartitionSpec as P

HD = 128
HEADS = 8
NY, NZH, NX, NZL, NC = 4, 2, 4, 4, 2
TOK = 256
CHUNK = TOK // HEADS
PER = TOK // NC
KEYS = NY * NX * PER
ROWS = 4 * TOK
SCALE = math.log2(math.e) / math.sqrt(HD)
TILE = 256
MIB = 1024 * 1024


def vmem(count=None):
    spec = pl.BlockSpec(memory_space=pltpu.VMEM)
    return spec if count is None else [spec] * count


def score_kernel(place_ref, docs_ref, keys_ref, q0, q1, q2, q3, probs_ref, stats_ref, raw_ref, q_ref):
    for i, q in enumerate((q0, q1, q2, q3)):
        q_ref[pl.ds(i * TOK, TOK), :] = q[...]
    y, zh, x, c = place_ref[0], place_ref[1], place_ref[2], place_ref[3]
    e0 = docs_ref[0]
    e1 = e0 + docs_ref[1]
    e2 = e1 + docs_ref[2]
    own = (y * 8 + zh * 4 + x) * TOK
    other = (y * 8 + (1 - zh) * 4 + x) * TOK
    lane = lax.broadcasted_iota(jnp.int32, (1, ROWS), 1)
    pos = jnp.where(lane < 2 * TOK, own, other) + lax.rem(lane, TOK)
    start = jnp.zeros_like(pos)
    for end in (e0, e1, e2):
        start = jnp.where(pos >= end, end, start)

    def first(t, peak):
        block = keys_ref[pl.ds(pl.multiple_of(t * TILE, TILE), TILE), :]
        raw = lax.dot_general(block, q_ref[...], (((1,), (1,)), ((), ())), preferred_element_type=jnp.float32)
        g = t * TILE + lax.broadcasted_iota(jnp.int32, (TILE, 1), 0)
        source = g // PER
        key_pos = (
            ((source // NX) * 8 + zh * 4 + source % NX) * TOK
            + ((g // CHUNK) % NZL * 2 + c) * CHUNK
            + g % CHUNK
        )
        raw = jnp.where((key_pos >= start) & (key_pos <= pos), raw, -jnp.inf)
        raw_ref[pl.ds(pl.multiple_of(t * TILE, TILE), TILE), :] = raw
        return jnp.maximum(peak, jnp.max(raw.reshape(TILE // 8, 8, ROWS), axis=0))

    peak = lax.fori_loop(0, KEYS // TILE, first, jnp.full((8, ROWS), -1e30, jnp.float32))
    row_max = jnp.max(peak, axis=0, keepdims=True)

    def second(t, total):
        rows = pl.ds(pl.multiple_of(t * TILE, TILE), TILE)
        probs = jnp.exp2((raw_ref[rows, :] - row_max) * SCALE)
        probs_ref[rows, :] = probs.astype(jnp.bfloat16)
        return total + jnp.sum(probs.reshape(TILE // 8, 8, ROWS), axis=0)

    total = lax.fori_loop(0, KEYS // TILE, second, jnp.zeros((8, ROWS), jnp.float32))
    stats_ref[0:1, :] = row_max
    stats_ref[1:2, :] = jnp.sum(total, axis=0, keepdims=True)


def column_kernel(probs_ref, s0, s1, s2, s3, cols_ref, weight_ref):
    def aligned(ref, flip):
        pieces = [ref[:, pl.ds((k ^ flip) * TOK, TOK)] for k in range(4)]
        both = jnp.concatenate(pieces, axis=1)
        return both[0:1, :], both[1:2, :]

    parts = [aligned(s, flip) for s, flip in ((s0, 0), (s1, 1), (s2, 2), (s3, 3))]
    top = functools.reduce(jnp.maximum, [m for m, _ in parts])
    norm = sum(l * jnp.exp2((m - top) * SCALE) for m, l in parts)
    weight = jnp.exp2((parts[0][0] - top) * SCALE) / norm
    weight_ref[...] = weight
    high = weight.astype(jnp.bfloat16).astype(jnp.float32)
    row = lax.broadcasted_iota(jnp.int32, (8, ROWS), 0)
    both = jnp.where(row == 0, high, jnp.where(row == 1, weight - high, 0.0)).astype(jnp.bfloat16)
    for k in range(NY * NX):
        sums = lax.dot_general(
            both, probs_ref[pl.ds(k * PER, PER), :], (((1,), (1,)), ((), ())), preferred_element_type=jnp.float32
        )
        line = jnp.sum(sums, axis=0, keepdims=True)
        cols_ref[pl.ds(k * NZL, NZL), :] = jnp.broadcast_to(line, (NZL, PER))


def value_kernel(probs_ref, values_ref, weight_ref, keep_ref, send_ref):
    acc = lax.dot_general(
        values_ref[...], probs_ref[...], (((0,), (0,)), ((), ())), preferred_element_type=jnp.float32
    )
    acc = acc * weight_ref[...]
    for k in range(2):
        keep_ref[k] = acc[:, (2 * k) * TOK : (2 * k + 1) * TOK]
        send_ref[k] = acc[:, (2 * k + 1) * TOK : (2 * k + 2) * TOK]


def body(queries, keys, values, doc_lengths):
    zc = ("zh", "zl", "c")
    place = jnp.stack([lax.axis_index(a) for a in ("y", "zh", "x", "c")]).astype(jnp.int32)
    c = lax.axis_index("c")

    def across(x):
        return lax.ppermute(x, "c", [(0, 1), (1, 0)])

    def partner(x, flip=12):
        return lax.ppermute(x, zc, [(i, i ^ flip) for i in range(16)])

    both = jnp.stack([keys, values]).reshape(2, NZL, NC, CHUNK, HD)
    mine = jnp.where(c == 0, both[:, :, 0], both[:, :, 1]).reshape(2, PER, HD)
    parts = lax.all_to_all(jnp.broadcast_to(mine[None], (NY * NX, 2, PER, HD)), ("y", "x"), 0, 0, tiled=True)
    q1 = across(queries)
    q2 = partner(queries)
    q3 = across(q2)
    k_all = parts[:, 0].reshape(KEYS, HD)
    v_all = parts[:, 1].reshape(KEYS, HD)

    smem = pl.BlockSpec(memory_space=pltpu.SMEM)
    probs, stats = pl.pallas_call(
        score_kernel,
        out_shape=(
            jax.ShapeDtypeStruct((KEYS, ROWS), jnp.bfloat16),
            jax.ShapeDtypeStruct((2, ROWS), jnp.float32),
        ),
        in_specs=[smem, smem] + vmem(5),
        out_specs=tuple(vmem(2)),
        scratch_shapes=[pltpu.VMEM((KEYS, ROWS), jnp.float32), pltpu.VMEM((ROWS, HD), jnp.bfloat16)],
        compiler_params=pltpu.CompilerParams(vmem_limit_bytes=40 * MIB),
        name="scores",
    )(place, doc_lengths, k_all, queries, q1, q2, q3)

    s1 = across(stats)
    s2 = partner(stats)
    s3 = partner(stats, 13)
    cols, weight = pl.pallas_call(
        column_kernel,
        out_shape=(
            jax.ShapeDtypeStruct((NY * NX * NZL, PER), jnp.float32),
            jax.ShapeDtypeStruct((1, ROWS), jnp.float32),
        ),
        in_specs=vmem(5),
        out_specs=tuple(vmem(2)),
        compiler_params=pltpu.CompilerParams(vmem_limit_bytes=24 * MIB),
        name="columns",
    )(probs, stats, s1, s2, s3)

    got = lax.all_to_all(cols.reshape(NY * NX * NZL, 1, PER), ("y", "x", "zl"), 0, 0, tiled=True)
    totals = jnp.sum(got.reshape(NY * NX * NZL, NZL, CHUNK), axis=0) / HEADS
    scores = lax.dynamic_index_in_dim(totals, lax.axis_index("zl"), 0, keepdims=False)

    keep, send = pl.pallas_call(
        value_kernel,
        out_shape=(jax.ShapeDtypeStruct((2, HD, TOK), jnp.float32),) * 2,
        in_specs=vmem(3),
        out_specs=tuple(vmem(2)),
        compiler_params=pltpu.CompilerParams(vmem_limit_bytes=24 * MIB),
        name="rows",
    )(probs, v_all, weight)
    half = keep + across(send)
    rows = (half[0] + partner(half[1])).T.astype(jnp.bfloat16)
    return rows, scores


def solution(mesh):
    fine = Mesh(mesh.devices.reshape(NY, NZH, NX, NZL, NC), ("y", "zh", "x", "zl", "c"))
    ctx, head = ("y", "zh", "x"), ("zl", "c")
    return jax.shard_map(
        body,
        mesh=fine,
        in_specs=(P(ctx, head), P(ctx, None), P(ctx, None), P()),
        out_specs=(P(ctx, head), P(ctx + head)),
        check_vma=False,
    )
```

time: 282 us -> 72.2 us (0.26)
  the two profiles are of different devices: /device:TPU:1 before, /device:TPU:32 now
where the time goes in v1:
time: 72.2 us; the launch traced here: 72 us
  waiting for transfers between devices  32.6 us (45%)
  starting transfers between devices  25.8 us (36%)
  Pallas kernels  9.16 us (13%)
  local copies, waits for them, and re-layouts  2.65 us (4%)
  other arithmetic  1.05 us (1%)
  between operations  0.76 us (1%)
    ppermute x4, waiting for transfers between devices, partner(): return lax.ppermute(x, zc, [(i, i ^ flip) for i in range(16)])  16.1 us
    ppermute x4, starting transfers between devices, partner(): return lax.ppermute(x, zc, [(i, i ^ flip) for i in range(16)])  11.2 us
    all_to_all x1, waiting for transfers between devices, body(): lax.all_to_all(cols.reshape(NY * NX * NZL, 1, PER), ('y', 'x', 'zl'), 0,...  8.76 us
    all_to_all x1, waiting for transfers between devices, body(): lax.all_to_all(jnp.broadcast_to(mine[None], (NY * NX, 2, PER, HD)), ('y',...  7.77 us
    all_to_all x1, starting transfers between devices, body(): lax.all_to_all(jnp.broadcast_to(mine[None], (NY * NX, 2, PER, HD)), ('y',...  7.03 us
    pallas_call x1, Pallas kernels, body(): pl.pallas_call(score_kernel, out_shape=(jax.ShapeDtypeStruct((KEYS, ROWS)...  6.57 us
    all_to_all x1, starting transfers between devices, body(): lax.all_to_all(cols.reshape(NY * NX * NZL, 1, PER), ('y', 'x', 'zl'), 0,...  5.88 us
    pallas_call x1, Pallas kernels, body(): pl.pallas_call(column_kernel, out_shape=(jax.ShapeDtypeStruct((NY * NX *...  1.83 us
  transfers between devices with their start and end apart: 10, of which 5 were waited for; matrix products, arithmetic and copies ran while one was open for 1% of the time, Pallas kernels for 0%

profile of v1, /device:TPU:32, one launch (start us, length us, event | category | flops | bytes accessed | tf_op | source)
XLA Modules:
  0.0 72.0 jit_solution(8926670614615036863)
XLA Ops:
  0.7 0.8 %fusion.3 = bf16[2,4,1,32,128]{4,3,2,1,0:T(8,128)(2,1)S(1)} fusion(bf16[1,4,2,32,128]{4,3,2,1,0:T(8,128)(2,1)} %bitcast.29, bf16[1,4,2,32,128]{4,3,2,1,0:T(8,128)(2,1)} %bitcast.30, pred[]{:T(512)S(6)} %eq.3), kind=kLoop, calls=%fused_computation.7 | loop fusion | flops 98304 | bytes 196609 | tf_op jit(solution)/shard_map/jit(_where)/select_n | solution.py:116
  1.5 1.2 %broadcast_in_dim.2 = bf16[16,2,128,128]{3,2,1,0:T(8,128)(2,1)} broadcast(bf16[2,128,128]{2,1,0:T(8,128)(2,1)S(1)} %bitcast.28), dimensions={1,2,3} | broadcast | bytes 1114112 | tf_op jit(solution)/shard_map/broadcast_in_dim | solution.py:117
  2.7 7.0 %all-to-all-start = ((bf16[16,2,128,128]{3,2,1,0:T(8,128)(2,1)}), bf16[16,2,128,128]{3,2,1,0:T(8,128)(2,1)S(1)}, u32[]{:S(2)}, u32[]{:S(2)}) async-start(bf16[16,2,128,128]{3,2,1,0:T(8,128)(2,1)} %broadcast_in_dim.2), calls=%async_computation | async-start | bytes 2097152 | tf_op jit(solution)/shard_map/all_to_all | solution.py:117
  9.8 0.1 collective-permute-start
  9.9 5.5 %collective-permute-start.1 = (bf16[256,128]{1,0:T(8,128)(2,1)}, bf16[256,128]{1,0:T(8,128)(2,1)S(1)}, u32[]{:S(2)}, u32[]{:S(2)}) collective-permute-start(bf16[256,128]{1,0:T(8,128)(2,1)} %q0.1), channel_id=1, source_target_pairs={{0,36},{1,37},{2,38},{3,39},{4,32},{5,33},{6,34},{7,35},{32,4},{33... | collective-permute-start | bytes 196616 | tf_op jit(solution)/shard_map/ppermute | solution.py:113
  15.4 0.1 pad_add_fusion.place_ref
  15.4 4.2 %collective-permute-done.1.q2 = bf16[256,128]{1,0:T(8,128)(2,1)S(1)} collective-permute-done((bf16[256,128]{1,0:T(8,128)(2,1)}, bf16[256,128]{1,0:T(8,128)(2,1)S(1)}, u32[]{:S(2)}, u32[]{:S(2)}) %collective-permute-start.1) | collective-permute-done | bytes 65568 | tf_op jit(solution)/shard_map/ppermute | solution.py:113
  19.6 7.8 %all-to-all-done = bf16[16,2,128,128]{3,2,1,0:T(8,128)(2,1)S(1)} async-done(((bf16[16,2,128,128]{3,2,1,0:T(8,128)(2,1)}), bf16[16,2,128,128]{3,2,1,0:T(8,128)(2,1)S(1)}, u32[]{:S(2)}, u32[]{:S(2)}) %all-to-all-start) | async-done | bytes 1048608 | tf_op jit(solution)/shard_map/all_to_all | solution.py:117
  27.4 0.1 fusion.5
  27.5 6.6 %scores.1 = (bf16[2048,1024]{1,0:T(8,128)(2,1)S(1)}, f32[2,1024]{1,0:T(2,128)S(1)}) custom-call(s32[4]{0:T(128)S(1)} %pad_add_fusion.place_ref, s32[4]{0:T(128)S(1)} %copy-done.1, bf16[2048,128]{1,0:T(8,128)(2,1)S(1)} %bitcast.26, bf16[256,128]{1,0:T(8,128)(2,1)S(1)} %copy-done, bf16[256,128]{1,0:T(8,128)(2,1)S(1)} %collective-permute-done.q1, ...), custom_call_target="tpu_custom_call" | custom-call | tf_op jit(solution)/shard_map/scores/pallas_call | solution.py:125
  34.1 3.0 %collective-permute-start.5 = (f32[2,1024]{1,0:T(2,128)S(1)}, f32[2,1024]{1,0:T(2,128)S(1)}, u32[]{:S(2)}, u32[]{:S(2)}) collective-permute-start(f32[2,1024]{1,0:T(2,128)S(1)} %get-tuple-element.9.s0), channel_id=1, source_target_pairs={{0,37},{1,36},{2,39},{3,38},{4,33},{5,32},{6,35},{7,34},{32,5},{33... | collective-permute-start | bytes 24584 | tf_op jit(solution)/shard_map/ppermute | solution.py:113
  37.1 2.6 %collective-permute-start.4 = (f32[2,1024]{1,0:T(2,128)S(1)}, f32[2,1024]{1,0:T(2,128)S(1)}, u32[]{:S(2)}, u32[]{:S(2)}) collective-permute-start(f32[2,1024]{1,0:T(2,128)S(1)} %get-tuple-element.9.s0), channel_id=1, source_target_pairs={{0,36},{1,37},{2,38},{3,39},{4,32},{5,33},{6,34},{7,35},{32,4},{33... | collective-permute-start | bytes 24584 | tf_op jit(solution)/shard_map/ppermute | solution.py:113
  39.7 3.1 %collective-permute-done.4.s2 = f32[2,1024]{1,0:T(2,128)S(1)} collective-permute-done((f32[2,1024]{1,0:T(2,128)S(1)}, f32[2,1024]{1,0:T(2,128)S(1)}, u32[]{:S(2)}, u32[]{:S(2)}) %collective-permute-start.4) | collective-permute-done | bytes 8224 | tf_op jit(solution)/shard_map/ppermute | solution.py:113
  42.8 1.8 %columns.1 = (f32[64,128]{1,0:T(8,128)}, f32[1,1024]{1,0:T(1,128)S(1)}) custom-call(bf16[2048,1024]{1,0:T(8,128)(2,1)S(1)} %get-tuple-element.8.probs_ref, f32[2,1024]{1,0:T(2,128)S(1)} %get-tuple-element.9.s0, f32[2,1024]{1,0:T(2,128)S(1)} %collective-permute-done.3.s1, f32[2,1024]{1,0:T(2,128)S(1)} %collective-permute-done.4.s2, ...), custom_call_target="tpu_custom_call" | custom-call | tf_op jit(solution)/shard_map/columns/pallas_call | solution.py:141
  44.7 0.8 %rows.1 = (f32[2,128,256]{2,1,0:T(8,128)S(1)}, f32[2,128,256]{2,1,0:T(8,128)S(1)}) custom-call(bf16[2048,1024]{1,0:T(8,128)(2,1)S(1)} %get-tuple-element.8.probs_ref, bf16[2048,128]{1,0:T(8,128)(2,1)S(1)} %bitcast.27, f32[1,1024]{1,0:T(1,128)S(1)} %get-tuple-element.10.weight_ref), custom_call_target="tpu_custom_call" | custom-call | tf_op jit(solution)/shard_map/rows/pallas_call | solution.py:157
  45.4 1.6 %collective-permute-start.6 = (f32[2,128,256]{2,1,0:T(8,128)S(1)}, f32[2,128,256]{2,1,0:T(8,128)S(1)}, u32[]{:S(2)}, u32[]{:S(2)}) collective-permute-start(f32[2,128,256]{2,1,0:T(8,128)S(1)} %get-tuple-element.12), channel_id=1, source_target_pairs={{0,1},{1,0},{2,3},{3,2},{4,5},{5,4},{6,7},{7,6},{8,9},{9,8},{10,11... | collective-permute-start | bytes 786440 | tf_op jit(solution)/shard_map/ppermute | solution.py:110
  47.0 5.9 %all-to-all-start.1 = ((f32[64,1,128]{2,1,0:T(1,128)}), f32[64,1,128]{2,1,0:T(1,128)S(1)}, u32[]{:S(2)}, u32[]{:S(2)}) async-start(f32[64,1,128]{2,1,0:T(1,128)} %bitcast.13), calls=%async_computation.1 | async-start | bytes 65536 | tf_op jit(solution)/shard_map/all_to_all | solution.py:153
  52.9 8.8 %all-to-all-done.1 = f32[64,1,128]{2,1,0:T(1,128)S(1)} async-done(((f32[64,1,128]{2,1,0:T(1,128)}), f32[64,1,128]{2,1,0:T(1,128)S(1)}, u32[]{:S(2)}, u32[]{:S(2)}) %all-to-all-start.1) | async-done | bytes 32800 | tf_op jit(solution)/shard_map/all_to_all | solution.py:153
  61.6 0.1 reduce_sum.9
  61.8 0.1 collective-permute-start.7
  61.9 0.1 div.10
  62.0 0.5 dynamic-slice_bitcast_fusion
  62.5 8.7 %collective-permute-done.7 = f32[128,256]{1,0:T(8,128)S(1)} collective-permute-done((f32[128,256]{1,0:T(8,128)S(1)}, f32[128,256]{1,0:T(8,128)S(1)}, u32[]{:S(2)}, u32[]{:S(2)}) %collective-permute-start.7) | collective-permute-done | bytes 131104 | tf_op jit(solution)/shard_map/ppermute | solution.py:113
  71.3 0.7 %copy.8 = bf16[256,128]{1,0:T(8,128)(2,1)} copy(bf16[256,128]{0,1:T(8,128)(2,1)S(1)} %fusion.4) | data formatting | bytes 131072
  (15 shorter events, 0.1 us)
Async XLA Ops:
  0.6 26.9 %copy-start = (bf16[256,128]{1,0:T(8,128)(2,1)S(1)}, bf16[256,128]{1,0:T(8,128)(2,1)}, u32[]{:S(2)}) copy-start(bf16[256,128]{1,0:T(8,128)(2,1)} %q0.1) | copy-start | bytes 196612
  0.6 26.9 %copy-start.1 = (s32[4]{0:T(128)S(1)}, s32[4]{0:T(128)}, u32[]{:S(2)}) copy-start(s32[4]{0:T(128)} %docs_ref.1) | copy-start | bytes 52
  2.7 24.7 %all-to-all-start = ((bf16[16,2,128,128]{3,2,1,0:T(8,128)(2,1)}), bf16[16,2,128,128]{3,2,1,0:T(8,128)(2,1)S(1)}, u32[]{:S(2)}, u32[]{:S(2)}) async-start(bf16[16,2,128,128]{3,2,1,0:T(8,128)(2,1)} %broadcast_in_dim.2), calls=%async_computation | async-start | bytes 2097152 | tf_op jit(solution)/shard_map/all_to_all | solution.py:117
  9.8 17.7 %collective-permute-start = (bf16[256,128]{1,0:T(8,128)(2,1)}, bf16[256,128]{1,0:T(8,128)(2,1)S(1)}, u32[]{:S(2)}, u32[]{:S(2)}) collective-permute-start(bf16[256,128]{1,0:T(8,128)(2,1)} %q0.1), channel_id=1, source_target_pairs={{0,1},{1,0},{2,3},{3,2},{4,5},{5,4},{6,7},{7,6},{8,9},{9,8},{10,11... | collective-permute-start | bytes 196616 | tf_op jit(solution)/shard_map/ppermute | solution.py:110
  9.9 9.8 %collective-permute-start.1 = (bf16[256,128]{1,0:T(8,128)(2,1)}, bf16[256,128]{1,0:T(8,128)(2,1)S(1)}, u32[]{:S(2)}, u32[]{:S(2)}) collective-permute-start(bf16[256,128]{1,0:T(8,128)(2,1)} %q0.1), channel_id=1, source_target_pairs={{0,36},{1,37},{2,38},{3,39},{4,32},{5,33},{6,34},{7,35},{32,4},{33... | collective-permute-start | bytes 196616 | tf_op jit(solution)/shard_map/ppermute | solution.py:113
  19.6 7.9 %collective-permute-start.2 = (bf16[256,128]{1,0:T(8,128)(2,1)S(1)}, bf16[256,128]{1,0:T(8,128)(2,1)S(1)}, u32[]{:S(2)}, u32[]{:S(2)}) collective-permute-start(bf16[256,128]{1,0:T(8,128)(2,1)S(1)} %collective-permute-done.1.q2), channel_id=1, source_target_pairs={{0,1},{1,0},{2,3},{3,2},{4,5},{5,4},{6,7},{7,6},{8,9},{9,8},{10,11... | collective-permute-start | bytes 196616 | tf_op jit(solution)/shard_map/ppermute | solution.py:110
  34.1 5.6 %collective-permute-start.5 = (f32[2,1024]{1,0:T(2,128)S(1)}, f32[2,1024]{1,0:T(2,128)S(1)}, u32[]{:S(2)}, u32[]{:S(2)}) collective-permute-start(f32[2,1024]{1,0:T(2,128)S(1)} %get-tuple-element.9.s0), channel_id=1, source_target_pairs={{0,37},{1,36},{2,39},{3,38},{4,33},{5,32},{6,35},{7,34},{32,5},{33... | collective-permute-start | bytes 24584 | tf_op jit(solution)/shard_map/ppermute | solution.py:113
  37.1 5.8 %collective-permute-start.4 = (f32[2,1024]{1,0:T(2,128)S(1)}, f32[2,1024]{1,0:T(2,128)S(1)}, u32[]{:S(2)}, u32[]{:S(2)}) collective-permute-start(f32[2,1024]{1,0:T(2,128)S(1)} %get-tuple-element.9.s0), channel_id=1, source_target_pairs={{0,36},{1,37},{2,38},{3,39},{4,32},{5,33},{6,34},{7,35},{32,4},{33... | collective-permute-start | bytes 24584 | tf_op jit(solution)/shard_map/ppermute | solution.py:113
  39.7 3.2 %collective-permute-start.3 = (f32[2,1024]{1,0:T(2,128)S(1)}, f32[2,1024]{1,0:T(2,128)S(1)}, u32[]{:S(2)}, u32[]{:S(2)}) collective-permute-start(f32[2,1024]{1,0:T(2,128)S(1)} %get-tuple-element.9.s0), channel_id=1, source_target_pairs={{0,1},{1,0},{2,3},{3,2},{4,5},{5,4},{6,7},{7,6},{8,9},{9,8},{10,11... | collective-permute-start | bytes 24584 | tf_op jit(solution)/shard_map/ppermute | solution.py:110
  45.4 16.3 %collective-permute-start.6 = (f32[2,128,256]{2,1,0:T(8,128)S(1)}, f32[2,128,256]{2,1,0:T(8,128)S(1)}, u32[]{:S(2)}, u32[]{:S(2)}) collective-permute-start(f32[2,128,256]{2,1,0:T(8,128)S(1)} %get-tuple-element.12), channel_id=1, source_target_pairs={{0,1},{1,0},{2,3},{3,2},{4,5},{5,4},{6,7},{7,6},{8,9},{9,8},{10,11... | collective-permute-start | bytes 786440 | tf_op jit(solution)/shard_map/ppermute | solution.py:110
  47.0 14.7 %all-to-all-start.1 = ((f32[64,1,128]{2,1,0:T(1,128)}), f32[64,1,128]{2,1,0:T(1,128)S(1)}, u32[]{:S(2)}, u32[]{:S(2)}) async-start(f32[64,1,128]{2,1,0:T(1,128)} %bitcast.13), calls=%async_computation.1 | async-start | bytes 65536 | tf_op jit(solution)/shard_map/all_to_all | solution.py:153
  61.8 9.4 %collective-permute-start.7 = (f32[128,256]{1,0:T(8,128)S(1)}, f32[128,256]{1,0:T(8,128)S(1)}, u32[]{:S(2)}, u32[]{:S(2)}) collective-permute-start(f32[128,256]{1,0:T(8,128)S(1)} %slice_bitcast_fusion), channel_id=1, source_target_pairs={{0,36},{1,37},{2,38},{3,39},{4,32},{5,33},{6,34},{7,35},{32,4},{33... | collective-permute-start | bytes 393224 | tf_op jit(solution)/shard_map/ppermute | solution.py:113

commit v2 on v0

v2 whole, which is shorter than its diff:
```python
import math

import jax
import jax.numpy as jnp
from jax import lax
from jax.experimental import pallas as pl
from jax.experimental.pallas import tpu as pltpu
from jax.sharding import Mesh, PartitionSpec as P

HD = 128
HEADS = 8
NY, NZH, NX, NZL, NC = 4, 2, 4, 4, 2
TOK = 256
CHUNK = TOK // HEADS
HALF = TOK // NC
BLOCKS = NY * NX
SIDE = BLOCKS * HALF
KEYS = NC * SIDE
ROWS = 2 * TOK
TILE = 512
SCALE = math.log2(math.e) / math.sqrt(HD)
MIB = 1024 * 1024
VMEM = pl.BlockSpec(memory_space=pltpu.VMEM)
SMEM = pl.BlockSpec(memory_space=pltpu.SMEM)


def spread_kernel(place_ref, keys_ref, values_ref, out_ref):
    half = pl.ds(pl.multiple_of(place_ref[3] * HALF, HALF), HALF)
    k, v = keys_ref[half, :], values_ref[half, :]
    for i in range(BLOCKS):
        out_ref[i, 0] = k
        out_ref[i, 1] = v


def score_kernel(place_ref, docs_ref, near_ref, far_ref, own_ref, other_ref, probs_ref, stats_ref, raw_ref):
    y, zh, x, c = place_ref[0], place_ref[1], place_ref[2], place_ref[3]
    e0 = docs_ref[0]
    e1 = e0 + docs_ref[1]
    e2 = e1 + docs_ref[2]
    own = (y * 8 + zh * 4 + x) * TOK
    other = (y * 8 + (1 - zh) * 4 + x) * TOK
    row = lax.broadcasted_iota(jnp.int32, (ROWS, 128), 0)
    pos = jnp.where(row < TOK, own, other) + lax.rem(row, TOK)
    start = jnp.zeros_like(pos)
    for end in (e0, e1, e2):
        start = jnp.where(pos >= end, end, start)
    lane = lax.broadcasted_iota(jnp.int32, (1, HALF), 1)
    queries = jnp.concatenate([own_ref[...], other_ref[...]], axis=0)

    peak = jnp.full((ROWS, 128), -1e30, jnp.float32)
    per = TILE // HALF
    for t in range(KEYS // TILE):
        ref, half = (near_ref, c) if t * TILE < SIDE else (far_ref, 1 - c)
        first = t * per % BLOCKS
        block = ref[pl.ds(first, per), 0].reshape(TILE, HD)
        raw = lax.dot_general(queries, block, (((1,), (1,)), ((), ())), preferred_element_type=jnp.float32)
        for j in range(per):
            source = first + j
            key_pos = (source // NX * 8 + zh * 4 + source % NX) * TOK + half * HALF + lane
            part = raw[:, j * HALF : (j + 1) * HALF]
            part = jnp.where((key_pos >= start) & (key_pos <= pos), part, -jnp.inf)
            raw_ref[:, t * TILE + j * HALF : t * TILE + (j + 1) * HALF] = part
            peak = jnp.maximum(peak, part)
    row_max = jnp.max(peak, axis=1, keepdims=True)

    total = jnp.zeros((ROWS, 128), jnp.float32)
    for j in range(KEYS // HALF):
        cut = slice(j * HALF, (j + 1) * HALF)
        probs = jnp.exp2((raw_ref[:, cut] - row_max) * SCALE)
        probs_ref[:, cut] = probs.astype(jnp.bfloat16)
        total = total + probs
    row_sum = jnp.sum(total, axis=1, keepdims=True)
    first_lane = lax.broadcasted_iota(jnp.int32, (ROWS, 128), 1) == 0
    stats_ref[...] = jnp.where(first_lane, row_max, row_sum).T[0:2, :]


def value_kernel(probs_ref, near_ref, far_ref, keep_ref, send_ref):
    acc = jnp.dot(probs_ref[:, :SIDE], near_ref[:, 1].reshape(SIDE, HD), preferred_element_type=jnp.float32)
    acc += jnp.dot(probs_ref[:, SIDE:], far_ref[:, 1].reshape(SIDE, HD), preferred_element_type=jnp.float32)
    keep_ref[...] = acc[:TOK]
    send_ref[...] = acc[TOK:].astype(jnp.bfloat16)


def shares(mine_ref, theirs_ref):
    both = theirs_ref[...]
    both = jnp.concatenate([both[:, TOK:], both[:, :TOK]], axis=1)
    m0, l0, m1, l1 = mine_ref[0:1, :], mine_ref[1:2, :], both[0:1, :], both[1:2, :]
    top = jnp.maximum(m0, m1)
    w0, w1 = jnp.exp2((m0 - top) * SCALE), jnp.exp2((m1 - top) * SCALE)
    norm = w0 * l0 + w1 * l1
    return w0 / norm, w1 / norm


def column_kernel(place_ref, probs_ref, mine_ref, theirs_ref, cols_ref):
    weight, _ = shares(mine_ref, theirs_ref)
    high = weight.astype(jnp.bfloat16).astype(jnp.float32)
    row = lax.broadcasted_iota(jnp.int32, (8, ROWS), 0)
    both = jnp.where(row == 0, high, jnp.where(row == 1, weight - high, 0.0)).astype(jnp.bfloat16)
    straight = place_ref[3] == 0

    def line(first):
        sums = jnp.dot(both, probs_ref[:, first : first + 2 * HALF], preferred_element_type=jnp.float32)
        return jnp.sum(sums, axis=0, keepdims=True)

    for b in range(0, BLOCKS, 2):
        near, far = line(b * HALF), line(SIDE + b * HALF)
        low, top = jnp.where(straight, near, far), jnp.where(straight, far, near)
        for i in range(2):
            cut = slice(i * HALF, (i + 1) * HALF)
            cols_ref[(b + i) * 8 : (b + i) * 8 + 4, :] = jnp.broadcast_to(low[:, cut], (4, HALF))
            cols_ref[(b + i) * 8 + 4 : (b + i) * 8 + 8, :] = jnp.broadcast_to(top[:, cut], (4, HALF))


def merge_kernel(keep_ref, got_ref, mine_ref, theirs_ref, out_ref):
    w0, w1 = shares(mine_ref, theirs_ref)
    w0 = jnp.broadcast_to(w0[:, :TOK], (HD, TOK)).T
    w1 = jnp.broadcast_to(w1[:, :TOK], (HD, TOK)).T
    out_ref[...] = (keep_ref[...] * w0 + got_ref[...].astype(jnp.float32) * w1).astype(jnp.bfloat16)


def kernel(fn, name, shapes, specs, scratch=(), limit=24):
    return pl.pallas_call(
        fn,
        out_shape=shapes,
        in_specs=specs,
        out_specs=jax.tree.map(lambda _: VMEM, shapes),
        scratch_shapes=scratch,
        compiler_params=pltpu.CompilerParams(vmem_limit_bytes=limit * MIB),
        name=name,
    )


def body(queries, keys, values, doc_lengths):
    shape = jax.ShapeDtypeStruct
    f32, bf16 = jnp.float32, jnp.bfloat16
    place = jnp.stack([lax.axis_index(a) for a in ("y", "zh", "x", "c")]).astype(jnp.int32)

    def across(x):
        return lax.ppermute(x, "c", [(0, 1), (1, 0)])

    def partner(x):
        return lax.ppermute(x, ("zh", "zl", "c"), [(i, i ^ 12) for i in range(16)])

    copies = kernel(spread_kernel, "spread", shape((BLOCKS, 2, HALF, HD), bf16), [SMEM, VMEM, VMEM])(
        place, keys, values
    )
    other = partner(queries)
    near = lax.all_to_all(copies, ("y", "x"), 0, 0, tiled=True)
    far = across(near)
    probs, mine = kernel(
        score_kernel,
        "scores",
        (shape((ROWS, KEYS), bf16), shape((2, ROWS), f32)),
        [SMEM, SMEM, VMEM, VMEM, VMEM, VMEM],
        [pltpu.VMEM((ROWS, KEYS), f32)],
        limit=32,
    )(place, doc_lengths, near, far, queries, other)
    theirs = partner(mine)
    keep, send = kernel(
        value_kernel, "rows", (shape((TOK, HD), f32), shape((TOK, HD), bf16)), [VMEM, VMEM, VMEM]
    )(probs, near, far)
    got = partner(send)
    cols = kernel(column_kernel, "columns", shape((BLOCKS * HEADS, HALF), f32), [SMEM, VMEM, VMEM, VMEM])(
        place, probs, mine, theirs
    )
    parts = lax.all_to_all(cols.reshape(BLOCKS * HEADS, 1, HALF), ("y", "x", "zl", "c"), 0, 0, tiled=True)
    rows = kernel(merge_kernel, "merge", shape((TOK, HD), bf16), [VMEM, VMEM, VMEM, VMEM])(keep, got, mine, theirs)
    totals = (jnp.sum(parts, axis=(0, 1)) / HEADS).reshape(HALF // CHUNK, CHUNK)
    piece = lax.rem(lax.axis_index("zl") * NC + lax.axis_index("c"), HALF // CHUNK)
    return rows, lax.dynamic_index_in_dim(totals, piece, 0, keepdims=False)


def solution(mesh):
    fine = Mesh(mesh.devices.reshape(NY, NZH, NX, NZL, NC), ("y", "zh", "x", "zl", "c"))
    ctx, head = ("y", "zh", "x"), ("zl", "c")
    return jax.shard_map(
        body,
        mesh=fine,
        in_specs=(P(ctx, head), P(ctx, None), P(ctx, None), P()),
        out_specs=(P(ctx, head), P(ctx + head)),
        check_vma=False,
    )
```

time: 282 us -> 72.5 us (0.26)
  waiting for transfers between devices: 173 us -> 6.29 us
  blocking collectives: 73.4 us -> 23.5 us
  starting transfers between devices: 0.08 us -> 24.4 us
  between operations: 14.7 us -> 0.68 us
  Pallas kernels: 0 us -> 8.35 us
  other arithmetic: 8.58 us -> 0.23 us
  matrix products: 7.59 us -> 0 us
  local copies, waits for them, and re-layouts: 4.43 us -> 7.92 us
    all_gather x2 -> x0, waiting for transfers between devices: 172 us -> none  [the longest x1 91.3 us: body(): key_part = lax.all_gather(keys, 'ctx', axis=0, tiled=True)]
    unnamed x1 -> x0, blocking collectives: 73.4 us -> none
    all_to_all x0 -> x1, blocking collectives: none -> 23.5 us  [body(): near = lax.all_to_all(copies, ('y', 'x'), 0, 0, tiled=True)]
    ppermute x0 -> x4, starting transfers between devices: none -> 17 us  [the longest x3 15 us: partner(): return lax.ppermute(x, ('zh', 'zl', 'c'), [(i, i ^ 12) for i in range(16)])]
    pallas_call x0 -> x5, Pallas kernels: none -> 8.35 us  [the longest x1 3.72 us: body(): kernel(score_kernel, 'scores', (shape((ROWS, KEYS), bf16), shape((2, ROWS...]
    dot_general x3 -> x0, matrix products: 7.59 us -> none  [the longest x2 6.35 us: masked_logits(): jnp.einsum('qhd,kd->hqk', q_three, portion, preferred_element_type=jnp.fl...]
    all_to_all x0 -> x1, starting transfers between devices: none -> 7.36 us  [body(): lax.all_to_all(cols.reshape(BLOCKS * HEADS, 1, HALF), ('y', 'x', 'zl', 'c...]
    unnamed x2 -> x12, local copies, waits for them, and re-layouts: 0.01 us -> 7.31 us
  transfers between devices with their start and end apart: 2 -> 5, of which waited for: 2 -> 3; matrix products, arithmetic and copies ran while one was open for 5% -> 0% of each run, Pallas kernels for 0% -> 3%
where the time goes in v2:
time: 72.5 us; the launch traced here: 71.4 us
  starting transfers between devices  24.4 us (34%)
  blocking collectives  23.5 us (32%)
  Pallas kernels  8.35 us (12%)
  local copies, waits for them, and re-layouts  7.92 us (11%)
  waiting for transfers between devices  6.29 us (9%)
    all_to_all x1, blocking collectives, body(): near = lax.all_to_all(copies, ('y', 'x'), 0, 0, tiled=True)  23.5 us
    ppermute x3, starting transfers between devices, partner(): return lax.ppermute(x, ('zh', 'zl', 'c'), [(i, i ^ 12) for i in range(16)])  15 us
    all_to_all x1, starting transfers between devices, body(): lax.all_to_all(cols.reshape(BLOCKS * HEADS, 1, HALF), ('y', 'x', 'zl', 'c...  7.36 us
    unnamed x12, local copies, waits for them, and re-layouts  7.31 us
    ppermute x3, waiting for transfers between devices, partner(): return lax.ppermute(x, ('zh', 'zl', 'c'), [(i, i ^ 12) for i in range(16)])  6.28 us
    pallas_call x1, Pallas kernels, body(): kernel(score_kernel, 'scores', (shape((ROWS, KEYS), bf16), shape((2, ROWS...  3.72 us
    ppermute x1, starting transfers between devices, across(): return lax.ppermute(x, 'c', [(0, 1), (1, 0)])  1.98 us
    pallas_call x1, Pallas kernels, body(): kernel(column_kernel, 'columns', shape((BLOCKS * HEADS, HALF), f32), [SME...  1.85 us
  transfers between devices with their start and end apart: 5, of which 3 were waited for; matrix products, arithmetic and copies ran while one was open for 0% of the time, Pallas kernels for 3%

profile of v2, /device:TPU:1, one launch (start us, length us, event | category | flops | bytes accessed | tf_op | source)
XLA Modules:
  0.0 71.4 jit_solution(241224188765418169)
XLA Ops:
  0.6 0.1 pad_add_fusion.place_ref
  0.7 0.8 %copy-done.2 = bf16[256,128]{1,0:T(8,128)(2,1)S(1)} copy-done((bf16[256,128]{1,0:T(8,128)(2,1)S(1)}, bf16[256,128]{1,0:T(8,128)(2,1)}, u32[]{:S(2)}) %copy-start.2) | copy-done | bytes 65560
  1.6 0.8 %copy-done.3 = bf16[256,128]{1,0:T(8,128)(2,1)S(1)} copy-done((bf16[256,128]{1,0:T(8,128)(2,1)S(1)}, bf16[256,128]{1,0:T(8,128)(2,1)}, u32[]{:S(2)}) %copy-start.3) | copy-done | bytes 65560
  2.4 0.7 %spread.1 = bf16[16,2,128,128]{3,2,1,0:T(8,128)(2,1)S(1)} custom-call(s32[4]{0:T(128)S(1)} %pad_add_fusion.place_ref, bf16[256,128]{1,0:T(8,128)(2,1)S(1)} %copy-done.2, bf16[256,128]{1,0:T(8,128)(2,1)S(1)} %copy-done.3), custom_call_target="tpu_custom_call" | custom-call | tf_op jit(solution)/shard_map/spread/pallas_call | solution.py:144
  3.1 23.5 %all_to_all.10.near_ref = bf16[16,2,128,128]{3,2,1,0:T(8,128)(2,1)S(1)} all-to-all(bf16[16,2,128,128]{3,2,1,0:T(8,128)(2,1)S(1)} %spread.1), channel_id=1, replica_groups=mesh['y'=4,'zh'=2,'x'=4,'zl'=4,'c'=2] {'y','x'}, dimensions={0} | all-to-all | bytes 2097152 | tf_op jit(solution)/shard_map/all_to_all | solution.py:148
  26.7 2.0 %collective-permute-start = (bf16[16,2,128,128]{3,2,1,0:T(8,128)(2,1)S(1)}, bf16[16,2,128,128]{3,2,1,0:T(8,128)(2,1)S(1)}, u32[]{:S(2)}, u32[]{:S(2)}) collective-permute-start(bf16[16,2,128,128]{3,2,1,0:T(8,128)(2,1)S(1)} %all_to_all.10.near_ref), channel_id=1, source_target_pairs={{0,1},{1,0},{2,3},{3,2},{4,5},{5,4},{6,7},{7,6},{8,9},{9,8},{10,11... | collective-permute-start | bytes 3145736 | tf_op jit(solution)/shard_map/ppermute | solution.py:139
  28.6 6.0 %collective-permute-start.1 = (bf16[256,128]{1,0:T(8,128)(2,1)}, bf16[256,128]{1,0:T(8,128)(2,1)S(1)}, u32[]{:S(2)}, u32[]{:S(2)}) collective-permute-start(bf16[256,128]{1,0:T(8,128)(2,1)} %own_ref.1), channel_id=1, source_target_pairs={{0,36},{1,37},{2,38},{3,39},{4,32},{5,33},{6,34},{7,35},{32,4},{33... | collective-permute-start | bytes 196616 | tf_op jit(solution)/shard_map/ppermute | solution.py:142
  34.7 3.1 %collective-permute-done.1.other_ref = bf16[256,128]{1,0:T(8,128)(2,1)S(1)} collective-permute-done((bf16[256,128]{1,0:T(8,128)(2,1)}, bf16[256,128]{1,0:T(8,128)(2,1)S(1)}, u32[]{:S(2)}, u32[]{:S(2)}) %collective-permute-start.1) | collective-permute-done | bytes 65568 | tf_op jit(solution)/shard_map/ppermute | solution.py:142
  37.8 0.8 %copy-done.4 = bf16[256,128]{1,0:T(8,128)(2,1)S(1)} copy-done((bf16[256,128]{1,0:T(8,128)(2,1)S(1)}, bf16[256,128]{1,0:T(8,128)(2,1)}, u32[]{:S(2)}) %copy-start.4) | copy-done | bytes 65560
  38.6 0.7 copy-done.5
  39.3 3.7 %scores.1 = (bf16[512,4096]{1,0:T(8,128)(2,1)S(1)}, f32[2,512]{1,0:T(2,128)S(1)}) custom-call(s32[4]{0:T(128)S(1)} %pad_add_fusion.place_ref, s32[4]{0:T(128)S(1)} %copy-done.5, bf16[16,2,128,128]{3,2,1,0:T(8,128)(2,1)S(1)} %all_to_all.10.near_ref, bf16[16,2,128,128]{3,2,1,0:T(8,128)(2,1)S(1)} %collective-permute-done.far_ref, ...), custom_call_target="tpu_custom_call" | custom-call | tf_op jit(solution)/shard_map/scores/pallas_call | solution.py:150
  43.0 4.4 %collective-permute-start.3 = (f32[2,512]{1,0:T(2,128)S(1)}, f32[2,512]{1,0:T(2,128)S(1)}, u32[]{:S(2)}, u32[]{:S(2)}) collective-permute-start(f32[2,512]{1,0:T(2,128)S(1)} %get-tuple-element.9.mine_ref), channel_id=1, source_target_pairs={{0,36},{1,37},{2,38},{3,39},{4,32},{5,33},{6,34},{7,35},{32,4},{33... | collective-permute-start | bytes 12296 | tf_op jit(solution)/shard_map/ppermute | solution.py:142
  47.4 1.0 %collective-permute-done.3.theirs_ref = f32[2,512]{1,0:T(2,128)S(1)} collective-permute-done((f32[2,512]{1,0:T(2,128)S(1)}, f32[2,512]{1,0:T(2,128)S(1)}, u32[]{:S(2)}, u32[]{:S(2)}) %collective-permute-start.3) | collective-permute-done | bytes 4128 | tf_op jit(solution)/shard_map/ppermute | solution.py:142
  48.4 1.8 %columns.1 = f32[128,128]{1,0:T(8,128)} custom-call(s32[4]{0:T(128)S(1)} %pad_add_fusion.place_ref, bf16[512,4096]{1,0:T(8,128)(2,1)S(1)} %get-tuple-element.6.probs_ref, f32[2,512]{1,0:T(2,128)S(1)} %get-tuple-element.9.mine_ref, f32[2,512]{1,0:T(2,128)S(1)} %collective-permute-done.3.theirs_ref), custom_call_target="tpu_custom_call" | custom-call | tf_op jit(solution)/shard_map/columns/pallas_call | solution.py:163
  50.2 2.0 %copy-done = bf16[512,4096]{1,0:T(8,128)(2,1)} copy-done((bf16[512,4096]{1,0:T(8,128)(2,1)}, bf16[512,4096]{1,0:T(8,128)(2,1)S(1)}, u32[]{:S(2)}) %copy-start) | copy-done | bytes 4194328
  52.2 7.4 %all-to-all-start.1 = ((f32[128,1,128]{2,1,0:T(1,128)}), f32[128,1,128]{2,1,0:T(1,128)S(1)}, u32[]{:S(2)}, u32[]{:S(2)}) async-start(f32[128,1,128]{2,1,0:T(1,128)} %bitcast.5), calls=%async_computation.1 | async-start | bytes 131072 | tf_op jit(solution)/shard_map/all_to_all | solution.py:166
  59.6 2.2 %copy-done.1 = bf16[512,4096]{1,0:T(8,128)(2,1)S(1)} copy-done((bf16[512,4096]{1,0:T(8,128)(2,1)S(1)}, bf16[512,4096]{1,0:T(8,128)(2,1)}, u32[]{:S(2)}) %copy-start.1) | copy-done | bytes 4194328
  61.8 1.2 %rows.1 = (f32[256,128]{1,0:T(8,128)S(1)}, bf16[256,128]{1,0:T(8,128)(2,1)S(1)}) custom-call(bf16[512,4096]{1,0:T(8,128)(2,1)S(1)} %copy-done.1, bf16[16,2,128,128]{3,2,1,0:T(8,128)(2,1)S(1)} %all_to_all.10.near_ref, bf16[16,2,128,128]{3,2,1,0:T(8,128)(2,1)S(1)} %collective-permute-done.far_ref), custom_call_target="tpu_custom_call" | custom-call | tf_op jit(solution)/shard_map/rows/pallas_call | solution.py:159
  63.0 4.6 %collective-permute-start.2 = (bf16[256,128]{1,0:T(8,128)(2,1)S(1)}, bf16[256,128]{1,0:T(8,128)(2,1)S(1)}, u32[]{:S(2)}, u32[]{:S(2)}) collective-permute-start(bf16[256,128]{1,0:T(8,128)(2,1)S(1)} %get-tuple-element.8), channel_id=1, source_target_pairs={{0,36},{1,37},{2,38},{3,39},{4,32},{5,33},{6,34},{7,35},{32,4},{33... | collective-permute-start | bytes 196616 | tf_op jit(solution)/shard_map/ppermute | solution.py:142
  67.6 2.2 %collective-permute-done.2.got_ref = bf16[256,128]{1,0:T(8,128)(2,1)S(1)} collective-permute-done((bf16[256,128]{1,0:T(8,128)(2,1)S(1)}, bf16[256,128]{1,0:T(8,128)(2,1)S(1)}, u32[]{:S(2)}, u32[]{:S(2)}) %collective-permute-start.2) | collective-permute-done | bytes 65568 | tf_op jit(solution)/shard_map/ppermute | solution.py:142
  69.8 0.8 %merge.1 = bf16[256,128]{1,0:T(8,128)(2,1)} custom-call(f32[256,128]{1,0:T(8,128)S(1)} %get-tuple-element.7.keep_ref, bf16[256,128]{1,0:T(8,128)(2,1)S(1)} %collective-permute-done.2.got_ref, f32[2,512]{1,0:T(2,128)S(1)} %get-tuple-element.9.mine_ref, f32[2,512]{1,0:T(2,128)S(1)} %collective-permute-done.3.theirs_ref), custom_call_target="tpu_custom_call" | custom-call | tf_op jit(solution)/shard_map/merge/pallas_call | solution.py:167
  70.6 0.2 reduce_sum.9
  70.7 0.1 div.10
  70.8 0.5 dynamic-slice_bitcast_fusion
  (9 shorter events, 0.0 us)
Async XLA Ops:
  0.7 0.8 %copy-start.2 = (bf16[256,128]{1,0:T(8,128)(2,1)S(1)}, bf16[256,128]{1,0:T(8,128)(2,1)}, u32[]{:S(2)}) copy-start(bf16[256,128]{1,0:T(8,128)(2,1)} %keys_ref.1) | copy-start | bytes 196612
  1.6 0.8 %copy-start.3 = (bf16[256,128]{1,0:T(8,128)(2,1)S(1)}, bf16[256,128]{1,0:T(8,128)(2,1)}, u32[]{:S(2)}) copy-start(bf16[256,128]{1,0:T(8,128)(2,1)} %values_ref.1) | copy-start | bytes 196612
  26.7 11.1 %collective-permute-start = (bf16[16,2,128,128]{3,2,1,0:T(8,128)(2,1)S(1)}, bf16[16,2,128,128]{3,2,1,0:T(8,128)(2,1)S(1)}, u32[]{:S(2)}, u32[]{:S(2)}) collective-permute-start(bf16[16,2,128,128]{3,2,1,0:T(8,128)(2,1)S(1)} %all_to_all.10.near_ref), channel_id=1, source_target_pairs={{0,1},{1,0},{2,3},{3,2},{4,5},{5,4},{6,7},{7,6},{8,9},{9,8},{10,11... | collective-permute-start | bytes 3145736 | tf_op jit(solution)/shard_map/ppermute | solution.py:139
  28.6 9.1 %collective-permute-start.1 = (bf16[256,128]{1,0:T(8,128)(2,1)}, bf16[256,128]{1,0:T(8,128)(2,1)S(1)}, u32[]{:S(2)}, u32[]{:S(2)}) collective-permute-start(bf16[256,128]{1,0:T(8,128)(2,1)} %own_ref.1), channel_id=1, source_target_pairs={{0,36},{1,37},{2,38},{3,39},{4,32},{5,33},{6,34},{7,35},{32,4},{33... | collective-permute-start | bytes 196616 | tf_op jit(solution)/shard_map/ppermute | solution.py:142
  37.8 0.8 %copy-start.4 = (bf16[256,128]{1,0:T(8,128)(2,1)S(1)}, bf16[256,128]{1,0:T(8,128)(2,1)}, u32[]{:S(2)}) copy-start(bf16[256,128]{1,0:T(8,128)(2,1)} %own_ref.1) | copy-start | bytes 196612
  38.6 0.7 copy-start.5
  43.0 5.4 %collective-permute-start.3 = (f32[2,512]{1,0:T(2,128)S(1)}, f32[2,512]{1,0:T(2,128)S(1)}, u32[]{:S(2)}, u32[]{:S(2)}) collective-permute-start(f32[2,512]{1,0:T(2,128)S(1)} %get-tuple-element.9.mine_ref), channel_id=1, source_target_pairs={{0,36},{1,37},{2,38},{3,39},{4,32},{5,33},{6,34},{7,35},{32,4},{33... | collective-permute-start | bytes 12296 | tf_op jit(solution)/shard_map/ppermute | solution.py:142
  50.2 2.0 %copy-start = (bf16[512,4096]{1,0:T(8,128)(2,1)}, bf16[512,4096]{1,0:T(8,128)(2,1)S(1)}, u32[]{:S(2)}) copy-start(bf16[512,4096]{1,0:T(8,128)(2,1)S(1)} %get-tuple-element.6.probs_ref) | copy-start | bytes 12582916
  52.2 18.4 %all-to-all-start.1 = ((f32[128,1,128]{2,1,0:T(1,128)}), f32[128,1,128]{2,1,0:T(1,128)S(1)}, u32[]{:S(2)}, u32[]{:S(2)}) async-start(f32[128,1,128]{2,1,0:T(1,128)} %bitcast.5), calls=%async_computation.1 | async-start | bytes 131072 | tf_op jit(solution)/shard_map/all_to_all | solution.py:166
  59.6 2.2 %copy-start.1 = (bf16[512,4096]{1,0:T(8,128)(2,1)S(1)}, bf16[512,4096]{1,0:T(8,128)(2,1)}, u32[]{:S(2)}) copy-start(bf16[512,4096]{1,0:T(8,128)(2,1)} %copy-done) | copy-start | bytes 12582916
  63.0 6.8 %collective-permute-start.2 = (bf16[256,128]{1,0:T(8,128)(2,1)S(1)}, bf16[256,128]{1,0:T(8,128)(2,1)S(1)}, u32[]{:S(2)}, u32[]{:S(2)}) collective-permute-start(bf16[256,128]{1,0:T(8,128)(2,1)S(1)} %get-tuple-element.8), channel_id=1, source_target_pairs={{0,36},{1,37},{2,38},{3,39},{4,32},{5,33},{6,34},{7,35},{32,4},{33... | collective-permute-start | bytes 196616 | tf_op jit(solution)/shard_map/ppermute | solution.py:142

commit v3 on v2

v3 whole, which is shorter than its diff:
```python
import functools
import math

import jax
import jax.numpy as jnp
from jax import lax
from jax.experimental import pallas as pl
from jax.experimental.pallas import tpu as pltpu
from jax.sharding import Mesh, PartitionSpec as P

HD = 128
HEADS = 8
AXES = {"y": 4, "zh": 2, "x": 4, "u": 2, "s": 2, "c": 2}
NX = AXES["x"]
TOK = 256
CHUNK = TOK // HEADS
PART = 2 * CHUNK
BLOCKS = AXES["y"] * NX
SIDE = BLOCKS * PART
KEYS = 2 * SIDE
FLIPS = 4
ROWS = FLIPS * TOK
TILE = 512
LANES = 128
SCALE = math.log2(math.e) / math.sqrt(HD)
MIB = 1024 * 1024
VMEM = pl.BlockSpec(memory_space=pltpu.VMEM)
SMEM = pl.BlockSpec(memory_space=pltpu.SMEM)
ANY = pl.BlockSpec(memory_space=pl.ANY)


def spread_kernel(place_ref, keys_ref, values_ref, out_ref, k_ref, v_ref, sems):
    copies = [
        pltpu.make_async_copy(keys_ref, k_ref, sems.at[0]),
        pltpu.make_async_copy(values_ref, v_ref, sems.at[1]),
    ]
    for copy in copies:
        copy.start()
    s, c = place_ref[3], place_ref[4]
    for n, (copy, ref) in enumerate(zip(copies, (k_ref, v_ref))):
        copy.wait()
        for u in range(2):
            piece = ref[pl.ds(pl.multiple_of(((u * 2 + s) * 2 + c) * CHUNK, CHUNK), CHUNK), :]
            for i in range(BLOCKS):
                out_ref[i, n, u * CHUNK : (u + 1) * CHUNK] = piece


def score_kernel(place_ref, docs_ref, near_ref, far_ref, q0, q1, q2, q3, probs_ref, stats_ref, raw_ref):
    y, zh, x, s, c = (place_ref[i] for i in range(5))
    e0 = docs_ref[0]
    e1 = e0 + docs_ref[1]
    e2 = e1 + docs_ref[2]
    own = (y * 8 + zh * 4 + x) * TOK
    other = (y * 8 + (1 - zh) * 4 + x) * TOK
    row = lax.broadcasted_iota(jnp.int32, (ROWS, LANES), 0)
    pos = jnp.where(row < 2 * TOK, own, other) + lax.rem(row, TOK)
    start = jnp.zeros_like(pos)
    for end in (e0, e1, e2):
        start = jnp.where(pos >= end, end, start)
    lane = lax.broadcasted_iota(jnp.int32, (1, LANES), 1)
    queries = jnp.concatenate([q[...] for q in (q0, q1, q2, q3)], axis=0)

    peak = jnp.full((ROWS, LANES), -1e30, jnp.float32)
    per = TILE // PART
    for t in range(KEYS // TILE):
        ref, side = (near_ref, c) if t * TILE < SIDE else (far_ref, 1 - c)
        first = t * per % BLOCKS
        block = ref[pl.ds(first, per), 0].reshape(TILE, HD)
        raw = lax.dot_general(queries, block, (((1,), (1,)), ((), ())), preferred_element_type=jnp.float32)
        for j in range(TILE // LANES):
            source = first + j * (LANES // PART) + lane // PART
            key_pos = (
                (source // NX * 8 + zh * 4 + source % NX) * TOK
                + ((lane % PART // CHUNK * 2 + s) * 2 + side) * CHUNK
                + lane % CHUNK
            )
            part = raw[:, j * LANES : (j + 1) * LANES]
            part = jnp.where((key_pos >= start) & (key_pos <= pos), part, -jnp.inf)
            raw_ref[:, t * TILE + j * LANES : t * TILE + (j + 1) * LANES] = part
            peak = jnp.maximum(peak, part)
    row_max = jnp.max(peak, axis=1, keepdims=True)

    total = jnp.zeros((ROWS, LANES), jnp.float32)
    for j in range(KEYS // LANES):
        cut = slice(j * LANES, (j + 1) * LANES)
        probs = jnp.exp2((raw_ref[:, cut] - row_max) * SCALE)
        probs_ref[:, cut] = probs.astype(jnp.bfloat16)
        total = total + probs
    row_sum = jnp.sum(total, axis=1, keepdims=True)
    first_lane = lax.broadcasted_iota(jnp.int32, (ROWS, LANES), 1) == 0
    stats_ref[...] = jnp.where(first_lane, row_max, row_sum).T[0:2, :]


def value_kernel(probs_ref, near_ref, far_ref, keep_ref, a_ref, b_ref, ab_ref):
    acc = jnp.dot(probs_ref[:, :SIDE], near_ref[:, 1].reshape(SIDE, HD), preferred_element_type=jnp.float32)
    acc += jnp.dot(probs_ref[:, SIDE:], far_ref[:, 1].reshape(SIDE, HD), preferred_element_type=jnp.float32)
    keep_ref[...] = acc[:TOK]
    for k, ref in enumerate((a_ref, b_ref, ab_ref)):
        ref[...] = acc[(k + 1) * TOK : (k + 2) * TOK].astype(jnp.bfloat16)


def shares(refs):
    parts = []
    for flip, ref in enumerate(refs):
        both = jnp.concatenate([ref[:, (k ^ flip) * TOK : ((k ^ flip) + 1) * TOK] for k in range(FLIPS)], axis=1)
        parts.append((both[0:1, :], both[1:2, :]))
    top = functools.reduce(jnp.maximum, [m for m, _ in parts])
    weights = [jnp.exp2((m - top) * SCALE) for m, _ in parts]
    norm = sum(w * l for w, (_, l) in zip(weights, parts))
    return [w / norm for w in weights]


def column_kernel(place_ref, probs_ref, s0, s1, s2, s3, a_ref, cols_ref):
    weight = shares((s0, s1, s2, s3))[0]
    high = weight.astype(jnp.bfloat16).astype(jnp.float32)
    row = lax.broadcasted_iota(jnp.int32, (8, ROWS), 0)
    both = jnp.where(row == 0, high, jnp.where(row == 1, weight - high, 0.0)).astype(jnp.bfloat16)
    straight = place_ref[4] == 0

    def line(first):
        sums = jnp.dot(both, probs_ref[:, first : first + 2 * LANES], preferred_element_type=jnp.float32)
        return jnp.sum(sums, axis=0, keepdims=True)

    row8 = lax.broadcasted_iota(jnp.int32, (8, LANES), 0)
    for b in range(0, SIDE // LANES, 2):
        near, far = line(b * LANES), line(SIDE + b * LANES)
        even, odd = jnp.where(straight, near, far), jnp.where(straight, far, near)
        for i in range(2):
            cut = slice(i * LANES, (i + 1) * LANES)
            cols_ref[(b + i) * 8 : (b + i + 1) * 8, :] = jnp.where(row8 % 2 == 0, even[:, cut], odd[:, cut])


def merge_kernel(keep_ref, a_ref, b_ref, ab_ref, s0, s1, s2, s3, out_ref):
    weights = shares((s0, s1, s2, s3))
    out = jnp.zeros((TOK, HD), jnp.float32)
    for w, ref in zip(weights, (keep_ref, a_ref, b_ref, ab_ref)):
        out += ref[...].astype(jnp.float32) * jnp.broadcast_to(w[:, :TOK], (HD, TOK)).T
    out_ref[...] = out.astype(jnp.bfloat16)


def kernel(fn, name, shapes, specs, scratch=(), limit=24):
    return pl.pallas_call(
        fn,
        out_shape=shapes,
        in_specs=specs,
        out_specs=jax.tree.map(lambda _: VMEM, shapes),
        scratch_shapes=scratch,
        compiler_params=pltpu.CompilerParams(vmem_limit_bytes=limit * MIB),
        name=name,
    )


def body(queries, keys, values, doc_lengths):
    shape = jax.ShapeDtypeStruct
    f32, bf16 = jnp.float32, jnp.bfloat16
    place = jnp.stack([lax.axis_index(a) for a in ("y", "zh", "x", "s", "c")]).astype(jnp.int32)

    def across(x):
        return lax.ppermute(x, "c", [(0, 1), (1, 0)])

    def flipped(x, flip):
        mask = {1: 2, 2: 12, 3: 14}[flip]
        return lax.ppermute(x, ("zh", "u", "s", "c"), [(i, i ^ mask) for i in range(16)])

    copies = kernel(
        spread_kernel,
        "spread",
        shape((BLOCKS, 2, PART, HD), bf16),
        [SMEM, ANY, ANY],
        [pltpu.VMEM((TOK, HD), bf16), pltpu.VMEM((TOK, HD), bf16), pltpu.SemaphoreType.DMA((2,))],
    )(place, keys, values)
    others = [flipped(queries, k) for k in (1, 2, 3)]
    near = lax.all_to_all(copies, ("y", "x"), 0, 0, tiled=True)
    near, others = lax.optimization_barrier((near, others))
    far = across(near)
    probs, mine = kernel(
        score_kernel,
        "scores",
        (shape((ROWS, KEYS), bf16), shape((2, ROWS), f32)),
        [SMEM, SMEM] + [VMEM] * 6,
        [pltpu.VMEM((ROWS, KEYS), f32)],
        limit=32,
    )(place, doc_lengths, near, far, queries, *others)
    stats = [mine] + [flipped(mine, k) for k in (1, 2, 3)]
    keep, *send = kernel(
        value_kernel, "rows", (shape((TOK, HD), f32),) + (shape((TOK, HD), bf16),) * 3, [VMEM, VMEM, VMEM]
    )(probs, near, far)
    got = [flipped(piece, k + 1) for k, piece in enumerate(send)]
    cols = kernel(column_kernel, "columns", shape((BLOCKS * 4, LANES), f32), [SMEM] + [VMEM] * 5 + [ANY])(
        place, probs, *stats, send[0]
    )
    parts = lax.all_to_all(cols.reshape(BLOCKS * 4, 1, LANES), ("y", "x", "u", "c"), 0, 0, tiled=True)
    rows = kernel(merge_kernel, "merge", shape((TOK, HD), bf16), [VMEM] * 8)(keep, *got, *stats)
    totals = (jnp.sum(parts, axis=(0, 1)) / HEADS).reshape(LANES // CHUNK, CHUNK)
    piece = lax.rem(lax.axis_index("x"), 2) * 2 + lax.axis_index("u")
    return rows, lax.dynamic_index_in_dim(totals, piece, 0, keepdims=False)


def solution(mesh):
    fine = Mesh(mesh.devices.reshape(tuple(AXES.values())), tuple(AXES))
    ctx, head = ("y", "zh", "x"), ("u", "s", "c")
    return jax.shard_map(
        body,
        mesh=fine,
        in_specs=(P(ctx, head), P(ctx, None), P(ctx, None), P()),
        out_specs=(P(ctx, head), P(ctx + head)),
        check_vma=False,
    )
```

time: 72.5 us -> 66.4 us (0.916); the launches traced: 71.4 us -> 66 us
  blocking collectives: 23.5 us -> 0 us
  starting transfers between devices: 24.4 us -> 37.9 us
  waiting for transfers between devices: 6.29 us -> 14.1 us
  local copies, waits for them, and re-layouts: 7.92 us -> 3.86 us
  Pallas kernels: 8.35 us -> 9.34 us
    all_to_all x1 -> x0, blocking collectives: 23.5 us -> none  [body(): near = lax.all_to_all(copies, ('y', 'x'), 0, 0, tiled=True)]
    all_to_all x1 -> x2, starting transfers between devices: 7.36 us -> 18 us  [the longest x1 10.4 us: body(): lax.all_to_all(cols.reshape(BLOCKS * 4, 1, LANES), ('y', 'x', 'u', 'c'),...]
    all_to_all x1 -> x2, waiting for transfers between devices: 0.01 us -> 7.74 us  [the longest x1 7.74 us: body(): lax.all_to_all(cols.reshape(BLOCKS * 4, 1, LANES), ('y', 'x', 'u', 'c'),...]
    unnamed x12 -> x8, local copies, waits for them, and re-layouts: 7.31 us -> 3.17 us
    ppermute x3 -> x9, starting transfers between devices: 15 us -> 17.5 us  [flipped(): lax.ppermute(x, ('zh', 'u', 's', 'c'), [(i, i ^ mask) for i in range(16)])]
    ppermute x1, waiting for transfers between devices: 0.01 us -> 1.54 us  [across(): return lax.ppermute(x, 'c', [(0, 1), (1, 0)])]
    ppermute x3 -> x9, waiting for transfers between devices: 6.28 us -> 4.84 us  [flipped(): lax.ppermute(x, ('zh', 'u', 's', 'c'), [(i, i ^ mask) for i in range(16)])]
    pallas_call x4, Pallas kernels: 4.63 us -> 5.56 us  [the longest x1 1.83 us: body(): kernel(column_kernel, 'columns', shape((BLOCKS * 4, LANES), f32), [SMEM]...]
  transfers between devices with their start and end apart: 5 -> 12, of which waited for: 3 -> 5; matrix products, arithmetic and copies ran while one was open for 0% -> 0% of each run, Pallas kernels for 3% -> 6%
where the time goes in v3:
time: 66.4 us; the launch traced here: 66 us
  starting transfers between devices  37.9 us (57%)
  waiting for transfers between devices  14.1 us (21%)
  Pallas kernels  9.34 us (14%)
  local copies, waits for them, and re-layouts  3.86 us (6%)
  between operations  0.72 us (1%)
    ppermute x9, starting transfers between devices, flipped(): lax.ppermute(x, ('zh', 'u', 's', 'c'), [(i, i ^ mask) for i in range(16)])  17.5 us
    all_to_all x1, starting transfers between devices, body(): lax.all_to_all(cols.reshape(BLOCKS * 4, 1, LANES), ('y', 'x', 'u', 'c'),...  10.4 us
    all_to_all x1, waiting for transfers between devices, body(): lax.all_to_all(cols.reshape(BLOCKS * 4, 1, LANES), ('y', 'x', 'u', 'c'),...  7.74 us
    all_to_all x1, starting transfers between devices, body(): near = lax.all_to_all(copies, ('y', 'x'), 0, 0, tiled=True)  7.6 us
    ppermute x9, waiting for transfers between devices, flipped(): lax.ppermute(x, ('zh', 'u', 's', 'c'), [(i, i ^ mask) for i in range(16)])  4.84 us
    pallas_call x1, Pallas kernels, body(): kernel(score_kernel, 'scores', (shape((ROWS, KEYS), bf16), shape((2, ROWS...  3.78 us
    unnamed x8, local copies, waits for them, and re-layouts  3.17 us
    ppermute x1, starting transfers between devices, across(): return lax.ppermute(x, 'c', [(0, 1), (1, 0)])  2.44 us
  transfers between devices with their start and end apart: 12, of which 5 were waited for; matrix products, arithmetic and copies ran while one was open for 0% of the time, Pallas kernels for 6%

profile of v3, /device:TPU:1, one launch (start us, length us, event | category | flops | bytes accessed | tf_op | source)
XLA Modules:
  0.0 66.0 jit_solution(8652145280268034152)
XLA Ops:
  0.7 0.8 %copy-done = bf16[256,128]{1,0:T(8,128)(2,1)S(1)} copy-done((bf16[256,128]{1,0:T(8,128)(2,1)S(1)}, bf16[256,128]{1,0:T(8,128)(2,1)}, u32[]{:S(2)}) %copy-start) | copy-done | bytes 65560
  1.6 0.8 %copy-done.1 = bf16[256,128]{1,0:T(8,128)(2,1)S(1)} copy-done((bf16[256,128]{1,0:T(8,128)(2,1)S(1)}, bf16[256,128]{1,0:T(8,128)(2,1)}, u32[]{:S(2)}) %copy-start.1) | copy-done | bytes 65560
  2.4 1.6 %spread.1 = bf16[16,2,64,128]{3,2,1,0:T(8,128)(2,1)} custom-call(s32[5]{0:T(128)S(1)} %stack.23.place_ref, bf16[256,128]{1,0:T(8,128)(2,1)S(1)} %copy-done, bf16[256,128]{1,0:T(8,128)(2,1)S(1)} %copy-done.1), custom_call_target="tpu_custom_call" | custom-call | tf_op jit(solution)/shard_map/spread/pallas_call | solution.py:165
  4.0 7.6 %all-to-all-start = ((bf16[16,2,64,128]{3,2,1,0:T(8,128)(2,1)}), bf16[16,2,64,128]{3,2,1,0:T(8,128)(2,1)S(1)}, u32[]{:S(2)}, u32[]{:S(2)}) async-start(bf16[16,2,64,128]{3,2,1,0:T(8,128)(2,1)} %spread.1), calls=%async_computation | async-start | bytes 1048576 | tf_op jit(solution)/shard_map/all_to_all | solution.py:173
  11.6 6.1 %collective-permute-start.1 = (bf16[256,128]{1,0:T(8,128)(2,1)}, bf16[256,128]{1,0:T(8,128)(2,1)S(1)}, u32[]{:S(2)}, u32[]{:S(2)}) collective-permute-start(bf16[256,128]{1,0:T(8,128)(2,1)} %q0.1), channel_id=1, source_target_pairs={{0,36},{1,37},{2,38},{3,39},{4,32},{5,33},{6,34},{7,35},{32,4},{33... | collective-permute-start | bytes 196616 | tf_op jit(solution)/shard_map/ppermute | solution.py:163
  17.7 0.7 %collective-permute-start = (bf16[256,128]{1,0:T(8,128)(2,1)}, bf16[256,128]{1,0:T(8,128)(2,1)S(1)}, u32[]{:S(2)}, u32[]{:S(2)}) collective-permute-start(bf16[256,128]{1,0:T(8,128)(2,1)} %q0.1), channel_id=1, source_target_pairs={{0,2},{1,3},{2,0},{3,1},{4,6},{5,7},{6,4},{7,5},{32,34},{33,35},{3... | collective-permute-start | bytes 196616 | tf_op jit(solution)/shard_map/ppermute | solution.py:163
  18.5 1.4 %collective-permute-done.1.q2 = bf16[256,128]{1,0:T(8,128)(2,1)S(1)} collective-permute-done((bf16[256,128]{1,0:T(8,128)(2,1)}, bf16[256,128]{1,0:T(8,128)(2,1)S(1)}, u32[]{:S(2)}, u32[]{:S(2)}) %collective-permute-start.1) | collective-permute-done | bytes 65568 | tf_op jit(solution)/shard_map/ppermute | solution.py:163
  19.9 1.5 %collective-permute-done.q1 = bf16[256,128]{1,0:T(8,128)(2,1)S(1)} collective-permute-done((bf16[256,128]{1,0:T(8,128)(2,1)}, bf16[256,128]{1,0:T(8,128)(2,1)S(1)}, u32[]{:S(2)}, u32[]{:S(2)}) %collective-permute-start) | collective-permute-done | bytes 65568 | tf_op jit(solution)/shard_map/ppermute | solution.py:163
  21.4 1.9 %collective-permute-done.2.q3 = bf16[256,128]{1,0:T(8,128)(2,1)S(1)} collective-permute-done((bf16[256,128]{1,0:T(8,128)(2,1)}, bf16[256,128]{1,0:T(8,128)(2,1)S(1)}, u32[]{:S(2)}, u32[]{:S(2)}) %collective-permute-start.2) | collective-permute-done | bytes 65568 | tf_op jit(solution)/shard_map/ppermute | solution.py:163
  23.3 2.4 %collective-permute-start.3 = (bf16[16,2,64,128]{3,2,1,0:T(8,128)(2,1)S(1)}, bf16[16,2,64,128]{3,2,1,0:T(8,128)(2,1)S(1)}, u32[]{:S(2)}, u32[]{:S(2)}) collective-permute-start(bf16[16,2,64,128]{3,2,1,0:T(8,128)(2,1)S(1)} %all-to-all-done.near_ref), channel_id=1, source_target_pairs={{0,1},{1,0},{2,3},{3,2},{4,5},{5,4},{6,7},{7,6},{8,9},{9,8},{10,11... | collective-permute-start | bytes 1572872 | tf_op jit(solution)/shard_map/ppermute | solution.py:159
  25.8 1.5 %collective-permute-done.3.far_ref = bf16[16,2,64,128]{3,2,1,0:T(8,128)(2,1)S(1)} collective-permute-done((bf16[16,2,64,128]{3,2,1,0:T(8,128)(2,1)S(1)}, bf16[16,2,64,128]{3,2,1,0:T(8,128)(2,1)S(1)}, u32[]{:S(2)}, u32[]{:S(2)}) %collective-permute-start.3) | collective-permute-done | bytes 524320 | tf_op jit(solution)/shard_map/ppermute | solution.py:159
  27.3 0.8 %copy-done.2 = bf16[256,128]{1,0:T(8,128)(2,1)S(1)} copy-done((bf16[256,128]{1,0:T(8,128)(2,1)S(1)}, bf16[256,128]{1,0:T(8,128)(2,1)}, u32[]{:S(2)}) %copy-start.2) | copy-done | bytes 65560
  28.1 0.7 copy-done.3
  28.8 3.8 %scores.1 = (bf16[1024,2048]{1,0:T(8,128)(2,1)S(1)}, f32[2,1024]{1,0:T(2,128)S(1)}) custom-call(s32[5]{0:T(128)S(1)} %stack.23.place_ref, s32[4]{0:T(128)S(1)} %copy-done.3, bf16[16,2,64,128]{3,2,1,0:T(8,128)(2,1)S(1)} %all-to-all-done.near_ref, bf16[16,2,64,128]{3,2,1,0:T(8,128)(2,1)S(1)} %collective-permute-done.3.far_ref, bf16[256,128]{1,0:T(8,128)(2,1)S(1)} %copy-done.2, ...), custom_call_target="tpu_custom_call" | custom-call | tf_op jit(solution)/shard_map/scores/pallas_call | solution.py:176
  32.6 4.0 %collective-permute-start.9 = (f32[2,1024]{1,0:T(2,128)S(1)}, f32[2,1024]{1,0:T(2,128)S(1)}, u32[]{:S(2)}, u32[]{:S(2)}) collective-permute-start(f32[2,1024]{1,0:T(2,128)S(1)} %get-tuple-element.21.s0), channel_id=1, source_target_pairs={{0,38},{1,39},{2,36},{3,37},{4,34},{5,35},{6,32},{7,33},{32,6},{33... | collective-permute-start | bytes 24584 | tf_op jit(solution)/shard_map/ppermute | solution.py:163
  36.6 1.8 %collective-permute-start.8 = (f32[2,1024]{1,0:T(2,128)S(1)}, f32[2,1024]{1,0:T(2,128)S(1)}, u32[]{:S(2)}, u32[]{:S(2)}) collective-permute-start(f32[2,1024]{1,0:T(2,128)S(1)} %get-tuple-element.21.s0), channel_id=1, source_target_pairs={{0,36},{1,37},{2,38},{3,39},{4,32},{5,33},{6,34},{7,35},{32,4},{33... | collective-permute-start | bytes 24584 | tf_op jit(solution)/shard_map/ppermute | solution.py:163
  38.4 1.2 %rows.1 = (f32[256,128]{1,0:T(8,128)S(1)}, bf16[256,128]{1,0:T(8,128)(2,1)S(1)}, bf16[256,128]{1,0:T(8,128)(2,1)S(1)}, bf16[256,128]{1,0:T(8,128)(2,1)S(1)}) custom-call(bf16[1024,2048]{1,0:T(8,128)(2,1)S(1)} %get-tuple-element.16.probs_ref, bf16[16,2,64,128]{3,2,1,0:T(8,128)(2,1)S(1)} %all-to-all-done.near_ref, ...), custom_call_target="tpu_custom_call" | custom-call | tf_op jit(solution)/shard_map/rows/pallas_call | solution.py:185
  39.6 3.5 %collective-permute-start.5 = (bf16[256,128]{1,0:T(8,128)(2,1)S(1)}, bf16[256,128]{1,0:T(8,128)(2,1)S(1)}, u32[]{:S(2)}, u32[]{:S(2)}) collective-permute-start(bf16[256,128]{1,0:T(8,128)(2,1)S(1)} %get-tuple-element.19), channel_id=1, source_target_pairs={{0,36},{1,37},{2,38},{3,39},{4,32},{5,33},{6,34},{7,35},{32,4},{33... | collective-permute-start | bytes 196616 | tf_op jit(solution)/shard_map/ppermute | solution.py:163
  43.6 0.9 %collective-permute-start.4 = (bf16[256,128]{1,0:T(8,128)(2,1)S(1)}, bf16[256,128]{1,0:T(8,128)(2,1)S(1)}, u32[]{:S(2)}, u32[]{:S(2)}) collective-permute-start(bf16[256,128]{1,0:T(8,128)(2,1)S(1)} %get-tuple-element.18.a_ref), channel_id=1, source_target_pairs={{0,2},{1,3},{2,0},{3,1},{4,6},{5,7},{6,4},{7,5},{32,34},{33,35},{3... | collective-permute-start | bytes 196616 | tf_op jit(solution)/shard_map/ppermute | solution.py:163
  44.5 1.8 %columns.1 = f32[64,128]{1,0:T(8,128)} custom-call(s32[5]{0:T(128)S(1)} %stack.23.place_ref, bf16[1024,2048]{1,0:T(8,128)(2,1)S(1)} %get-tuple-element.16.probs_ref, f32[2,1024]{1,0:T(2,128)S(1)} %get-tuple-element.21.s0, f32[2,1024]{1,0:T(2,128)S(1)} %collective-permute-done.7.s1, f32[2,1024]{1,0:T(2,128)S(1)} %collective-permute-done.8.s2, ...), custom_call_target="tpu_custom_call" | custom-call | tf_op jit(solution)/shard_map/columns/pallas_call | solution.py:189
  46.3 10.4 %all-to-all-start.1 = ((f32[64,1,128]{2,1,0:T(1,128)}), f32[64,1,128]{2,1,0:T(1,128)S(1)}, u32[]{:S(2)}, u32[]{:S(2)}) async-start(f32[64,1,128]{2,1,0:T(1,128)} %bitcast.6), calls=%async_computation.1 | async-start | bytes 65536 | tf_op jit(solution)/shard_map/all_to_all | solution.py:192
  56.7 0.9 %merge.1 = bf16[256,128]{1,0:T(8,128)(2,1)} custom-call(f32[256,128]{1,0:T(8,128)S(1)} %get-tuple-element.17.keep_ref, bf16[256,128]{1,0:T(8,128)(2,1)S(1)} %collective-permute-done.4.a_ref, bf16[256,128]{1,0:T(8,128)(2,1)S(1)} %collective-permute-done.5.b_ref, bf16[256,128]{1,0:T(8,128)(2,1)S(1)} %collective-permute-done.6.ab_ref, ...), custom_call_target="tpu_custom_call" | custom-call | tf_op jit(solution)/shard_map/merge/pallas_call | solution.py:193
  57.6 7.7 %all-to-all-done.1 = f32[64,1,128]{2,1,0:T(1,128)S(1)} async-done(((f32[64,1,128]{2,1,0:T(1,128)}), f32[64,1,128]{2,1,0:T(1,128)S(1)}, u32[]{:S(2)}, u32[]{:S(2)}) %all-to-all-start.1) | async-done | bytes 32800 | tf_op jit(solution)/shard_map/all_to_all | solution.py:192
  65.5 0.5 dynamic-slice_bitcast_fusion
  (18 shorter events, 0.8 us)
Async XLA Ops:
  0.7 0.8 %copy-start = (bf16[256,128]{1,0:T(8,128)(2,1)S(1)}, bf16[256,128]{1,0:T(8,128)(2,1)}, u32[]{:S(2)}) copy-start(bf16[256,128]{1,0:T(8,128)(2,1)} %keys_ref.1) | copy-start | bytes 196612
  1.6 0.8 %copy-start.1 = (bf16[256,128]{1,0:T(8,128)(2,1)S(1)}, bf16[256,128]{1,0:T(8,128)(2,1)}, u32[]{:S(2)}) copy-start(bf16[256,128]{1,0:T(8,128)(2,1)} %values_ref.1) | copy-start | bytes 196612
  4.0 19.3 %all-to-all-start = ((bf16[16,2,64,128]{3,2,1,0:T(8,128)(2,1)}), bf16[16,2,64,128]{3,2,1,0:T(8,128)(2,1)S(1)}, u32[]{:S(2)}, u32[]{:S(2)}) async-start(bf16[16,2,64,128]{3,2,1,0:T(8,128)(2,1)} %spread.1), calls=%async_computation | async-start | bytes 1048576 | tf_op jit(solution)/shard_map/all_to_all | solution.py:173
  11.6 8.3 %collective-permute-start.1 = (bf16[256,128]{1,0:T(8,128)(2,1)}, bf16[256,128]{1,0:T(8,128)(2,1)S(1)}, u32[]{:S(2)}, u32[]{:S(2)}) collective-permute-start(bf16[256,128]{1,0:T(8,128)(2,1)} %q0.1), channel_id=1, source_target_pairs={{0,36},{1,37},{2,38},{3,39},{4,32},{5,33},{6,34},{7,35},{32,4},{33... | collective-permute-start | bytes 196616 | tf_op jit(solution)/shard_map/ppermute | solution.py:163
  17.7 3.7 %collective-permute-start = (bf16[256,128]{1,0:T(8,128)(2,1)}, bf16[256,128]{1,0:T(8,128)(2,1)S(1)}, u32[]{:S(2)}, u32[]{:S(2)}) collective-permute-start(bf16[256,128]{1,0:T(8,128)(2,1)} %q0.1), channel_id=1, source_target_pairs={{0,2},{1,3},{2,0},{3,1},{4,6},{5,7},{6,4},{7,5},{32,34},{33,35},{3... | collective-permute-start | bytes 196616 | tf_op jit(solution)/shard_map/ppermute | solution.py:163
  18.5 4.8 %collective-permute-start.2 = (bf16[256,128]{1,0:T(8,128)(2,1)}, bf16[256,128]{1,0:T(8,128)(2,1)S(1)}, u32[]{:S(2)}, u32[]{:S(2)}) collective-permute-start(bf16[256,128]{1,0:T(8,128)(2,1)} %q0.1), channel_id=1, source_target_pairs={{0,38},{1,39},{2,36},{3,37},{4,34},{5,35},{6,32},{7,33},{32,6},{33... | collective-permute-start | bytes 196616 | tf_op jit(solution)/shard_map/ppermute | solution.py:163
  23.3 4.0 %collective-permute-start.3 = (bf16[16,2,64,128]{3,2,1,0:T(8,128)(2,1)S(1)}, bf16[16,2,64,128]{3,2,1,0:T(8,128)(2,1)S(1)}, u32[]{:S(2)}, u32[]{:S(2)}) collective-permute-start(bf16[16,2,64,128]{3,2,1,0:T(8,128)(2,1)S(1)} %all-to-all-done.near_ref), channel_id=1, source_target_pairs={{0,1},{1,0},{2,3},{3,2},{4,5},{5,4},{6,7},{7,6},{8,9},{9,8},{10,11... | collective-permute-start | bytes 1572872 | tf_op jit(solution)/shard_map/ppermute | solution.py:159
  27.3 0.8 %copy-start.2 = (bf16[256,128]{1,0:T(8,128)(2,1)S(1)}, bf16[256,128]{1,0:T(8,128)(2,1)}, u32[]{:S(2)}) copy-start(bf16[256,128]{1,0:T(8,128)(2,1)} %q0.1) | copy-start | bytes 196612
  28.1 0.7 copy-start.3
  32.6 11.0 %collective-permute-start.9 = (f32[2,1024]{1,0:T(2,128)S(1)}, f32[2,1024]{1,0:T(2,128)S(1)}, u32[]{:S(2)}, u32[]{:S(2)}) collective-permute-start(f32[2,1024]{1,0:T(2,128)S(1)} %get-tuple-element.21.s0), channel_id=1, source_target_pairs={{0,38},{1,39},{2,36},{3,37},{4,34},{5,35},{6,32},{7,33},{32,6},{33... | collective-permute-start | bytes 24584 | tf_op jit(solution)/shard_map/ppermute | solution.py:163
  36.6 7.9 %collective-permute-start.8 = (f32[2,1024]{1,0:T(2,128)S(1)}, f32[2,1024]{1,0:T(2,128)S(1)}, u32[]{:S(2)}, u32[]{:S(2)}) collective-permute-start(f32[2,1024]{1,0:T(2,128)S(1)} %get-tuple-element.21.s0), channel_id=1, source_target_pairs={{0,36},{1,37},{2,38},{3,39},{4,32},{5,33},{6,34},{7,35},{32,4},{33... | collective-permute-start | bytes 24584 | tf_op jit(solution)/shard_map/ppermute | solution.py:163
  38.4 6.1 %collective-permute-start.7 = (f32[2,1024]{1,0:T(2,128)S(1)}, f32[2,1024]{1,0:T(2,128)S(1)}, u32[]{:S(2)}, u32[]{:S(2)}) collective-permute-start(f32[2,1024]{1,0:T(2,128)S(1)} %get-tuple-element.21.s0), channel_id=1, source_target_pairs={{0,2},{1,3},{2,0},{3,1},{4,6},{5,7},{6,4},{7,5},{32,34},{33,35},{3... | collective-permute-start | bytes 24584 | tf_op jit(solution)/shard_map/ppermute | solution.py:163
  39.6 17.1 %collective-permute-start.5 = (bf16[256,128]{1,0:T(8,128)(2,1)S(1)}, bf16[256,128]{1,0:T(8,128)(2,1)S(1)}, u32[]{:S(2)}, u32[]{:S(2)}) collective-permute-start(bf16[256,128]{1,0:T(8,128)(2,1)S(1)} %get-tuple-element.19), channel_id=1, source_target_pairs={{0,36},{1,37},{2,38},{3,39},{4,32},{5,33},{6,34},{7,35},{32,4},{33... | collective-permute-start | bytes 196616 | tf_op jit(solution)/shard_map/ppermute | solution.py:163
  43.1 13.6 %collective-permute-start.6 = (bf16[256,128]{1,0:T(8,128)(2,1)S(1)}, bf16[256,128]{1,0:T(8,128)(2,1)S(1)}, u32[]{:S(2)}, u32[]{:S(2)}) collective-permute-start(bf16[256,128]{1,0:T(8,128)(2,1)S(1)} %get-tuple-element.20), channel_id=1, source_target_pairs={{0,38},{1,39},{2,36},{3,37},{4,34},{5,35},{6,32},{7,33},{32,6},{33... | collective-permute-start | bytes 196616 | tf_op jit(solution)/shard_map/ppermute | solution.py:163
  43.6 13.1 %collective-permute-start.4 = (bf16[256,128]{1,0:T(8,128)(2,1)S(1)}, bf16[256,128]{1,0:T(8,128)(2,1)S(1)}, u32[]{:S(2)}, u32[]{:S(2)}) collective-permute-start(bf16[256,128]{1,0:T(8,128)(2,1)S(1)} %get-tuple-element.18.a_ref), channel_id=1, source_target_pairs={{0,2},{1,3},{2,0},{3,1},{4,6},{5,7},{6,4},{7,5},{32,34},{33,35},{3... | collective-permute-start | bytes 196616 | tf_op jit(solution)/shard_map/ppermute | solution.py:163
  46.3 19.0 %all-to-all-start.1 = ((f32[64,1,128]{2,1,0:T(1,128)}), f32[64,1,128]{2,1,0:T(1,128)S(1)}, u32[]{:S(2)}, u32[]{:S(2)}) async-start(f32[64,1,128]{2,1,0:T(1,128)} %bitcast.6), calls=%async_computation.1 | async-start | bytes 65536 | tf_op jit(solution)/shard_map/all_to_all | solution.py:192

commit v4 on v2

v4 whole, which is shorter than its diff:
```python
import math

import jax
import jax.numpy as jnp
from jax import lax
from jax.experimental import pallas as pl
from jax.experimental.pallas import tpu as pltpu
from jax.sharding import Mesh, PartitionSpec as P

HD = 128
HEADS = 8
AXES = {"y": 4, "zh": 2, "x": 4, "zl": 4, "c": 2}
NX = AXES["x"]
TOK = 256
CHUNK = TOK // HEADS
HALF = TOK // 2
BLOCKS = AXES["y"] * NX
SIDE = BLOCKS * HALF
KEYS = 2 * SIDE
ROWS = 2 * TOK
TILE = 512
SCALE = math.log2(math.e) / math.sqrt(HD)
HEAD = 32
MIB = 1024 * 1024
VMEM = pl.BlockSpec(memory_space=pltpu.VMEM)
ANY = pl.BlockSpec(memory_space=pl.ANY)
SMEM = pl.BlockSpec(memory_space=pltpu.SMEM)


def my_half():
    return pl.ds(pl.multiple_of(lax.axis_index("c") * HALF, HALF), HALF)


def row_positions():
    y, zh, x = (lax.axis_index(a) for a in ("y", "zh", "x"))
    own = (y * 8 + zh * 4 + x) * TOK
    other = (y * 8 + (1 - zh) * 4 + x) * TOK
    row = lax.broadcasted_iota(jnp.int32, (ROWS, HALF), 0)
    return jnp.where(row < TOK, own, other) + lax.rem(row, TOK)


def spread_kernel(keys_ref, values_ref, out_ref, piece_ref, in_sems, out_sems):
    reads = [
        pltpu.make_async_copy(ref.at[my_half()], piece_ref.at[n], in_sems.at[n])
        for n, ref in enumerate((keys_ref, values_ref))
    ]
    for copy in reads:
        copy.start()
    for copy in reads:
        copy.wait()
    writes = [pltpu.make_async_copy(piece_ref, out_ref.at[i], out_sems.at[i]) for i in range(BLOCKS)]
    for copy in writes:
        copy.start()
    for copy in writes:
        copy.wait()


def limit_kernel(docs_ref, own_ref, q_ref, start_ref):
    q_ref[...] = own_ref[...]
    pos = row_positions()
    start = jnp.zeros_like(pos)
    end = 0
    for i in range(3):
        end = end + docs_ref[i]
        start = jnp.where(pos >= end, end, start)
    start_ref[...] = start


def masked_logits(keys_ref, half, own_ref, other_ref, start_ref, raw_ref):
    zh = lax.axis_index("zh")
    pos, start = row_positions(), start_ref[...]
    lane = lax.broadcasted_iota(jnp.int32, (1, HALF), 1)
    queries = jnp.concatenate([own_ref[...], other_ref[...]], axis=0)
    peak = jnp.full((ROWS, HALF), -1e30, jnp.float32)
    per = TILE // HALF
    for t in range(SIDE // TILE):
        block = keys_ref[pl.ds(t * per, per)].reshape(TILE, HD)
        raw = lax.dot_general(queries, block, (((1,), (1,)), ((), ())), preferred_element_type=jnp.float32)
        for j in range(per):
            source = t * per + j
            key_pos = (source // NX * 8 + zh * 4 + source % NX) * TOK + half * HALF + lane
            part = raw[:, j * HALF : (j + 1) * HALF]
            part = jnp.where((key_pos >= start) & (key_pos <= pos), part, -jnp.inf)
            raw_ref[:, source * HALF : (source + 1) * HALF] = part
            peak = jnp.maximum(peak, part)
    return peak


def near_kernel(near_ref, own_ref, other_ref, start_ref, raw_ref, peak_ref):
    peak_ref[...] = masked_logits(near_ref, lax.axis_index("c"), own_ref, other_ref, start_ref, raw_ref)


def score_kernel(
    k_ref, own_ref, other_ref, start_ref, near_raw_ref, peak_ref, near_ref, far_ref,
    probs_ref, stats_ref, keep_ref, send_ref, far_raw_ref,
):
    peak = masked_logits(k_ref, 1 - lax.axis_index("c"), own_ref, other_ref, start_ref, far_raw_ref)
    row_max = jnp.max(jnp.maximum(peak, peak_ref[...]), axis=1, keepdims=True)
    total = jnp.zeros((ROWS, HALF), jnp.float32)
    for side, raw_ref in enumerate((near_raw_ref, far_raw_ref)):
        for j in range(BLOCKS):
            probs = jnp.exp2((raw_ref[:, j * HALF : (j + 1) * HALF] - row_max) * SCALE)
            first = side * SIDE + j * HALF
            probs_ref[:, first : first + HALF] = probs.astype(jnp.bfloat16)
            total = total + probs
    acc = jnp.dot(probs_ref[:, :SIDE], near_ref[...].reshape(SIDE, HD), preferred_element_type=jnp.float32)
    acc += jnp.dot(probs_ref[:, SIDE:], far_ref[...].reshape(SIDE, HD), preferred_element_type=jnp.float32)
    row_sum = jnp.sum(total, axis=1, keepdims=True)
    first_lane = lax.broadcasted_iota(jnp.int32, (ROWS, HALF), 1) == 0
    stats = jnp.where(first_lane, row_max, row_sum).T[0:2, :]
    stats_ref[...] = stats
    pieces, rest = [], stats
    for _ in range(3):
        piece = rest.astype(jnp.bfloat16).astype(jnp.float32)
        pieces.append(piece)
        rest = rest - piece
    table = jnp.concatenate(pieces + [jnp.zeros_like(rest)], axis=0)
    table = jnp.concatenate([table[:, i * 128 : (i + 1) * 128] for i in range(ROWS // 128)], axis=0)
    keep_ref[...] = acc[:TOK]
    send_ref[0:HEAD, :] = table.astype(jnp.bfloat16)
    send_ref[HEAD:, :] = acc[TOK:].astype(jnp.bfloat16)


def shares(mine_ref, got_ref):
    table = got_ref[0:HEAD, :].astype(jnp.float32)
    rows = []
    for i in (2, 3, 0, 1):
        part = table[i * 8 : (i + 1) * 8]
        rows.append(part[0:2] + part[2:4] + part[4:6])
    both = jnp.concatenate(rows, axis=1)
    m0, l0, m1, l1 = mine_ref[0:1, :], mine_ref[1:2, :], both[0:1, :], both[1:2, :]
    top = jnp.maximum(m0, m1)
    w0, w1 = jnp.exp2((m0 - top) * SCALE), jnp.exp2((m1 - top) * SCALE)
    norm = w0 * l0 + w1 * l1
    return w0 / norm, w1 / norm


def column_kernel(probs_ref, mine_ref, got_ref, cols_ref):
    weight, _ = shares(mine_ref, got_ref)
    high = weight.astype(jnp.bfloat16).astype(jnp.float32)
    row = lax.broadcasted_iota(jnp.int32, (8, ROWS), 0)
    both = jnp.where(row == 0, high, jnp.where(row == 1, weight - high, 0.0)).astype(jnp.bfloat16)
    straight = lax.axis_index("c") == 0

    def line(first):
        sums = jnp.dot(both, probs_ref[:, first : first + 2 * HALF], preferred_element_type=jnp.float32)
        return jnp.sum(sums, axis=0, keepdims=True)

    row8 = lax.broadcasted_iota(jnp.int32, (8, HALF), 0)
    for b in range(0, BLOCKS, 2):
        near, far = line(b * HALF), line(SIDE + b * HALF)
        low, top = jnp.where(straight, near, far), jnp.where(straight, far, near)
        for i in range(2):
            cut = slice(i * HALF, (i + 1) * HALF)
            cols_ref[(b + i) * 8 : (b + i + 1) * 8, :] = jnp.where(row8 < 4, low[:, cut], top[:, cut])


def merge_kernel(keep_ref, got_ref, mine_ref, out_ref):
    w0, w1 = shares(mine_ref, got_ref)
    w0 = jnp.broadcast_to(w0[:, :TOK], (HD, TOK)).T
    w1 = jnp.broadcast_to(w1[:, :TOK], (HD, TOK)).T
    got = got_ref[HEAD:, :].astype(jnp.float32)
    out_ref[...] = (keep_ref[...] * w0 + got * w1).astype(jnp.bfloat16)


def kernel(fn, name, shapes, specs, scratch=(), limit=8, space=VMEM):
    return pl.pallas_call(
        fn,
        out_shape=shapes,
        in_specs=specs,
        out_specs=jax.tree.map(lambda _: space, shapes),
        scratch_shapes=scratch,
        compiler_params=pltpu.CompilerParams(vmem_limit_bytes=limit * MIB),
        name=name,
    )


def body(queries, keys, values, doc_lengths):
    shape = jax.ShapeDtypeStruct
    f32, bf16 = jnp.float32, jnp.bfloat16
    def across(x):
        return lax.ppermute(x, "c", [(0, 1), (1, 0)])

    def partner(x):
        return lax.ppermute(x, ("zh", "zl", "c"), [(i, i ^ 12) for i in range(16)])

    copies = kernel(
        spread_kernel,
        "spread",
        shape((BLOCKS, 2, HALF, HD), bf16),
        [ANY] * 2,
        [
            pltpu.VMEM((2, HALF, HD), bf16),
            pltpu.SemaphoreType.DMA((2,)),
            pltpu.SemaphoreType.DMA((BLOCKS,)),
        ],
        limit=60,
        space=ANY,
    )(keys, values)
    near = lax.all_to_all(copies, ("y", "x"), 0, 0, tiled=True)
    other = partner(queries)
    own, start = kernel(
        limit_kernel, "limits", (shape((TOK, HD), bf16), shape((ROWS, HALF), jnp.int32)), [SMEM, VMEM]
    )(doc_lengths, queries)
    near, other, own, start = lax.optimization_barrier((near, other, own, start))
    k_near, v_near = near[:, 0], near[:, 1]
    k_far, v_far = across(k_near), across(v_near)
    raw, peak = kernel(
        near_kernel, "near_scores", (shape((ROWS, SIDE), f32), shape((ROWS, HALF), f32)), [VMEM] * 4, limit=12
    )(k_near, own, other, start)
    probs, mine, keep, send = kernel(
        score_kernel,
        "scores",
        (
            shape((ROWS, KEYS), bf16),
            shape((2, ROWS), f32),
            shape((TOK, HD), f32),
            shape((HEAD + TOK, HD), bf16),
        ),
        [VMEM] * 8,
        [pltpu.VMEM((ROWS, SIDE), f32)],
        limit=20,
    )(k_far, own, other, start, raw, peak, v_near, v_far)
    got = partner(send)
    cols = kernel(column_kernel, "columns", shape((BLOCKS * HEADS, HALF), f32), [VMEM] * 3)(probs, mine, got)
    parts = lax.all_to_all(cols.reshape(BLOCKS * HEADS, 1, HALF), ("y", "x", "zl", "c"), 0, 0, tiled=True)
    rows = kernel(merge_kernel, "merge", shape((TOK, HD), bf16), [VMEM] * 3)(keep, got, mine)
    totals = (jnp.sum(parts, axis=(0, 1)) / HEADS).reshape(HALF // CHUNK, CHUNK)
    piece = lax.rem(lax.axis_index("zl") * 2 + lax.axis_index("c"), HALF // CHUNK)
    return rows, lax.dynamic_index_in_dim(totals, piece, 0, keepdims=False)


def solution(mesh):
    fine = Mesh(mesh.devices.reshape(tuple(AXES.values())), tuple(AXES))
    ctx, head = ("y", "zh", "x"), ("zl", "c")
    return jax.shard_map(
        body,
        mesh=fine,
        in_specs=(P(ctx, head), P(ctx, None), P(ctx, None), P()),
        out_specs=(P(ctx, head), P(ctx + head)),
        check_vma=False,
    )
```

time: 72.5 us -> 63.7 us (0.88); the launches traced: 71.4 us -> 63.4 us
  blocking collectives: 23.5 us -> 0 us
  waiting for transfers between devices: 6.29 us -> 20.9 us
  local copies, waits for them, and re-layouts: 7.92 us -> 2.21 us
  starting transfers between devices: 24.4 us -> 29.3 us
  Pallas kernels: 8.35 us -> 10.1 us
    all_to_all x1 -> x0, blocking collectives: 23.5 us -> none  [body(): near = lax.all_to_all(copies, ('y', 'x'), 0, 0, tiled=True)]
    all_to_all x1, waiting for transfers between devices: 0.01 us -> 8.92 us  [body(): lax.all_to_all(cols.reshape(BLOCKS * HEADS, 1, HALF), ('y', 'x', 'zl', 'c...]
    all_to_all x0 -> x1, waiting for transfers between devices: none -> 7.71 us  [body(): near = lax.all_to_all(copies, ('y', 'x'), 0, 0, tiled=True)]
    all_to_all x0 -> x1, starting transfers between devices: none -> 7.6 us  [body(): near = lax.all_to_all(copies, ('y', 'x'), 0, 0, tiled=True)]
    unnamed x12 -> x4, local copies, waits for them, and re-layouts: 7.31 us -> 1.53 us
    ppermute x3 -> x2, waiting for transfers between devices: 6.28 us -> 3 us  [partner(): return lax.ppermute(x, ('zh', 'zl', 'c'), [(i, i ^ 12) for i in range(16)])]
    ppermute x3 -> x2, starting transfers between devices: 15 us -> 12.2 us  [partner(): return lax.ppermute(x, ('zh', 'zl', 'c'), [(i, i ^ 12) for i in range(16)])]
    ppermute x1 -> x2, waiting for transfers between devices: 0.01 us -> 1.27 us  [across(): return lax.ppermute(x, 'c', [(0, 1), (1, 0)])]
  transfers between devices with their start and end apart: 5 -> 6, of which waited for: 3 -> 5; matrix products, arithmetic and copies ran while one was open for 0% -> 0% of each run, Pallas kernels for 3% -> 4%
where the time goes in v4:
time: 63.7 us; the launch traced here: 63.4 us
  starting transfers between devices  29.3 us (46%)
  waiting for transfers between devices  20.9 us (33%)
  Pallas kernels  10.1 us (16%)
  local copies, waits for them, and re-layouts  2.21 us (3%)
  between operations  0.71 us (1%)
    ppermute x2, starting transfers between devices, partner(): return lax.ppermute(x, ('zh', 'zl', 'c'), [(i, i ^ 12) for i in range(16)])  12.2 us
    all_to_all x1, waiting for transfers between devices, body(): lax.all_to_all(cols.reshape(BLOCKS * HEADS, 1, HALF), ('y', 'x', 'zl', 'c...  8.92 us
    all_to_all x1, waiting for transfers between devices, body(): near = lax.all_to_all(copies, ('y', 'x'), 0, 0, tiled=True)  7.71 us
    all_to_all x1, starting transfers between devices, body(): near = lax.all_to_all(copies, ('y', 'x'), 0, 0, tiled=True)  7.6 us
    all_to_all x1, starting transfers between devices, body(): lax.all_to_all(cols.reshape(BLOCKS * HEADS, 1, HALF), ('y', 'x', 'zl', 'c...  6.69 us
    pallas_call x1, Pallas kernels, body(): kernel(score_kernel, 'scores', (shape((ROWS, KEYS), bf16), shape((2, ROWS...  4.51 us
    ppermute x2, waiting for transfers between devices, partner(): return lax.ppermute(x, ('zh', 'zl', 'c'), [(i, i ^ 12) for i in range(16)])  3 us
    ppermute x2, starting transfers between devices, across(): return lax.ppermute(x, 'c', [(0, 1), (1, 0)])  2.8 us
  transfers between devices with their start and end apart: 6, of which 5 were waited for; matrix products, arithmetic and copies ran while one was open for 0% of the time, Pallas kernels for 4%

profile of v4, /device:TPU:1, one launch (start us, length us, event | category | flops | bytes accessed | tf_op | source)
XLA Modules:
  0.0 63.4 jit_solution(10019981869625415072)
XLA Ops:
  0.6 1.9 %spread.1 = bf16[16,2,128,128]{3,2,1,0:T(8,128)(2,1)} custom-call(bf16[256,128]{1,0:T(8,128)(2,1)} %keys_ref.1, bf16[256,128]{1,0:T(8,128)(2,1)} %values_ref.1), custom_call_target="tpu_custom_call" | custom-call | tf_op jit(solution)/shard_map/spread/pallas_call | solution.py:187
  2.5 7.6 %all-to-all-start = ((bf16[16,2,128,128]{3,2,1,0:T(8,128)(2,1)}), bf16[16,2,128,128]{3,2,1,0:T(8,128)(2,1)S(1)}, u32[]{:S(2)}, u32[]{:S(2)}) async-start(bf16[16,2,128,128]{3,2,1,0:T(8,128)(2,1)} %spread.1), calls=%async_computation | async-start | bytes 2097152 | tf_op jit(solution)/shard_map/all_to_all | solution.py:200
  10.2 6.1 %collective-permute-start = (bf16[256,128]{1,0:T(8,128)(2,1)}, bf16[256,128]{1,0:T(8,128)(2,1)S(1)}, u32[]{:S(2)}, u32[]{:S(2)}) collective-permute-start(bf16[256,128]{1,0:T(8,128)(2,1)} %own_ref.1), channel_id=1, source_target_pairs={{0,36},{1,37},{2,38},{3,39},{4,32},{5,33},{6,34},{7,35},{32,4},{33... | collective-permute-start | bytes 196616 | tf_op jit(solution)/shard_map/ppermute | solution.py:185
  16.3 0.9 %copy-done = bf16[256,128]{1,0:T(8,128)(2,1)S(1)} copy-done((bf16[256,128]{1,0:T(8,128)(2,1)S(1)}, bf16[256,128]{1,0:T(8,128)(2,1)}, u32[]{:S(2)}) %copy-start) | copy-done | bytes 65560
  17.1 0.7 %copy-done.1 = s32[4]{0:T(128)S(1)} copy-done((s32[4]{0:T(128)S(1)}, s32[4]{0:T(128)}, u32[]{:S(2)}) %copy-start.1) | copy-done | bytes 40
  17.8 0.6 limits.1
  18.4 0.0 collective-permute-done.other_ref
  18.4 7.7 %all-to-all-done = bf16[16,2,128,128]{3,2,1,0:T(8,128)(2,1)S(1)} async-done(((bf16[16,2,128,128]{3,2,1,0:T(8,128)(2,1)}), bf16[16,2,128,128]{3,2,1,0:T(8,128)(2,1)S(1)}, u32[]{:S(2)}, u32[]{:S(2)}) %all-to-all-start) | async-done | bytes 1048608 | tf_op jit(solution)/shard_map/all_to_all | solution.py:200
  26.1 0.1 slice_bitcast_fusion
  26.2 2.7 %collective-permute-start.1 = (bf16[16,128,128]{2,1,0:T(8,128)(2,1)S(1)}, bf16[16,128,128]{2,1,0:T(8,128)(2,1)S(1)}, u32[]{:S(2)}, u32[]{:S(2)}) collective-permute-start(bf16[16,128,128]{2,1,0:T(8,128)(2,1)S(1)} %get-tuple-element.27.near_ref), channel_id=1, source_target_pairs={{0,1},{1,0},{2,3},{3,2},{4,5},{5,4},{6,7},{7,6},{8,9},{9,8},{10,11... | collective-permute-start | bytes 1572872 | tf_op jit(solution)/shard_map/ppermute | solution.py:182
  28.9 0.1 collective-permute-start.2
  29.0 0.9 %near_scores.1 = (f32[512,2048]{1,0:T(8,128)S(1)}, f32[512,128]{1,0:T(8,128)S(1)}) custom-call(bf16[16,128,128]{2,1,0:T(8,128)(2,1)S(1)} %get-tuple-element.27.near_ref, bf16[256,128]{1,0:T(8,128)(2,1)S(1)} %get-tuple-element.17.own_ref, bf16[256,128]{1,0:T(8,128)(2,1)S(1)} %collective-permute-done.other_ref, s32[512,128]{1,0:T(8,128)S(1)} %get-tuple-element.19.start_ref), custom_call_target="tpu_custom_call" | custom-call | tf_op jit(solution)/shard_map/near_scores/pallas_call | solution.py:208
  29.9 0.5 collective-permute-done.1.k_ref
  30.5 0.7 %collective-permute-done.2.far_ref = bf16[16,128,128]{2,1,0:T(8,128)(2,1)S(1)} collective-permute-done((bf16[16,128,128]{2,1,0:T(8,128)(2,1)S(1)}, bf16[16,128,128]{2,1,0:T(8,128)(2,1)S(1)}, u32[]{:S(2)}, u32[]{:S(2)}) %collective-permute-start.2) | collective-permute-done | bytes 524320 | tf_op jit(solution)/shard_map/ppermute | solution.py:182
  31.2 4.5 %scores.1 = (bf16[512,4096]{1,0:T(8,128)(2,1)S(1)}, f32[2,512]{1,0:T(2,128)S(1)}, f32[256,128]{1,0:T(8,128)S(1)}, bf16[288,128]{1,0:T(8,128)(2,1)S(1)}) custom-call(bf16[16,128,128]{2,1,0:T(8,128)(2,1)S(1)} %collective-permute-done.1.k_ref, bf16[256,128]{1,0:T(8,128)(2,1)S(1)} %get-tuple-element.17.own_ref, ...), custom_call_target="tpu_custom_call" | custom-call | tf_op jit(solution)/shard_map/scores/pallas_call | solution.py:211
  35.7 6.1 %collective-permute-start.3 = (bf16[288,128]{1,0:T(8,128)(2,1)S(1)}, bf16[288,128]{1,0:T(8,128)(2,1)S(1)}, u32[]{:S(2)}, u32[]{:S(2)}) collective-permute-start(bf16[288,128]{1,0:T(8,128)(2,1)S(1)} %get-tuple-element.23), channel_id=1, source_target_pairs={{0,36},{1,37},{2,38},{3,39},{4,32},{5,33},{6,34},{7,35},{32,4},{33... | collective-permute-start | bytes 221192 | tf_op jit(solution)/shard_map/ppermute | solution.py:185
  41.8 3.0 %collective-permute-done.3.got_ref = bf16[288,128]{1,0:T(8,128)(2,1)S(1)} collective-permute-done((bf16[288,128]{1,0:T(8,128)(2,1)S(1)}, bf16[288,128]{1,0:T(8,128)(2,1)S(1)}, u32[]{:S(2)}, u32[]{:S(2)}) %collective-permute-start.3) | collective-permute-done | bytes 73760 | tf_op jit(solution)/shard_map/ppermute | solution.py:185
  44.8 1.3 %columns.1 = f32[128,128]{1,0:T(8,128)} custom-call(bf16[512,4096]{1,0:T(8,128)(2,1)S(1)} %get-tuple-element.25.probs_ref, f32[2,512]{1,0:T(2,128)S(1)} %get-tuple-element.24.mine_ref, bf16[288,128]{1,0:T(8,128)(2,1)S(1)} %collective-permute-done.3.got_ref), custom_call_target="tpu_custom_call" | custom-call | tf_op jit(solution)/shard_map/columns/pallas_call | solution.py:225
  46.2 6.7 %all-to-all-start.1 = ((f32[128,1,128]{2,1,0:T(1,128)}), f32[128,1,128]{2,1,0:T(1,128)S(1)}, u32[]{:S(2)}, u32[]{:S(2)}) async-start(f32[128,1,128]{2,1,0:T(1,128)} %bitcast.3), calls=%async_computation.1 | async-start | bytes 131072 | tf_op jit(solution)/shard_map/all_to_all | solution.py:226
  52.9 0.8 %merge.1 = bf16[256,128]{1,0:T(8,128)(2,1)} custom-call(f32[256,128]{1,0:T(8,128)S(1)} %get-tuple-element.22.keep_ref, bf16[288,128]{1,0:T(8,128)(2,1)S(1)} %collective-permute-done.3.got_ref, f32[2,512]{1,0:T(2,128)S(1)} %get-tuple-element.24.mine_ref), custom_call_target="tpu_custom_call" | custom-call | tf_op jit(solution)/shard_map/merge/pallas_call | solution.py:227
  53.7 8.9 %all-to-all-done.1 = f32[128,1,128]{2,1,0:T(1,128)S(1)} async-done(((f32[128,1,128]{2,1,0:T(1,128)}), f32[128,1,128]{2,1,0:T(1,128)S(1)}, u32[]{:S(2)}, u32[]{:S(2)}) %all-to-all-start.1) | async-done | bytes 65568 | tf_op jit(solution)/shard_map/all_to_all | solution.py:226
  62.6 0.2 reduce_sum.9
  62.7 0.1 div.10
  62.8 0.5 dynamic-slice_bitcast_fusion
  (3 shorter events, 0.0 us)
Async XLA Ops:
  2.5 23.6 %all-to-all-start = ((bf16[16,2,128,128]{3,2,1,0:T(8,128)(2,1)}), bf16[16,2,128,128]{3,2,1,0:T(8,128)(2,1)S(1)}, u32[]{:S(2)}, u32[]{:S(2)}) async-start(bf16[16,2,128,128]{3,2,1,0:T(8,128)(2,1)} %spread.1), calls=%async_computation | async-start | bytes 2097152 | tf_op jit(solution)/shard_map/all_to_all | solution.py:200
  10.2 8.3 %collective-permute-start = (bf16[256,128]{1,0:T(8,128)(2,1)}, bf16[256,128]{1,0:T(8,128)(2,1)S(1)}, u32[]{:S(2)}, u32[]{:S(2)}) collective-permute-start(bf16[256,128]{1,0:T(8,128)(2,1)} %own_ref.1), channel_id=1, source_target_pairs={{0,36},{1,37},{2,38},{3,39},{4,32},{5,33},{6,34},{7,35},{32,4},{33... | collective-permute-start | bytes 196616 | tf_op jit(solution)/shard_map/ppermute | solution.py:185
  16.3 0.9 %copy-start = (bf16[256,128]{1,0:T(8,128)(2,1)S(1)}, bf16[256,128]{1,0:T(8,128)(2,1)}, u32[]{:S(2)}) copy-start(bf16[256,128]{1,0:T(8,128)(2,1)} %own_ref.1) | copy-start | bytes 196612
  17.1 0.7 %copy-start.1 = (s32[4]{0:T(128)S(1)}, s32[4]{0:T(128)}, u32[]{:S(2)}) copy-start(s32[4]{0:T(128)} %docs_ref.1) | copy-start | bytes 52
  26.2 4.2 %collective-permute-start.1 = (bf16[16,128,128]{2,1,0:T(8,128)(2,1)S(1)}, bf16[16,128,128]{2,1,0:T(8,128)(2,1)S(1)}, u32[]{:S(2)}, u32[]{:S(2)}) collective-permute-start(bf16[16,128,128]{2,1,0:T(8,128)(2,1)S(1)} %get-tuple-element.27.near_ref), channel_id=1, source_target_pairs={{0,1},{1,0},{2,3},{3,2},{4,5},{5,4},{6,7},{7,6},{8,9},{9,8},{10,11... | collective-permute-start | bytes 1572872 | tf_op jit(solution)/shard_map/ppermute | solution.py:182
  28.9 2.3 %collective-permute-start.2 = (bf16[16,128,128]{2,1,0:T(8,128)(2,1)S(1)}, bf16[16,128,128]{2,1,0:T(8,128)(2,1)S(1)}, u32[]{:S(2)}, u32[]{:S(2)}) collective-permute-start(bf16[16,128,128]{2,1,0:T(8,128)(2,1)S(1)} %get-tuple-element.26.near_ref), channel_id=1, source_target_pairs={{0,1},{1,0},{2,3},{3,2},{4,5},{5,4},{6,7},{7,6},{8,9},{9,8},{10,11... | collective-permute-start | bytes 1572872 | tf_op jit(solution)/shard_map/ppermute | solution.py:182
  35.7 9.1 %collective-permute-start.3 = (bf16[288,128]{1,0:T(8,128)(2,1)S(1)}, bf16[288,128]{1,0:T(8,128)(2,1)S(1)}, u32[]{:S(2)}, u32[]{:S(2)}) collective-permute-start(bf16[288,128]{1,0:T(8,128)(2,1)S(1)} %get-tuple-element.23), channel_id=1, source_target_pairs={{0,36},{1,37},{2,38},{3,39},{4,32},{5,33},{6,34},{7,35},{32,4},{33... | collective-permute-start | bytes 221192 | tf_op jit(solution)/shard_map/ppermute | solution.py:185
  46.2 16.4 %all-to-all-start.1 = ((f32[128,1,128]{2,1,0:T(1,128)}), f32[128,1,128]{2,1,0:T(1,128)S(1)}, u32[]{:S(2)}, u32[]{:S(2)}) async-start(f32[128,1,128]{2,1,0:T(1,128)} %bitcast.3), calls=%async_computation.1 | async-start | bytes 131072 | tf_op jit(solution)/shard_map/all_to_all | solution.py:226

commit v5 on v4

--- a/solution.py
+++ b/solution.py
@@ -20,7 +20,7 @@
 ROWS = 2 * TOK
 TILE = 512
 SCALE = math.log2(math.e) / math.sqrt(HD)
-HEAD = 32
+LONG = 20_000_000_000
 MIB = 1024 * 1024
 VMEM = pl.BlockSpec(memory_space=pltpu.VMEM)
 ANY = pl.BlockSpec(memory_space=pl.ANY)
@@ -91,8 +91,7 @@
 
 
 def score_kernel(
-    k_ref, own_ref, other_ref, start_ref, near_raw_ref, peak_ref, near_ref, far_ref,
-    probs_ref, stats_ref, keep_ref, send_ref, far_raw_ref,
+    k_ref, own_ref, other_ref, start_ref, near_raw_ref, peak_ref, probs_ref, stats_ref, far_raw_ref
 ):
     peak = masked_logits(k_ref, 1 - lax.axis_index("c"), own_ref, other_ref, start_ref, far_raw_ref)
     row_max = jnp.max(jnp.maximum(peak, peak_ref[...]), axis=1, keepdims=True)
@@ -103,31 +102,21 @@
             first = side * SIDE + j * HALF
             probs_ref[:, first : first + HALF] = probs.astype(jnp.bfloat16)
             total = total + probs
+    row_sum = jnp.sum(total, axis=1, keepdims=True)
+    first_lane = lax.broadcasted_iota(jnp.int32, (ROWS, HALF), 1) == 0
+    stats_ref[...] = jnp.where(first_lane, row_max, row_sum).T[0:2, :]
+
+
+def row_kernel(probs_ref, near_ref, far_ref, keep_ref, send_ref):
     acc = jnp.dot(probs_ref[:, :SIDE], near_ref[...].reshape(SIDE, HD), preferred_element_type=jnp.float32)
     acc += jnp.dot(probs_ref[:, SIDE:], far_ref[...].reshape(SIDE, HD), preferred_element_type=jnp.float32)
-    row_sum = jnp.sum(total, axis=1, keepdims=True)
-    first_lane = lax.broadcasted_iota(jnp.int32, (ROWS, HALF), 1) == 0
-    stats = jnp.where(first_lane, row_max, row_sum).T[0:2, :]
-    stats_ref[...] = stats
-    pieces, rest = [], stats
-    for _ in range(3):
-        piece = rest.astype(jnp.bfloat16).astype(jnp.float32)
-        pieces.append(piece)
-        rest = rest - piece
-    table = jnp.concatenate(pieces + [jnp.zeros_like(rest)], axis=0)
-    table = jnp.concatenate([table[:, i * 128 : (i + 1) * 128] for i in range(ROWS // 128)], axis=0)
     keep_ref[...] = acc[:TOK]
-    send_ref[0:HEAD, :] = table.astype(jnp.bfloat16)
-    send_ref[HEAD:, :] = acc[TOK:].astype(jnp.bfloat16)
-
-
-def shares(mine_ref, got_ref):
-    table = got_ref[0:HEAD, :].astype(jnp.float32)
-    rows = []
-    for i in (2, 3, 0, 1):
-        part = table[i * 8 : (i + 1) * 8]
-        rows.append(part[0:2] + part[2:4] + part[4:6])
-    both = jnp.concatenate(rows, axis=1)
+    send_ref[...] = acc[TOK:].astype(jnp.bfloat16)
+
+
+def shares(mine_ref, theirs_ref):
+    both = theirs_ref[...]
+    both = jnp.concatenate([both[:, TOK:], both[:, :TOK]], axis=1)
     m0, l0, m1, l1 = mine_ref[0:1, :], mine_ref[1:2, :], both[0:1, :], both[1:2, :]
     top = jnp.maximum(m0, m1)
     w0, w1 = jnp.exp2((m0 - top) * SCALE), jnp.exp2((m1 - top) * SCALE)
@@ -135,8 +124,8 @@
     return w0 / norm, w1 / norm
 
 
-def column_kernel(probs_ref, mine_ref, got_ref, cols_ref):
-    weight, _ = shares(mine_ref, got_ref)
+def column_kernel(probs_ref, mine_ref, theirs_ref, cols_ref):
+    weight, _ = shares(mine_ref, theirs_ref)
     high = weight.astype(jnp.bfloat16).astype(jnp.float32)
     row = lax.broadcasted_iota(jnp.int32, (8, ROWS), 0)
     both = jnp.where(row == 0, high, jnp.where(row == 1, weight - high, 0.0)).astype(jnp.bfloat16)
@@ -155,15 +144,14 @@
             cols_ref[(b + i) * 8 : (b + i + 1) * 8, :] = jnp.where(row8 < 4, low[:, cut], top[:, cut])
 
 
-def merge_kernel(keep_ref, got_ref, mine_ref, out_ref):
-    w0, w1 = shares(mine_ref, got_ref)
+def merge_kernel(keep_ref, got_ref, mine_ref, theirs_ref, out_ref):
+    w0, w1 = shares(mine_ref, theirs_ref)
     w0 = jnp.broadcast_to(w0[:, :TOK], (HD, TOK)).T
     w1 = jnp.broadcast_to(w1[:, :TOK], (HD, TOK)).T
-    got = got_ref[HEAD:, :].astype(jnp.float32)
-    out_ref[...] = (keep_ref[...] * w0 + got * w1).astype(jnp.bfloat16)
-
-
-def kernel(fn, name, shapes, specs, scratch=(), limit=8, space=VMEM):
+    out_ref[...] = (keep_ref[...] * w0 + got_ref[...].astype(jnp.float32) * w1).astype(jnp.bfloat16)
+
+
+def kernel(fn, name, shapes, specs, scratch=(), limit=8, space=VMEM, flops=0):
     return pl.pallas_call(
         fn,
         out_shape=shapes,
@@ -171,6 +159,7 @@
         out_specs=jax.tree.map(lambda _: space, shapes),
         scratch_shapes=scratch,
         compiler_params=pltpu.CompilerParams(vmem_limit_bytes=limit * MIB),
+        cost_estimate=pl.CostEstimate(flops=flops, bytes_accessed=0, transcendentals=0) if flops else None,
         name=name,
     )
 
@@ -208,23 +197,24 @@
     raw, peak = kernel(
         near_kernel, "near_scores", (shape((ROWS, SIDE), f32), shape((ROWS, HALF), f32)), [VMEM] * 4, limit=12
     )(k_near, own, other, start)
-    probs, mine, keep, send = kernel(
+    probs, mine = kernel(
         score_kernel,
         "scores",
-        (
-            shape((ROWS, KEYS), bf16),
-            shape((2, ROWS), f32),
-            shape((TOK, HD), f32),
-            shape((HEAD + TOK, HD), bf16),
-        ),
-        [VMEM] * 8,
+        (shape((ROWS, KEYS), bf16), shape((2, ROWS), f32)),
+        [VMEM] * 6,
         [pltpu.VMEM((ROWS, SIDE), f32)],
         limit=20,
-    )(k_far, own, other, start, raw, peak, v_near, v_far)
+    )(k_far, own, other, start, raw, peak)
+    theirs = partner(mine)
+    keep, send = kernel(
+        row_kernel, "rows", (shape((TOK, HD), f32), shape((TOK, HD), bf16)), [VMEM] * 3, flops=LONG
+    )(probs, v_near, v_far)
     got = partner(send)
-    cols = kernel(column_kernel, "columns", shape((BLOCKS * HEADS, HALF), f32), [VMEM] * 3)(probs, mine, got)
+    cols = kernel(
+        column_kernel, "columns", shape((BLOCKS * HEADS, HALF), f32), [VMEM] * 3, flops=LONG
+    )(probs, mine, theirs)
     parts = lax.all_to_all(cols.reshape(BLOCKS * HEADS, 1, HALF), ("y", "x", "zl", "c"), 0, 0, tiled=True)
-    rows = kernel(merge_kernel, "merge", shape((TOK, HD), bf16), [VMEM] * 3)(keep, got, mine)
+    rows = kernel(merge_kernel, "merge", shape((TOK, HD), bf16), [VMEM] * 4, flops=LONG)(keep, got, mine, theirs)
     totals = (jnp.sum(parts, axis=(0, 1)) / HEADS).reshape(HALF // CHUNK, CHUNK)
     piece = lax.rem(lax.axis_index("zl") * 2 + lax.axis_index("c"), HALF // CHUNK)
     return rows, lax.dynamic_index_in_dim(totals, piece, 0, keepdims=False)

time: 63.7 us -> 59.2 us (0.929)
  waiting for transfers between devices: 20.9 us -> 17.2 us
  Pallas kernels: 10.1 us -> 9.12 us
    ppermute x2 -> x3, waiting for transfers between devices: 3 us -> 0.01 us  [partner(): return lax.ppermute(x, ('zh', 'zl', 'c'), [(i, i ^ 12) for i in range(16)])]
    pallas_call x1, Pallas kernels: 4.51 us -> 2.34 us  [body(): kernel(score_kernel, 'scores', (shape((ROWS, KEYS), bf16), shape((2, ROWS...]
    pallas_call x1 -> x2, Pallas kernels: 0.8 us -> 2.05 us  [the longest x1 1.25 us: body(): kernel(row_kernel, 'rows', (shape((TOK, HD), f32), shape((TOK, HD), bf16)...]
    ppermute x2, waiting for transfers between devices: 1.27 us -> 0.55 us  [across(): return lax.ppermute(x, 'c', [(0, 1), (1, 0)])]
    ppermute x2 -> x3, starting transfers between devices: 12.2 us -> 12.3 us  [partner(): return lax.ppermute(x, ('zh', 'zl', 'c'), [(i, i ^ 12) for i in range(16)])]
  transfers between devices with their start and end apart: 6 -> 7, of which waited for: 5 -> 3; matrix products, arithmetic and copies ran while one was open for 0% -> 0% of each run, Pallas kernels for 4% -> 12%
where the time goes in v5:
time: 59.2 us; the launch traced here: 58.9 us
  starting transfers between devices  29.5 us (50%)
  waiting for transfers between devices  17.2 us (29%)
  Pallas kernels  9.12 us (15%)
  local copies, waits for them, and re-layouts  2.23 us (4%)
  between operations  0.71 us (1%)
    ppermute x3, starting transfers between devices, partner(): return lax.ppermute(x, ('zh', 'zl', 'c'), [(i, i ^ 12) for i in range(16)])  12.3 us
    all_to_all x1, waiting for transfers between devices, body(): lax.all_to_all(cols.reshape(BLOCKS * HEADS, 1, HALF), ('y', 'x', 'zl', 'c...  8.91 us
    all_to_all x1, waiting for transfers between devices, body(): near = lax.all_to_all(copies, ('y', 'x'), 0, 0, tiled=True)  7.71 us
    all_to_all x1, starting transfers between devices, body(): near = lax.all_to_all(copies, ('y', 'x'), 0, 0, tiled=True)  7.6 us
    all_to_all x1, starting transfers between devices, body(): lax.all_to_all(cols.reshape(BLOCKS * HEADS, 1, HALF), ('y', 'x', 'zl', 'c...  6.76 us
    ppermute x2, starting transfers between devices, across(): return lax.ppermute(x, 'c', [(0, 1), (1, 0)])  2.8 us
    pallas_call x1, Pallas kernels, body(): kernel(score_kernel, 'scores', (shape((ROWS, KEYS), bf16), shape((2, ROWS...  2.34 us
    pallas_call x1, Pallas kernels, body(): kernel(spread_kernel, 'spread', shape((BLOCKS, 2, HALF, HD), bf16), [ANY]...  1.91 us
  transfers between devices with their start and end apart: 7, of which 3 were waited for; matrix products, arithmetic and copies ran while one was open for 0% of the time, Pallas kernels for 12%

profile of v5, /device:TPU:1, one launch (start us, length us, event | category | flops | bytes accessed | tf_op | source)
XLA Modules:
  0.0 58.9 jit_solution(15028879161276631351)
XLA Ops:
  0.6 1.9 %spread.1 = bf16[16,2,128,128]{3,2,1,0:T(8,128)(2,1)} custom-call(bf16[256,128]{1,0:T(8,128)(2,1)} %keys_ref.1, bf16[256,128]{1,0:T(8,128)(2,1)} %values_ref.1), custom_call_target="tpu_custom_call" | custom-call | tf_op jit(solution)/shard_map/spread/pallas_call | solution.py:176
  2.5 7.6 %all-to-all-start = ((bf16[16,2,128,128]{3,2,1,0:T(8,128)(2,1)}), bf16[16,2,128,128]{3,2,1,0:T(8,128)(2,1)S(1)}, u32[]{:S(2)}, u32[]{:S(2)}) async-start(bf16[16,2,128,128]{3,2,1,0:T(8,128)(2,1)} %spread.1), calls=%async_computation | async-start | bytes 2097152 | tf_op jit(solution)/shard_map/all_to_all | solution.py:189
  10.2 6.1 %collective-permute-start = (bf16[256,128]{1,0:T(8,128)(2,1)}, bf16[256,128]{1,0:T(8,128)(2,1)S(1)}, u32[]{:S(2)}, u32[]{:S(2)}) collective-permute-start(bf16[256,128]{1,0:T(8,128)(2,1)} %own_ref.1), channel_id=1, source_target_pairs={{0,36},{1,37},{2,38},{3,39},{4,32},{5,33},{6,34},{7,35},{32,4},{33... | collective-permute-start | bytes 196616 | tf_op jit(solution)/shard_map/ppermute | solution.py:174
  16.3 0.9 %copy-done = bf16[256,128]{1,0:T(8,128)(2,1)S(1)} copy-done((bf16[256,128]{1,0:T(8,128)(2,1)S(1)}, bf16[256,128]{1,0:T(8,128)(2,1)}, u32[]{:S(2)}) %copy-start) | copy-done | bytes 65560
  17.1 0.7 %copy-done.1 = s32[4]{0:T(128)S(1)} copy-done((s32[4]{0:T(128)S(1)}, s32[4]{0:T(128)}, u32[]{:S(2)}) %copy-start.1) | copy-done | bytes 40
  17.8 0.6 %limits.1 = (bf16[256,128]{1,0:T(8,128)(2,1)S(1)}, s32[512,128]{1,0:T(8,128)S(1)}) custom-call(s32[4]{0:T(128)S(1)} %copy-done.1, bf16[256,128]{1,0:T(8,128)(2,1)S(1)} %copy-done), custom_call_target="tpu_custom_call" | custom-call | tf_op jit(solution)/shard_map/limits/pallas_call | solution.py:191
  18.4 0.0 collective-permute-done.other_ref
  18.4 7.7 %all-to-all-done = bf16[16,2,128,128]{3,2,1,0:T(8,128)(2,1)S(1)} async-done(((bf16[16,2,128,128]{3,2,1,0:T(8,128)(2,1)}), bf16[16,2,128,128]{3,2,1,0:T(8,128)(2,1)S(1)}, u32[]{:S(2)}, u32[]{:S(2)}) %all-to-all-start) | async-done | bytes 1048608 | tf_op jit(solution)/shard_map/all_to_all | solution.py:189
  26.1 0.1 slice_bitcast_fusion
  26.2 2.7 %collective-permute-start.1 = (bf16[16,128,128]{2,1,0:T(8,128)(2,1)S(1)}, bf16[16,128,128]{2,1,0:T(8,128)(2,1)S(1)}, u32[]{:S(2)}, u32[]{:S(2)}) collective-permute-start(bf16[16,128,128]{2,1,0:T(8,128)(2,1)S(1)} %get-tuple-element.27.near_ref), channel_id=1, source_target_pairs={{0,1},{1,0},{2,3},{3,2},{4,5},{5,4},{6,7},{7,6},{8,9},{9,8},{10,11... | collective-permute-start | bytes 1572872 | tf_op jit(solution)/shard_map/ppermute | solution.py:171
  28.9 0.1 collective-permute-start.2
  29.1 0.9 %near_scores.1 = (f32[512,2048]{1,0:T(8,128)S(1)}, f32[512,128]{1,0:T(8,128)S(1)}) custom-call(bf16[16,128,128]{2,1,0:T(8,128)(2,1)S(1)} %get-tuple-element.27.near_ref, bf16[256,128]{1,0:T(8,128)(2,1)S(1)} %get-tuple-element.17.own_ref, bf16[256,128]{1,0:T(8,128)(2,1)S(1)} %collective-permute-done.other_ref, s32[512,128]{1,0:T(8,128)S(1)} %get-tuple-element.19.start_ref), custom_call_target="tpu_custom_call" | custom-call | tf_op jit(solution)/shard_map/near_scores/pallas_call | solution.py:197
  29.9 0.6 collective-permute-done.1.k_ref
  30.5 2.3 %scores.1 = (bf16[512,4096]{1,0:T(8,128)(2,1)S(1)}, f32[2,512]{1,0:T(2,128)S(1)}) custom-call(bf16[16,128,128]{2,1,0:T(8,128)(2,1)S(1)} %collective-permute-done.1.k_ref, bf16[256,128]{1,0:T(8,128)(2,1)S(1)} %get-tuple-element.17.own_ref, bf16[256,128]{1,0:T(8,128)(2,1)S(1)} %collective-permute-done.other_ref, s32[512,128]{1,0:T(8,128)S(1)} %get-tuple-element.19.start_ref, ...), custom_call_target="tpu_custom_call" | custom-call | tf_op jit(solution)/shard_map/scores/pallas_call | solution.py:200
  32.8 6.1 %collective-permute-start.4 = (f32[2,512]{1,0:T(2,128)S(1)}, f32[2,512]{1,0:T(2,128)S(1)}, u32[]{:S(2)}, u32[]{:S(2)}) collective-permute-start(f32[2,512]{1,0:T(2,128)S(1)} %get-tuple-element.25.mine_ref), channel_id=1, source_target_pairs={{0,36},{1,37},{2,38},{3,39},{4,32},{5,33},{6,34},{7,35},{32,4},{33... | collective-permute-start | bytes 12296 | tf_op jit(solution)/shard_map/ppermute | solution.py:174
  38.9 1.2 %rows.1 = (f32[256,128]{1,0:T(8,128)S(1)}, bf16[256,128]{1,0:T(8,128)(2,1)S(1)}) custom-call(bf16[512,4096]{1,0:T(8,128)(2,1)S(1)} %get-tuple-element.22.probs_ref, bf16[16,128,128]{2,1,0:T(8,128)(2,1)S(1)} %get-tuple-element.26.near_ref, bf16[16,128,128]{2,1,0:T(8,128)(2,1)S(1)} %collective-permute-done.2.far_ref), custom_call_target="tpu_custom_call" | custom-call | flops 20000000000 | tf_op jit(solution)/shard_map/rows/pallas_call | solution.py:209
  40.2 0.1 collective-permute-start.3
  40.3 1.3 %columns.1 = f32[128,128]{1,0:T(8,128)} custom-call(bf16[512,4096]{1,0:T(8,128)(2,1)S(1)} %get-tuple-element.22.probs_ref, f32[2,512]{1,0:T(2,128)S(1)} %get-tuple-element.25.mine_ref, f32[2,512]{1,0:T(2,128)S(1)} %collective-permute-done.4.theirs_ref), custom_call_target="tpu_custom_call" | custom-call | flops 20000000000 | tf_op jit(solution)/shard_map/columns/pallas_call | solution.py:213
  41.6 6.8 %all-to-all-start.1 = ((f32[128,1,128]{2,1,0:T(1,128)}), f32[128,1,128]{2,1,0:T(1,128)S(1)}, u32[]{:S(2)}, u32[]{:S(2)}) async-start(f32[128,1,128]{2,1,0:T(1,128)} %bitcast.3), calls=%async_computation.1 | async-start | bytes 131072 | tf_op jit(solution)/shard_map/all_to_all | solution.py:216
  48.4 0.8 %merge.1 = bf16[256,128]{1,0:T(8,128)(2,1)} custom-call(f32[256,128]{1,0:T(8,128)S(1)} %get-tuple-element.23.keep_ref, bf16[256,128]{1,0:T(8,128)(2,1)S(1)} %collective-permute-done.3.got_ref, f32[2,512]{1,0:T(2,128)S(1)} %get-tuple-element.25.mine_ref, f32[2,512]{1,0:T(2,128)S(1)} %collective-permute-done.4.theirs_ref), custom_call_target="tpu_custom_call" | custom-call | flops 20000000000 | tf_op jit(solution)/shard_map/merge/pallas_call | solution.py:217
  49.2 8.9 %all-to-all-done.1 = f32[128,1,128]{2,1,0:T(1,128)S(1)} async-done(((f32[128,1,128]{2,1,0:T(1,128)}), f32[128,1,128]{2,1,0:T(1,128)S(1)}, u32[]{:S(2)}, u32[]{:S(2)}) %all-to-all-start.1) | async-done | bytes 65568 | tf_op jit(solution)/shard_map/all_to_all | solution.py:216
  58.1 0.2 reduce_sum.9
  58.3 0.1 div.10
  58.3 0.5 dynamic-slice_bitcast_fusion
  (6 shorter events, 0.0 us)
Async XLA Ops:
  2.5 23.6 %all-to-all-start = ((bf16[16,2,128,128]{3,2,1,0:T(8,128)(2,1)}), bf16[16,2,128,128]{3,2,1,0:T(8,128)(2,1)S(1)}, u32[]{:S(2)}, u32[]{:S(2)}) async-start(bf16[16,2,128,128]{3,2,1,0:T(8,128)(2,1)} %spread.1), calls=%async_computation | async-start | bytes 2097152 | tf_op jit(solution)/shard_map/all_to_all | solution.py:189
  10.2 8.3 %collective-permute-start = (bf16[256,128]{1,0:T(8,128)(2,1)}, bf16[256,128]{1,0:T(8,128)(2,1)S(1)}, u32[]{:S(2)}, u32[]{:S(2)}) collective-permute-start(bf16[256,128]{1,0:T(8,128)(2,1)} %own_ref.1), channel_id=1, source_target_pairs={{0,36},{1,37},{2,38},{3,39},{4,32},{5,33},{6,34},{7,35},{32,4},{33... | collective-permute-start | bytes 196616 | tf_op jit(solution)/shard_map/ppermute | solution.py:174
  16.3 0.9 %copy-start = (bf16[256,128]{1,0:T(8,128)(2,1)S(1)}, bf16[256,128]{1,0:T(8,128)(2,1)}, u32[]{:S(2)}) copy-start(bf16[256,128]{1,0:T(8,128)(2,1)} %own_ref.1) | copy-start | bytes 196612
  17.1 0.7 %copy-start.1 = (s32[4]{0:T(128)S(1)}, s32[4]{0:T(128)}, u32[]{:S(2)}) copy-start(s32[4]{0:T(128)} %docs_ref.1) | copy-start | bytes 52
  26.2 4.2 %collective-permute-start.1 = (bf16[16,128,128]{2,1,0:T(8,128)(2,1)S(1)}, bf16[16,128,128]{2,1,0:T(8,128)(2,1)S(1)}, u32[]{:S(2)}, u32[]{:S(2)}) collective-permute-start(bf16[16,128,128]{2,1,0:T(8,128)(2,1)S(1)} %get-tuple-element.27.near_ref), channel_id=1, source_target_pairs={{0,1},{1,0},{2,3},{3,2},{4,5},{5,4},{6,7},{7,6},{8,9},{9,8},{10,11... | collective-permute-start | bytes 1572872 | tf_op jit(solution)/shard_map/ppermute | solution.py:171
  28.9 10.0 %collective-permute-start.2 = (bf16[16,128,128]{2,1,0:T(8,128)(2,1)S(1)}, bf16[16,128,128]{2,1,0:T(8,128)(2,1)S(1)}, u32[]{:S(2)}, u32[]{:S(2)}) collective-permute-start(bf16[16,128,128]{2,1,0:T(8,128)(2,1)S(1)} %get-tuple-element.26.near_ref), channel_id=1, source_target_pairs={{0,1},{1,0},{2,3},{3,2},{4,5},{5,4},{6,7},{7,6},{8,9},{9,8},{10,11... | collective-permute-start | bytes 1572872 | tf_op jit(solution)/shard_map/ppermute | solution.py:171
  32.8 7.4 %collective-permute-start.4 = (f32[2,512]{1,0:T(2,128)S(1)}, f32[2,512]{1,0:T(2,128)S(1)}, u32[]{:S(2)}, u32[]{:S(2)}) collective-permute-start(f32[2,512]{1,0:T(2,128)S(1)} %get-tuple-element.25.mine_ref), channel_id=1, source_target_pairs={{0,36},{1,37},{2,38},{3,39},{4,32},{5,33},{6,34},{7,35},{32,4},{33... | collective-permute-start | bytes 12296 | tf_op jit(solution)/shard_map/ppermute | solution.py:174
  40.2 8.2 %collective-permute-start.3 = (bf16[256,128]{1,0:T(8,128)(2,1)S(1)}, bf16[256,128]{1,0:T(8,128)(2,1)S(1)}, u32[]{:S(2)}, u32[]{:S(2)}) collective-permute-start(bf16[256,128]{1,0:T(8,128)(2,1)S(1)} %get-tuple-element.24), channel_id=1, source_target_pairs={{0,36},{1,37},{2,38},{3,39},{4,32},{5,33},{6,34},{7,35},{32,4},{33... | collective-permute-start | bytes 196616 | tf_op jit(solution)/shard_map/ppermute | solution.py:174
  41.6 16.5 %all-to-all-start.1 = ((f32[128,1,128]{2,1,0:T(1,128)}), f32[128,1,128]{2,1,0:T(1,128)S(1)}, u32[]{:S(2)}, u32[]{:S(2)}) async-start(f32[128,1,128]{2,1,0:T(1,128)} %bitcast.3), calls=%async_computation.1 | async-start | bytes 131072 | tf_op jit(solution)/shard_map/all_to_all | solution.py:216

commit v6 on v5

v6 whole, which is shorter than its diff:
```python
import math

import jax
import jax.numpy as jnp
from jax import lax
from jax.experimental import pallas as pl
from jax.experimental.pallas import tpu as pltpu
from jax.sharding import Mesh, PartitionSpec as P

HD = 128
HEADS = 8
AXES = {"y": 4, "zh": 2, "x": 4, "zl": 4, "c": 2}
NX = AXES["x"]
NZL = AXES["zl"]
TOK = 256
CHUNK = TOK // HEADS
HALF = TOK // 2
BLOCKS = AXES["y"] * NX
KEYS = BLOCKS * HALF
FLIPS = 4
ROWS = FLIPS * TOK
TILE = 512
SCALE = math.log2(math.e) / math.sqrt(HD)
LONG = 20_000_000_000
MIB = 1024 * 1024
VMEM = pl.BlockSpec(memory_space=pltpu.VMEM)
ANY = pl.BlockSpec(memory_space=pl.ANY)
SMEM = pl.BlockSpec(memory_space=pltpu.SMEM)


def spread_kernel(keys_ref, values_ref, out_ref, piece_ref, in_sems, out_sems):
    c = lax.axis_index("c")
    reads = []
    for n, ref in enumerate((keys_ref, values_ref)):
        for z in range(NZL):
            rows = pl.ds(pl.multiple_of((z * 2 + c) * CHUNK, CHUNK), CHUNK)
            target = piece_ref.at[n, pl.ds(z * CHUNK, CHUNK)]
            reads.append(pltpu.make_async_copy(ref.at[rows], target, in_sems.at[n, z]))
    for copy in reads:
        copy.start()
    for copy in reads:
        copy.wait()
    writes = [pltpu.make_async_copy(piece_ref, out_ref.at[i], out_sems.at[i]) for i in range(BLOCKS)]
    for copy in writes:
        copy.start()
    for copy in writes:
        copy.wait()


def row_positions():
    y, zh, x = (lax.axis_index(a) for a in ("y", "zh", "x"))
    own = (y * 8 + zh * 4 + x) * TOK
    other = (y * 8 + (1 - zh) * 4 + x) * TOK
    row = lax.broadcasted_iota(jnp.int32, (ROWS, HALF), 0)
    return jnp.where(row < 2 * TOK, own, other) + lax.rem(row, TOK)


def limit_kernel(docs_ref, own_ref, q_ref, start_ref):
    q_ref[...] = own_ref[...]
    pos = row_positions()
    start = jnp.zeros_like(pos)
    end = 0
    for i in range(3):
        end = end + docs_ref[i]
        start = jnp.where(pos >= end, end, start)
    start_ref[...] = start


def score_kernel(near_ref, q0, q1, q2, q3, start_ref, probs_ref, stats_ref, raw_ref):
    zh, c = lax.axis_index("zh"), lax.axis_index("c")
    pos, start = row_positions(), start_ref[...]
    lane = lax.broadcasted_iota(jnp.int32, (1, HALF), 1)
    inside = (lane // CHUNK * 2 + c) * CHUNK + lane % CHUNK
    queries = jnp.concatenate([q[...] for q in (q0, q1, q2, q3)], axis=0)
    peak = jnp.full((ROWS, HALF), -1e30, jnp.float32)
    per = TILE // HALF
    for t in range(KEYS // TILE):
        block = near_ref[t * per : (t + 1) * per, 0].reshape(TILE, HD)
        raw = lax.dot_general(queries, block, (((1,), (1,)), ((), ())), preferred_element_type=jnp.float32)
        for j in range(per):
            source = t * per + j
            key_pos = (source // NX * 8 + zh * 4 + source % NX) * TOK + inside
            part = raw[:, j * HALF : (j + 1) * HALF]
            part = jnp.where((key_pos >= start) & (key_pos <= pos), part, -jnp.inf)
            raw_ref[:, source * HALF : (source + 1) * HALF] = part
            peak = jnp.maximum(peak, part)
    row_max = jnp.max(peak, axis=1, keepdims=True)
    total = jnp.zeros((ROWS, HALF), jnp.float32)
    for j in range(0, KEYS, HALF):
        probs = jnp.exp2((raw_ref[:, j : j + HALF] - row_max) * SCALE)
        probs_ref[:, j : j + HALF] = probs.astype(jnp.bfloat16)
        total = total + probs
    row_sum = jnp.sum(total, axis=1, keepdims=True)
    first_lane = lax.broadcasted_iota(jnp.int32, (ROWS, HALF), 1) == 0
    stats_ref[...] = jnp.where(first_lane, row_max, row_sum).T[0:2, :]


def row_kernel(probs_ref, near_ref, keep_ref, send_ref):
    acc = jnp.dot(probs_ref[...], near_ref[:, 1].reshape(KEYS, HD), preferred_element_type=jnp.float32)
    for k in range(2):
        keep_ref[k] = acc[2 * k * TOK : (2 * k + 1) * TOK]
        send_ref[k] = acc[(2 * k + 1) * TOK : (2 * k + 2) * TOK]


def stat(ref, k):
    cut = slice(k * TOK, (k + 1) * TOK)
    return ref[0:1, cut], ref[1:2, cut]


def as_column(row):
    return jnp.broadcast_to(row, (HD, TOK)).T


def pair_kernel(mine_ref, core_ref, send_ref, pair_ref):
    for k in range(FLIPS):
        (m0, l0), (m1, l1) = stat(mine_ref, k), stat(core_ref, k ^ 1)
        top = jnp.maximum(m0, m1)
        cut = slice(k * TOK, (k + 1) * TOK)
        pair_ref[0:1, cut] = top
        pair_ref[1:2, cut] = l0 * jnp.exp2((m0 - top) * SCALE) + l1 * jnp.exp2((m1 - top) * SCALE)


def join_kernel(keep_ref, got_ref, mine_ref, core_ref, keep_out_ref, send_ref):
    for k, ref in ((0, keep_out_ref), (2, send_ref)):
        m0, m1 = stat(mine_ref, k)[0], stat(core_ref, k ^ 1)[0]
        top = jnp.maximum(m0, m1)
        w0, w1 = jnp.exp2((m0 - top) * SCALE), jnp.exp2((m1 - top) * SCALE)
        joined = keep_ref[k // 2] * as_column(w0) + got_ref[k // 2] * as_column(w1)
        ref[...] = joined.astype(ref.dtype)


def column_kernel(probs_ref, mine_ref, pair_ref, plane_ref, send_ref, cols_ref):
    weight = []
    for k in range(FLIPS):
        (m0, l0), (m1, l1) = stat(pair_ref, k), stat(plane_ref, k ^ 2)
        top = jnp.maximum(m0, m1)
        norm = l0 * jnp.exp2((m0 - top) * SCALE) + l1 * jnp.exp2((m1 - top) * SCALE)
        weight.append(jnp.exp2((stat(mine_ref, k)[0] - top) * SCALE) / norm)
    weight = jnp.concatenate(weight, axis=1)
    high = weight.astype(jnp.bfloat16).astype(jnp.float32)
    row = lax.broadcasted_iota(jnp.int32, (8, ROWS), 0)
    both = jnp.where(row == 0, high, jnp.where(row == 1, weight - high, 0.0)).astype(jnp.bfloat16)
    for b in range(0, BLOCKS, 2):
        first = b * HALF
        sums = jnp.dot(both, probs_ref[:, first : first + 2 * HALF], preferred_element_type=jnp.float32)
        line = jnp.sum(sums, axis=0, keepdims=True)
        pair = [jnp.broadcast_to(line[:, i * HALF : (i + 1) * HALF], (NZL, HALF)) for i in range(2)]
        cols_ref[b * NZL : (b + 2) * NZL, :] = jnp.concatenate(pair, axis=0)


def merge_kernel(keep_ref, got_ref, pair_ref, plane_ref, out_ref):
    (m0, l0), (m1, l1) = stat(pair_ref, 0), stat(plane_ref, 2)
    top = jnp.maximum(m0, m1)
    w0, w1 = jnp.exp2((m0 - top) * SCALE), jnp.exp2((m1 - top) * SCALE)
    norm = w0 * l0 + w1 * l1
    out = keep_ref[...] * as_column(w0 / norm) + got_ref[...].astype(jnp.float32) * as_column(w1 / norm)
    out_ref[...] = out.astype(jnp.bfloat16)


def kernel(fn, name, shapes, specs, scratch=(), limit=8, space=VMEM, flops=0):
    return pl.pallas_call(
        fn,
        out_shape=shapes,
        in_specs=specs,
        out_specs=jax.tree.map(lambda _: space, shapes),
        scratch_shapes=scratch,
        compiler_params=pltpu.CompilerParams(vmem_limit_bytes=limit * MIB),
        cost_estimate=pl.CostEstimate(flops=flops, bytes_accessed=0, transcendentals=0) if flops else None,
        name=name,
    )


def body(queries, keys, values, doc_lengths):
    shape = jax.ShapeDtypeStruct
    f32, bf16 = jnp.float32, jnp.bfloat16
    def across(x):
        return lax.ppermute(x, "c", [(0, 1), (1, 0)])

    def partner(x):
        return lax.ppermute(x, ("zh", "zl", "c"), [(i, i ^ 12) for i in range(16)])

    copies = kernel(
        spread_kernel,
        "spread",
        shape((BLOCKS, 2, HALF, HD), bf16),
        [ANY] * 2,
        [
            pltpu.VMEM((2, HALF, HD), bf16),
            pltpu.SemaphoreType.DMA((2, NZL)),
            pltpu.SemaphoreType.DMA((BLOCKS,)),
        ],
        limit=60,
        space=ANY,
    )(keys, values)
    near = lax.all_to_all(copies, ("y", "x"), 0, 0, tiled=True)
    q1, q2 = across(queries), partner(queries)
    q3 = across(q2)
    own, start = kernel(
        limit_kernel, "limits", (shape((TOK, HD), bf16), shape((ROWS, HALF), jnp.int32)), [SMEM, VMEM]
    )(doc_lengths, queries)
    near, q1, q2, q3, own, start = lax.optimization_barrier((near, q1, q2, q3, own, start))
    probs, mine = kernel(
        score_kernel,
        "scores",
        (shape((ROWS, KEYS), bf16), shape((2, ROWS), f32)),
        [VMEM] * 6,
        [pltpu.VMEM((ROWS, KEYS), f32)],
        limit=24,
    )(near, own, q1, q2, q3, start)
    core = across(mine)
    keep, send = kernel(row_kernel, "rows", (shape((2, TOK, HD), f32),) * 2, [VMEM] * 2, flops=LONG)(probs, near)
    pair = kernel(pair_kernel, "pair", shape((2, ROWS), f32), [VMEM] * 2 + [ANY], flops=LONG)(mine, core, send)
    plane = partner(pair)
    keep, send = kernel(
        join_kernel, "join", (shape((TOK, HD), f32), shape((TOK, HD), bf16)), [VMEM] * 4, flops=LONG
    )(keep, across(send), mine, core)
    got = partner(send)
    cols = kernel(
        column_kernel, "columns", shape((BLOCKS * NZL, HALF), f32), [VMEM] * 4 + [ANY], flops=LONG
    )(probs, mine, pair, plane, send)
    parts = lax.all_to_all(cols.reshape(BLOCKS * NZL, 1, HALF), ("y", "x", "zl"), 0, 0, tiled=True)
    rows = kernel(merge_kernel, "merge", shape((TOK, HD), bf16), [VMEM] * 4, flops=LONG)(keep, got, pair, plane)
    parts, _ = lax.optimization_barrier((parts, rows))
    totals = (jnp.sum(parts, axis=(0, 1)) / HEADS).reshape(NZL, CHUNK)
    return rows, lax.dynamic_index_in_dim(totals, lax.axis_index("zl"), 0, keepdims=False)


def solution(mesh):
    fine = Mesh(mesh.devices.reshape(tuple(AXES.values())), tuple(AXES))
    ctx, head = ("y", "zh", "x"), ("zl", "c")
    return jax.shard_map(
        body,
        mesh=fine,
        in_specs=(P(ctx, head), P(ctx, None), P(ctx, None), P()),
        out_specs=(P(ctx, head), P(ctx + head)),
        check_vma=False,
    )
```

time: 59.2 us -> 57.2 us (0.966)
  waiting for transfers between devices: 17.2 us -> 12.4 us
  starting transfers between devices: 29.5 us -> 32 us
    all_to_all x1, waiting for transfers between devices: 7.71 us -> 3.58 us  [body(): near = lax.all_to_all(copies, ('y', 'x'), 0, 0, tiled=True)]
    ppermute x2 -> x4, starting transfers between devices: 2.8 us -> 5.93 us  [across(): return lax.ppermute(x, 'c', [(0, 1), (1, 0)])]
    all_to_all x1, starting transfers between devices: 6.76 us -> 4.74 us  [body(): lax.all_to_all(cols.reshape(BLOCKS * NZL, 1, HALF), ('y', 'x', 'zl'), 0,...]
    ppermute x3, starting transfers between devices: 12.3 us -> 13.7 us  [partner(): return lax.ppermute(x, ('zh', 'zl', 'c'), [(i, i ^ 12) for i in range(16)])]
    all_to_all x1, waiting for transfers between devices: 8.91 us -> 7.86 us  [body(): lax.all_to_all(cols.reshape(BLOCKS * NZL, 1, HALF), ('y', 'x', 'zl'), 0,...]
    ppermute x3, waiting for transfers between devices: 0.01 us -> 0.93 us  [partner(): return lax.ppermute(x, ('zh', 'zl', 'c'), [(i, i ^ 12) for i in range(16)])]
    pallas_call x1, Pallas kernels: 2.34 us -> 3.13 us  [body(): kernel(score_kernel, 'scores', (shape((ROWS, KEYS), bf16), shape((2, ROWS...]
    pallas_call x3 -> x4, Pallas kernels: 3.44 us -> 2.75 us  [the longest x1 1.28 us: body(): kernel(column_kernel, 'columns', shape((BLOCKS * NZL, HALF), f32), [VMEM]...]
  transfers between devices with their start and end apart: 7 -> 9, of which waited for: 3 -> 3; matrix products, arithmetic and copies ran while one was open for 0% -> 0% of each run, Pallas kernels for 12% -> 7%
where the time goes in v6:
time: 57.2 us; the launch traced here: 56.6 us
  starting transfers between devices  32 us (56%)
  waiting for transfers between devices  12.4 us (22%)
  Pallas kernels  9.38 us (16%)
  local copies, waits for them, and re-layouts  2.1 us (4%)
  between operations  0.72 us (1%)
    ppermute x3, starting transfers between devices, partner(): return lax.ppermute(x, ('zh', 'zl', 'c'), [(i, i ^ 12) for i in range(16)])  13.7 us
    all_to_all x1, waiting for transfers between devices, body(): lax.all_to_all(cols.reshape(BLOCKS * NZL, 1, HALF), ('y', 'x', 'zl'), 0,...  7.86 us
    all_to_all x1, starting transfers between devices, body(): near = lax.all_to_all(copies, ('y', 'x'), 0, 0, tiled=True)  7.6 us
    ppermute x4, starting transfers between devices, across(): return lax.ppermute(x, 'c', [(0, 1), (1, 0)])  5.93 us
    all_to_all x1, starting transfers between devices, body(): lax.all_to_all(cols.reshape(BLOCKS * NZL, 1, HALF), ('y', 'x', 'zl'), 0,...  4.74 us
    all_to_all x1, waiting for transfers between devices, body(): near = lax.all_to_all(copies, ('y', 'x'), 0, 0, tiled=True)  3.58 us
    pallas_call x1, Pallas kernels, body(): kernel(score_kernel, 'scores', (shape((ROWS, KEYS), bf16), shape((2, ROWS...  3.13 us
    pallas_call x1, Pallas kernels, body(): kernel(spread_kernel, 'spread', shape((BLOCKS, 2, HALF, HD), bf16), [ANY]...  2.01 us
  transfers between devices with their start and end apart: 9, of which 3 were waited for; matrix products, arithmetic and copies ran while one was open for 0% of the time, Pallas kernels for 7%

profile of v6, /device:TPU:1, one launch (start us, length us, event | category | flops | bytes accessed | tf_op | source)
XLA Modules:
  0.0 56.6 jit_solution(12677432853098234838)
XLA Ops:
  0.6 2.0 %spread.1 = bf16[16,2,128,128]{3,2,1,0:T(8,128)(2,1)} custom-call(bf16[256,128]{1,0:T(8,128)(2,1)} %keys_ref.1, bf16[256,128]{1,0:T(8,128)(2,1)} %values_ref.1), custom_call_target="tpu_custom_call" | custom-call | tf_op jit(solution)/shard_map/spread/pallas_call | solution.py:182
  2.7 7.6 %all-to-all-start = ((bf16[16,2,128,128]{3,2,1,0:T(8,128)(2,1)}), bf16[16,2,128,128]{3,2,1,0:T(8,128)(2,1)S(1)}, u32[]{:S(2)}, u32[]{:S(2)}) async-start(bf16[16,2,128,128]{3,2,1,0:T(8,128)(2,1)} %spread.1), calls=%async_computation | async-start | bytes 2097152 | tf_op jit(solution)/shard_map/all_to_all | solution.py:195
  10.3 6.1 %collective-permute-start.1 = (bf16[256,128]{1,0:T(8,128)(2,1)}, bf16[256,128]{1,0:T(8,128)(2,1)S(1)}, u32[]{:S(2)}, u32[]{:S(2)}) collective-permute-start(bf16[256,128]{1,0:T(8,128)(2,1)} %own_ref.1), channel_id=1, source_target_pairs={{0,36},{1,37},{2,38},{3,39},{4,32},{5,33},{6,34},{7,35},{32,4},{33... | collective-permute-start | bytes 196616 | tf_op jit(solution)/shard_map/ppermute | solution.py:180
  16.4 1.2 %collective-permute-start = (bf16[256,128]{1,0:T(8,128)(2,1)}, bf16[256,128]{1,0:T(8,128)(2,1)S(1)}, u32[]{:S(2)}, u32[]{:S(2)}) collective-permute-start(bf16[256,128]{1,0:T(8,128)(2,1)} %own_ref.1), channel_id=1, source_target_pairs={{0,1},{1,0},{2,3},{3,2},{4,5},{5,4},{6,7},{7,6},{8,9},{9,8},{10,11... | collective-permute-start | bytes 196616 | tf_op jit(solution)/shard_map/ppermute | solution.py:177
  17.6 0.9 %collective-permute-done.1.q2 = bf16[256,128]{1,0:T(8,128)(2,1)S(1)} collective-permute-done((bf16[256,128]{1,0:T(8,128)(2,1)}, bf16[256,128]{1,0:T(8,128)(2,1)S(1)}, u32[]{:S(2)}, u32[]{:S(2)}) %collective-permute-start.1) | collective-permute-done | bytes 65568 | tf_op jit(solution)/shard_map/ppermute | solution.py:180
  18.5 1.9 %collective-permute-start.2 = (bf16[256,128]{1,0:T(8,128)(2,1)S(1)}, bf16[256,128]{1,0:T(8,128)(2,1)S(1)}, u32[]{:S(2)}, u32[]{:S(2)}) collective-permute-start(bf16[256,128]{1,0:T(8,128)(2,1)S(1)} %collective-permute-done.1.q2), channel_id=1, source_target_pairs={{0,1},{1,0},{2,3},{3,2},{4,5},{5,4},{6,7},{7,6},{8,9},{9,8},{10,11... | collective-permute-start | bytes 196616 | tf_op jit(solution)/shard_map/ppermute | solution.py:177
  20.4 0.8 %copy-done = bf16[256,128]{1,0:T(8,128)(2,1)S(1)} copy-done((bf16[256,128]{1,0:T(8,128)(2,1)S(1)}, bf16[256,128]{1,0:T(8,128)(2,1)}, u32[]{:S(2)}) %copy-start) | copy-done | bytes 65560
  21.3 0.7 %copy-done.1 = s32[4]{0:T(128)S(1)} copy-done((s32[4]{0:T(128)S(1)}, s32[4]{0:T(128)}, u32[]{:S(2)}) %copy-start.1) | copy-done | bytes 40
  21.9 0.7 %limits.1 = (bf16[256,128]{1,0:T(8,128)(2,1)S(1)}, s32[1024,128]{1,0:T(8,128)S(1)}) custom-call(s32[4]{0:T(128)S(1)} %copy-done.1, bf16[256,128]{1,0:T(8,128)(2,1)S(1)} %copy-done), custom_call_target="tpu_custom_call" | custom-call | tf_op jit(solution)/shard_map/limits/pallas_call | solution.py:198
  22.7 3.6 %all-to-all-done.near_ref = bf16[16,2,128,128]{3,2,1,0:T(8,128)(2,1)S(1)} async-done(((bf16[16,2,128,128]{3,2,1,0:T(8,128)(2,1)}), bf16[16,2,128,128]{3,2,1,0:T(8,128)(2,1)S(1)}, u32[]{:S(2)}, u32[]{:S(2)}) %all-to-all-start) | async-done | bytes 1048608 | tf_op jit(solution)/shard_map/all_to_all | solution.py:195
  26.2 3.1 %scores.1 = (bf16[1024,2048]{1,0:T(8,128)(2,1)S(1)}, f32[2,1024]{1,0:T(2,128)S(1)}) custom-call(bf16[16,2,128,128]{3,2,1,0:T(8,128)(2,1)S(1)} %all-to-all-done.near_ref, bf16[256,128]{1,0:T(8,128)(2,1)S(1)} %get-tuple-element.20.q0, bf16[256,128]{1,0:T(8,128)(2,1)S(1)} %collective-permute-done.q1, bf16[256,128]{1,0:T(8,128)(2,1)S(1)} %collective-permute-done.1.q2, ...), custom_call_target="tpu_custom_call" | custom-call | tf_op jit(solution)/shard_map/scores/pallas_call | solution.py:202
  29.4 2.7 %collective-permute-start.4 = (f32[2,1024]{1,0:T(2,128)S(1)}, f32[2,1024]{1,0:T(2,128)S(1)}, u32[]{:S(2)}, u32[]{:S(2)}) collective-permute-start(f32[2,1024]{1,0:T(2,128)S(1)} %get-tuple-element.28.mine_ref), channel_id=1, source_target_pairs={{0,1},{1,0},{2,3},{3,2},{4,5},{5,4},{6,7},{7,6},{8,9},{9,8},{10,11... | collective-permute-start | bytes 24584 | tf_op jit(solution)/shard_map/ppermute | solution.py:177
  32.1 1.2 %rows.1 = (f32[2,256,128]{2,1,0:T(8,128)S(1)}, f32[2,256,128]{2,1,0:T(8,128)S(1)}) custom-call(bf16[1024,2048]{1,0:T(8,128)(2,1)S(1)} %get-tuple-element.25.probs_ref, bf16[16,2,128,128]{3,2,1,0:T(8,128)(2,1)S(1)} %all-to-all-done.near_ref), custom_call_target="tpu_custom_call" | custom-call | flops 20000000000 | tf_op jit(solution)/shard_map/rows/pallas_call | solution.py:211
  33.3 0.1 collective-permute-start.3
  33.4 6.1 %collective-permute-start.6 = (f32[2,1024]{1,0:T(2,128)S(1)}, f32[2,1024]{1,0:T(2,128)S(1)}, u32[]{:S(2)}, u32[]{:S(2)}) collective-permute-start(f32[2,1024]{1,0:T(2,128)S(1)} %pair.1.pair_ref), channel_id=1, source_target_pairs={{0,36},{1,37},{2,38},{3,39},{4,32},{5,33},{6,34},{7,35},{32,4},{33... | collective-permute-start | bytes 24584 | tf_op jit(solution)/shard_map/ppermute | solution.py:180
  39.5 0.2 join.1
  39.8 1.5 %collective-permute-start.5 = (bf16[256,128]{1,0:T(8,128)(2,1)S(1)}, bf16[256,128]{1,0:T(8,128)(2,1)S(1)}, u32[]{:S(2)}, u32[]{:S(2)}) collective-permute-start(bf16[256,128]{1,0:T(8,128)(2,1)S(1)} %get-tuple-element.30.send_ref), channel_id=1, source_target_pairs={{0,36},{1,37},{2,38},{3,39},{4,32},{5,33},{6,34},{7,35},{32,4},{33... | collective-permute-start | bytes 196616 | tf_op jit(solution)/shard_map/ppermute | solution.py:180
  41.2 1.3 %columns.1 = f32[64,128]{1,0:T(8,128)} custom-call(bf16[1024,2048]{1,0:T(8,128)(2,1)S(1)} %get-tuple-element.25.probs_ref, f32[2,1024]{1,0:T(2,128)S(1)} %get-tuple-element.28.mine_ref, f32[2,1024]{1,0:T(2,128)S(1)} %pair.1.pair_ref, f32[2,1024]{1,0:T(2,128)S(1)} %collective-permute-done.6.plane_ref, bf16[256,128]{1,0:T(8,128)(2,1)S(1)} %get-tuple-element.30.send_ref), custom_call_target="tpu_custom_call" | custom-call | flops 20000000000 | tf_op jit(solution)/shard_map/columns/pallas_call | solution.py:218
  42.5 4.7 %all-to-all-start.1 = ((f32[64,1,128]{2,1,0:T(1,128)}), f32[64,1,128]{2,1,0:T(1,128)S(1)}, u32[]{:S(2)}, u32[]{:S(2)}) async-start(f32[64,1,128]{2,1,0:T(1,128)} %bitcast.1), calls=%async_computation.1 | async-start | bytes 65536 | tf_op jit(solution)/shard_map/all_to_all | solution.py:221
  47.3 0.8 %merge.1 = bf16[256,128]{1,0:T(8,128)(2,1)} custom-call(f32[256,128]{1,0:T(8,128)S(1)} %get-tuple-element.29.keep_ref, bf16[256,128]{1,0:T(8,128)(2,1)S(1)} %collective-permute-done.5.got_ref, f32[2,1024]{1,0:T(2,128)S(1)} %pair.1.pair_ref, f32[2,1024]{1,0:T(2,128)S(1)} %collective-permute-done.6.plane_ref), custom_call_target="tpu_custom_call" | custom-call | flops 20000000000 | tf_op jit(solution)/shard_map/merge/pallas_call | solution.py:222
  48.1 7.9 %all-to-all-done.1 = f32[64,1,128]{2,1,0:T(1,128)S(1)} async-done(((f32[64,1,128]{2,1,0:T(1,128)}), f32[64,1,128]{2,1,0:T(1,128)S(1)}, u32[]{:S(2)}, u32[]{:S(2)}) %all-to-all-start.1) | async-done | bytes 32800 | tf_op jit(solution)/shard_map/all_to_all | solution.py:221
  55.9 0.1 reduce_sum.9
  56.0 0.1 div.10
  56.1 0.5 dynamic-slice_bitcast_fusion
  (10 shorter events, 0.0 us)
Async XLA Ops:
  2.7 23.6 %all-to-all-start = ((bf16[16,2,128,128]{3,2,1,0:T(8,128)(2,1)}), bf16[16,2,128,128]{3,2,1,0:T(8,128)(2,1)S(1)}, u32[]{:S(2)}, u32[]{:S(2)}) async-start(bf16[16,2,128,128]{3,2,1,0:T(8,128)(2,1)} %spread.1), calls=%async_computation | async-start | bytes 2097152 | tf_op jit(solution)/shard_map/all_to_all | solution.py:195
  10.3 8.3 %collective-permute-start.1 = (bf16[256,128]{1,0:T(8,128)(2,1)}, bf16[256,128]{1,0:T(8,128)(2,1)S(1)}, u32[]{:S(2)}, u32[]{:S(2)}) collective-permute-start(bf16[256,128]{1,0:T(8,128)(2,1)} %own_ref.1), channel_id=1, source_target_pairs={{0,36},{1,37},{2,38},{3,39},{4,32},{5,33},{6,34},{7,35},{32,4},{33... | collective-permute-start | bytes 196616 | tf_op jit(solution)/shard_map/ppermute | solution.py:180
  16.4 6.3 %collective-permute-start = (bf16[256,128]{1,0:T(8,128)(2,1)}, bf16[256,128]{1,0:T(8,128)(2,1)S(1)}, u32[]{:S(2)}, u32[]{:S(2)}) collective-permute-start(bf16[256,128]{1,0:T(8,128)(2,1)} %own_ref.1), channel_id=1, source_target_pairs={{0,1},{1,0},{2,3},{3,2},{4,5},{5,4},{6,7},{7,6},{8,9},{9,8},{10,11... | collective-permute-start | bytes 196616 | tf_op jit(solution)/shard_map/ppermute | solution.py:177
  18.5 4.1 %collective-permute-start.2 = (bf16[256,128]{1,0:T(8,128)(2,1)S(1)}, bf16[256,128]{1,0:T(8,128)(2,1)S(1)}, u32[]{:S(2)}, u32[]{:S(2)}) collective-permute-start(bf16[256,128]{1,0:T(8,128)(2,1)S(1)} %collective-permute-done.1.q2), channel_id=1, source_target_pairs={{0,1},{1,0},{2,3},{3,2},{4,5},{5,4},{6,7},{7,6},{8,9},{9,8},{10,11... | collective-permute-start | bytes 196616 | tf_op jit(solution)/shard_map/ppermute | solution.py:177
  20.4 0.8 %copy-start = (bf16[256,128]{1,0:T(8,128)(2,1)S(1)}, bf16[256,128]{1,0:T(8,128)(2,1)}, u32[]{:S(2)}) copy-start(bf16[256,128]{1,0:T(8,128)(2,1)} %own_ref.1) | copy-start | bytes 196612
  21.3 0.7 %copy-start.1 = (s32[4]{0:T(128)S(1)}, s32[4]{0:T(128)}, u32[]{:S(2)}) copy-start(s32[4]{0:T(128)} %docs_ref.1) | copy-start | bytes 52
  29.4 4.0 %collective-permute-start.4 = (f32[2,1024]{1,0:T(2,128)S(1)}, f32[2,1024]{1,0:T(2,128)S(1)}, u32[]{:S(2)}, u32[]{:S(2)}) collective-permute-start(f32[2,1024]{1,0:T(2,128)S(1)} %get-tuple-element.28.mine_ref), channel_id=1, source_target_pairs={{0,1},{1,0},{2,3},{3,2},{4,5},{5,4},{6,7},{7,6},{8,9},{9,8},{10,11... | collective-permute-start | bytes 24584 | tf_op jit(solution)/shard_map/ppermute | solution.py:177
  33.3 6.2 %collective-permute-start.3 = (f32[2,256,128]{2,1,0:T(8,128)S(1)}, f32[2,256,128]{2,1,0:T(8,128)S(1)}, u32[]{:S(2)}, u32[]{:S(2)}) collective-permute-start(f32[2,256,128]{2,1,0:T(8,128)S(1)} %get-tuple-element.27.send_ref), channel_id=1, source_target_pairs={{0,1},{1,0},{2,3},{3,2},{4,5},{5,4},{6,7},{7,6},{8,9},{9,8},{10,11... | collective-permute-start | bytes 786440 | tf_op jit(solution)/shard_map/ppermute | solution.py:177
  33.4 7.8 %collective-permute-start.6 = (f32[2,1024]{1,0:T(2,128)S(1)}, f32[2,1024]{1,0:T(2,128)S(1)}, u32[]{:S(2)}, u32[]{:S(2)}) collective-permute-start(f32[2,1024]{1,0:T(2,128)S(1)} %pair.1.pair_ref), channel_id=1, source_target_pairs={{0,36},{1,37},{2,38},{3,39},{4,32},{5,33},{6,34},{7,35},{32,4},{33... | collective-permute-start | bytes 24584 | tf_op jit(solution)/shard_map/ppermute | solution.py:180
  39.8 7.5 %collective-permute-start.5 = (bf16[256,128]{1,0:T(8,128)(2,1)S(1)}, bf16[256,128]{1,0:T(8,128)(2,1)S(1)}, u32[]{:S(2)}, u32[]{:S(2)}) collective-permute-start(bf16[256,128]{1,0:T(8,128)(2,1)S(1)} %get-tuple-element.30.send_ref), channel_id=1, source_target_pairs={{0,36},{1,37},{2,38},{3,39},{4,32},{5,33},{6,34},{7,35},{32,4},{33... | collective-permute-start | bytes 196616 | tf_op jit(solution)/shard_map/ppermute | solution.py:180
  42.5 13.4 %all-to-all-start.1 = ((f32[64,1,128]{2,1,0:T(1,128)}), f32[64,1,128]{2,1,0:T(1,128)S(1)}, u32[]{:S(2)}, u32[]{:S(2)}) async-start(f32[64,1,128]{2,1,0:T(1,128)} %bitcast.1), calls=%async_computation.1 | async-start | bytes 65536 | tf_op jit(solution)/shard_map/all_to_all | solution.py:221

commit v7 on v6

--- a/solution.py
+++ b/solution.py
@@ -21,6 +21,8 @@
 ROWS = FLIPS * TOK
 TILE = 512
 SCALE = math.log2(math.e) / math.sqrt(HD)
+OWN, OTHER = 4, 5
+BARRED = 32768.0
 LONG = 20_000_000_000
 MIB = 1024 * 1024
 VMEM = pl.BlockSpec(memory_space=pltpu.VMEM)
@@ -30,12 +32,10 @@
 
 def spread_kernel(keys_ref, values_ref, out_ref, piece_ref, in_sems, out_sems):
     c = lax.axis_index("c")
-    reads = []
-    for n, ref in enumerate((keys_ref, values_ref)):
-        for z in range(NZL):
-            rows = pl.ds(pl.multiple_of((z * 2 + c) * CHUNK, CHUNK), CHUNK)
-            target = piece_ref.at[n, pl.ds(z * CHUNK, CHUNK)]
-            reads.append(pltpu.make_async_copy(ref.at[rows], target, in_sems.at[n, z]))
+    reads = [
+        pltpu.make_async_copy(ref.at[:, c], piece_ref.at[n], in_sems.at[n])
+        for n, ref in enumerate((keys_ref, values_ref))
+    ]
     for copy in reads:
         copy.start()
     for copy in reads:
@@ -47,43 +47,65 @@
         copy.wait()
 
 
-def row_positions():
+def inside_block(index):
+    return (index // CHUNK * 2 + lax.axis_index("c")) * CHUNK + index % CHUNK
+
+
+def limit_kernel(docs_ref, own_ref, q_ref, row_mask_ref, key_mask_ref):
+    q_ref[...] = own_ref[...]
     y, zh, x = (lax.axis_index(a) for a in ("y", "zh", "x"))
-    own = (y * 8 + zh * 4 + x) * TOK
-    other = (y * 8 + (1 - zh) * 4 + x) * TOK
-    row = lax.broadcasted_iota(jnp.int32, (ROWS, HALF), 0)
-    return jnp.where(row < 2 * TOK, own, other) + lax.rem(row, TOK)
-
-
-def limit_kernel(docs_ref, own_ref, q_ref, start_ref):
-    q_ref[...] = own_ref[...]
-    pos = row_positions()
-    start = jnp.zeros_like(pos)
-    end = 0
-    for i in range(3):
-        end = end + docs_ref[i]
-        start = jnp.where(pos >= end, end, start)
-    start_ref[...] = start
-
-
-def score_kernel(near_ref, q0, q1, q2, q3, start_ref, probs_ref, stats_ref, raw_ref):
-    zh, c = lax.axis_index("zh"), lax.axis_index("c")
-    pos, start = row_positions(), start_ref[...]
-    lane = lax.broadcasted_iota(jnp.int32, (1, HALF), 1)
-    inside = (lane // CHUNK * 2 + c) * CHUNK + lane % CHUNK
+    own, other = y * 8 + zh * 4 + x, y * 8 + (1 - zh) * 4 + x
+    ends = [docs_ref[0]]
+    for i in (1, 2):
+        ends.append(ends[-1] + docs_ref[i])
+
+    def document(pos):
+        return sum((pos >= end).astype(jnp.int32) for end in ends)
+
+    row = lax.broadcasted_iota(jnp.int32, (ROWS, HD), 0)
+    lane = lax.broadcasted_iota(jnp.int32, (ROWS, HD), 1)
+    mine = row < 2 * TOK
+    doc = document(jnp.where(mine, own, other) * TOK + row % TOK)
+    hit = (lane == doc) | (lane == jnp.where(mine, OWN, OTHER))
+    row_mask_ref[...] = jnp.where(hit, 1.0, 0.0).astype(jnp.bfloat16)
+
+    key = lax.broadcasted_iota(jnp.int32, (KEYS, HD), 0)
+    lane = lax.broadcasted_iota(jnp.int32, (KEYS, HD), 1)
+    slot = key // HALF
+    block = slot // NX * 8 + zh * 4 + slot % NX
+    doc = document(block * TOK + inside_block(key % HALF))
+    barred = (lane < OWN) & (lane != doc)
+    barred = barred | ((lane == OWN) & (block >= own)) | ((lane == OTHER) & (block > other))
+    key_mask_ref[...] = jnp.where(barred, -BARRED, 0.0).astype(jnp.bfloat16)
+
+
+def score_kernel(near_ref, q0, q1, q2, q3, row_mask_ref, key_mask_ref, probs_ref, stats_ref, raw_ref):
+    across_depth = (((1,), (1,)), ((), ()))
     queries = jnp.concatenate([q[...] for q in (q0, q1, q2, q3)], axis=0)
-    peak = jnp.full((ROWS, HALF), -1e30, jnp.float32)
+    queries = jnp.concatenate([queries, row_mask_ref[...]], axis=1)
+    own = 2 * TOK
+    slot = lax.axis_index("y") * NX + lax.axis_index("x")
+    mask = key_mask_ref[pl.ds(pl.multiple_of(slot * HALF, HALF), HALF), :]
+    feature = lax.broadcasted_iota(jnp.int32, (HALF, HD), 1)
+    mask = jnp.where(feature == OWN, 0.0, mask.astype(jnp.float32)).astype(jnp.bfloat16)
+    block = jnp.concatenate([near_ref[slot, 0], mask], axis=1)
+    diagonal = lax.dot_general(queries[:own], block, across_depth, preferred_element_type=jnp.float32)
+    row = lax.broadcasted_iota(jnp.int32, (own, HALF), 0) % TOK
+    lane = lax.broadcasted_iota(jnp.int32, (own, HALF), 1)
+    diagonal = jnp.where(inside_block(lane) <= row, diagonal, -jnp.inf)
+    peak = jnp.maximum(jnp.full((own, HALF), -1e30, jnp.float32), diagonal)
+    peak = jnp.concatenate([peak, jnp.full((ROWS - own, HALF), -1e30, jnp.float32)], axis=0)
     per = TILE // HALF
     for t in range(KEYS // TILE):
         block = near_ref[t * per : (t + 1) * per, 0].reshape(TILE, HD)
-        raw = lax.dot_general(queries, block, (((1,), (1,)), ((), ())), preferred_element_type=jnp.float32)
+        block = jnp.concatenate([block, key_mask_ref[t * TILE : (t + 1) * TILE, :]], axis=1)
+        raw = lax.dot_general(queries, block, across_depth, preferred_element_type=jnp.float32)
         for j in range(per):
-            source = t * per + j
-            key_pos = (source // NX * 8 + zh * 4 + source % NX) * TOK + inside
             part = raw[:, j * HALF : (j + 1) * HALF]
-            part = jnp.where((key_pos >= start) & (key_pos <= pos), part, -jnp.inf)
-            raw_ref[:, source * HALF : (source + 1) * HALF] = part
+            first = t * TILE + j * HALF
+            raw_ref[:, first : first + HALF] = part
             peak = jnp.maximum(peak, part)
+    raw_ref[0:own, pl.ds(pl.multiple_of(slot * HALF, HALF), HALF)] = diagonal
     row_max = jnp.max(peak, axis=1, keepdims=True)
     total = jnp.zeros((ROWS, HALF), jnp.float32)
     for j in range(0, KEYS, HALF):
@@ -182,31 +204,36 @@
     copies = kernel(
         spread_kernel,
         "spread",
-        shape((BLOCKS, 2, HALF, HD), bf16),
+        shape((BLOCKS, 2, NZL, CHUNK, HD), bf16),
         [ANY] * 2,
         [
-            pltpu.VMEM((2, HALF, HD), bf16),
-            pltpu.SemaphoreType.DMA((2, NZL)),
+            pltpu.VMEM((2, NZL, CHUNK, HD), bf16),
+            pltpu.SemaphoreType.DMA((2,)),
             pltpu.SemaphoreType.DMA((BLOCKS,)),
         ],
         limit=60,
         space=ANY,
-    )(keys, values)
+    )(keys.reshape(NZL, 2, CHUNK, HD), values.reshape(NZL, 2, CHUNK, HD)).reshape(BLOCKS, 2, HALF, HD)
     near = lax.all_to_all(copies, ("y", "x"), 0, 0, tiled=True)
     q1, q2 = across(queries), partner(queries)
     q3 = across(q2)
-    own, start = kernel(
-        limit_kernel, "limits", (shape((TOK, HD), bf16), shape((ROWS, HALF), jnp.int32)), [SMEM, VMEM]
+    own, row_mask, key_mask = kernel(
+        limit_kernel,
+        "limits",
+        (shape((TOK, HD), bf16), shape((ROWS, HD), bf16), shape((KEYS, HD), bf16)),
+        [SMEM, VMEM],
     )(doc_lengths, queries)
-    near, q1, q2, q3, own, start = lax.optimization_barrier((near, q1, q2, q3, own, start))
+    near, q1, q2, q3, own, row_mask, key_mask = lax.optimization_barrier(
+        (near, q1, q2, q3, own, row_mask, key_mask)
+    )
     probs, mine = kernel(
         score_kernel,
         "scores",
         (shape((ROWS, KEYS), bf16), shape((2, ROWS), f32)),
-        [VMEM] * 6,
+        [VMEM] * 7,
         [pltpu.VMEM((ROWS, KEYS), f32)],
         limit=24,
-    )(near, own, q1, q2, q3, start)
+    )(near, own, q1, q2, q3, row_mask, key_mask)
     core = across(mine)
     keep, send = kernel(row_kernel, "rows", (shape((2, TOK, HD), f32),) * 2, [VMEM] * 2, flops=LONG)(probs, near)
     pair = kernel(pair_kernel, "pair", shape((2, ROWS), f32), [VMEM] * 2 + [ANY], flops=LONG)(mine, core, send)

time: 57.2 us -> 56.9 us (level)
  waiting for transfers between devices: 12.4 us -> 11.3 us
  Pallas kernels: 9.38 us -> 10.1 us
    all_to_all x1, waiting for transfers between devices: 3.58 us -> 2.49 us  [body(): near = lax.all_to_all(copies, ('y', 'x'), 0, 0, tiled=True)]
    pallas_call x2, Pallas kernels: 2.71 us -> 3.71 us  [the longest x1 1.92 us: body(): kernel(spread_kernel, 'spread', shape((BLOCKS, 2, NZL, CHUNK, HD), bf16),...]
  transfers between devices with their start and end apart: 9 -> 9, of which waited for: 3 -> 3; matrix products, arithmetic and copies ran while one was open for 0% -> 0% of each run, Pallas kernels for 7% -> 9%
where the time goes in v7:
time: 56.9 us; the launch traced here: 56.3 us
  starting transfers between devices  32 us (56%)
  waiting for transfers between devices  11.3 us (20%)
  Pallas kernels  10.1 us (18%)
  local copies, waits for them, and re-layouts  2.1 us (4%)
  between operations  0.73 us (1%)
    ppermute x3, starting transfers between devices, partner(): return lax.ppermute(x, ('zh', 'zl', 'c'), [(i, i ^ 12) for i in range(16)])  13.7 us
    all_to_all x1, waiting for transfers between devices, body(): lax.all_to_all(cols.reshape(BLOCKS * NZL, 1, HALF), ('y', 'x', 'zl'), 0,...  7.86 us
    all_to_all x1, starting transfers between devices, body(): near = lax.all_to_all(copies, ('y', 'x'), 0, 0, tiled=True)  7.6 us
    ppermute x4, starting transfers between devices, across(): return lax.ppermute(x, 'c', [(0, 1), (1, 0)])  5.93 us
    all_to_all x1, starting transfers between devices, body(): lax.all_to_all(cols.reshape(BLOCKS * NZL, 1, HALF), ('y', 'x', 'zl'), 0,...  4.74 us
    pallas_call x1, Pallas kernels, body(): kernel(score_kernel, 'scores', (shape((ROWS, KEYS), bf16), shape((2, ROWS...  2.89 us
    all_to_all x1, waiting for transfers between devices, body(): near = lax.all_to_all(copies, ('y', 'x'), 0, 0, tiled=True)  2.49 us
    pallas_call x1, Pallas kernels, body(): kernel(spread_kernel, 'spread', shape((BLOCKS, 2, NZL, CHUNK, HD), bf16),...  1.92 us
  transfers between devices with their start and end apart: 9, of which 3 were waited for; matrix products, arithmetic and copies ran while one was open for 0% of the time, Pallas kernels for 9%

profile of v7, /device:TPU:1, one launch (start us, length us, event | category | flops | bytes accessed | tf_op | source)
XLA Modules:
  0.0 56.3 jit_solution(12890268802227183161)
XLA Ops:
  0.6 1.9 %spread.1 = bf16[16,2,4,32,128]{4,3,2,1,0:T(8,128)(2,1)} custom-call(bf16[4,2,32,128]{3,2,1,0:T(8,128)(2,1)} %bitcast.9, bf16[4,2,32,128]{3,2,1,0:T(8,128)(2,1)} %bitcast.10), custom_call_target="tpu_custom_call" | custom-call | tf_op jit(solution)/shard_map/spread/pallas_call | solution.py:204
  2.6 7.6 %all-to-all-start = ((bf16[16,2,128,128]{3,2,1,0:T(8,128)(2,1)}), bf16[16,2,128,128]{3,2,1,0:T(8,128)(2,1)S(1)}, u32[]{:S(2)}, u32[]{:S(2)}) async-start(bf16[16,2,128,128]{3,2,1,0:T(8,128)(2,1)} %bitcast.8), calls=%async_computation | async-start | bytes 2097152 | tf_op jit(solution)/shard_map/all_to_all | solution.py:217
  10.2 6.1 %collective-permute-start.1 = (bf16[256,128]{1,0:T(8,128)(2,1)}, bf16[256,128]{1,0:T(8,128)(2,1)S(1)}, u32[]{:S(2)}, u32[]{:S(2)}) collective-permute-start(bf16[256,128]{1,0:T(8,128)(2,1)} %own_ref.1), channel_id=1, source_target_pairs={{0,36},{1,37},{2,38},{3,39},{4,32},{5,33},{6,34},{7,35},{32,4},{33... | collective-permute-start | bytes 196616 | tf_op jit(solution)/shard_map/ppermute | solution.py:202
  16.3 1.2 %collective-permute-start = (bf16[256,128]{1,0:T(8,128)(2,1)}, bf16[256,128]{1,0:T(8,128)(2,1)S(1)}, u32[]{:S(2)}, u32[]{:S(2)}) collective-permute-start(bf16[256,128]{1,0:T(8,128)(2,1)} %own_ref.1), channel_id=1, source_target_pairs={{0,1},{1,0},{2,3},{3,2},{4,5},{5,4},{6,7},{7,6},{8,9},{9,8},{10,11... | collective-permute-start | bytes 196616 | tf_op jit(solution)/shard_map/ppermute | solution.py:199
  17.5 0.9 %collective-permute-done.1.q2 = bf16[256,128]{1,0:T(8,128)(2,1)S(1)} collective-permute-done((bf16[256,128]{1,0:T(8,128)(2,1)}, bf16[256,128]{1,0:T(8,128)(2,1)S(1)}, u32[]{:S(2)}, u32[]{:S(2)}) %collective-permute-start.1) | collective-permute-done | bytes 65568 | tf_op jit(solution)/shard_map/ppermute | solution.py:202
  18.4 1.9 %collective-permute-start.2 = (bf16[256,128]{1,0:T(8,128)(2,1)S(1)}, bf16[256,128]{1,0:T(8,128)(2,1)S(1)}, u32[]{:S(2)}, u32[]{:S(2)}) collective-permute-start(bf16[256,128]{1,0:T(8,128)(2,1)S(1)} %collective-permute-done.1.q2), channel_id=1, source_target_pairs={{0,1},{1,0},{2,3},{3,2},{4,5},{5,4},{6,7},{7,6},{8,9},{9,8},{10,11... | collective-permute-start | bytes 196616 | tf_op jit(solution)/shard_map/ppermute | solution.py:199
  20.3 0.8 %copy-done = bf16[256,128]{1,0:T(8,128)(2,1)S(1)} copy-done((bf16[256,128]{1,0:T(8,128)(2,1)S(1)}, bf16[256,128]{1,0:T(8,128)(2,1)}, u32[]{:S(2)}) %copy-start) | copy-done | bytes 65560
  21.2 0.7 %copy-done.1 = s32[4]{0:T(128)S(1)} copy-done((s32[4]{0:T(128)S(1)}, s32[4]{0:T(128)}, u32[]{:S(2)}) %copy-start.1) | copy-done | bytes 40
  21.8 1.8 %limits.1 = (bf16[256,128]{1,0:T(8,128)(2,1)S(1)}, bf16[1024,128]{1,0:T(8,128)(2,1)S(1)}, bf16[2048,128]{1,0:T(8,128)(2,1)S(1)}) custom-call(s32[4]{0:T(128)S(1)} %copy-done.1, bf16[256,128]{1,0:T(8,128)(2,1)S(1)} %copy-done), custom_call_target="tpu_custom_call" | custom-call | tf_op jit(solution)/shard_map/limits/pallas_call | solution.py:220
  23.7 2.5 %all-to-all-done.near_ref = bf16[16,2,128,128]{3,2,1,0:T(8,128)(2,1)S(1)} async-done(((bf16[16,2,128,128]{3,2,1,0:T(8,128)(2,1)}), bf16[16,2,128,128]{3,2,1,0:T(8,128)(2,1)S(1)}, u32[]{:S(2)}, u32[]{:S(2)}) %all-to-all-start) | async-done | bytes 1048608 | tf_op jit(solution)/shard_map/all_to_all | solution.py:217
  26.1 2.9 %scores.1 = (bf16[1024,2048]{1,0:T(8,128)(2,1)S(1)}, f32[2,1024]{1,0:T(2,128)S(1)}) custom-call(bf16[16,2,128,128]{3,2,1,0:T(8,128)(2,1)S(1)} %all-to-all-done.near_ref, bf16[256,128]{1,0:T(8,128)(2,1)S(1)} %get-tuple-element.23.q0, bf16[256,128]{1,0:T(8,128)(2,1)S(1)} %collective-permute-done.q1, bf16[256,128]{1,0:T(8,128)(2,1)S(1)} %collective-permute-done.1.q2, ...), custom_call_target="tpu_custom_call" | custom-call | tf_op jit(solution)/shard_map/scores/pallas_call | solution.py:229
  29.0 2.7 %collective-permute-start.4 = (f32[2,1024]{1,0:T(2,128)S(1)}, f32[2,1024]{1,0:T(2,128)S(1)}, u32[]{:S(2)}, u32[]{:S(2)}) collective-permute-start(f32[2,1024]{1,0:T(2,128)S(1)} %get-tuple-element.32.mine_ref), channel_id=1, source_target_pairs={{0,1},{1,0},{2,3},{3,2},{4,5},{5,4},{6,7},{7,6},{8,9},{9,8},{10,11... | collective-permute-start | bytes 24584 | tf_op jit(solution)/shard_map/ppermute | solution.py:199
  31.7 1.2 %rows.1 = (f32[2,256,128]{2,1,0:T(8,128)S(1)}, f32[2,256,128]{2,1,0:T(8,128)S(1)}) custom-call(bf16[1024,2048]{1,0:T(8,128)(2,1)S(1)} %get-tuple-element.29.probs_ref, bf16[16,2,128,128]{3,2,1,0:T(8,128)(2,1)S(1)} %all-to-all-done.near_ref), custom_call_target="tpu_custom_call" | custom-call | flops 20000000000 | tf_op jit(solution)/shard_map/rows/pallas_call | solution.py:238
  33.0 0.1 collective-permute-start.3
  33.1 6.1 %collective-permute-start.6 = (f32[2,1024]{1,0:T(2,128)S(1)}, f32[2,1024]{1,0:T(2,128)S(1)}, u32[]{:S(2)}, u32[]{:S(2)}) collective-permute-start(f32[2,1024]{1,0:T(2,128)S(1)} %pair.1.pair_ref), channel_id=1, source_target_pairs={{0,36},{1,37},{2,38},{3,39},{4,32},{5,33},{6,34},{7,35},{32,4},{33... | collective-permute-start | bytes 24584 | tf_op jit(solution)/shard_map/ppermute | solution.py:202
  39.2 0.2 join.1
  39.4 1.5 %collective-permute-start.5 = (bf16[256,128]{1,0:T(8,128)(2,1)S(1)}, bf16[256,128]{1,0:T(8,128)(2,1)S(1)}, u32[]{:S(2)}, u32[]{:S(2)}) collective-permute-start(bf16[256,128]{1,0:T(8,128)(2,1)S(1)} %get-tuple-element.34.send_ref), channel_id=1, source_target_pairs={{0,36},{1,37},{2,38},{3,39},{4,32},{5,33},{6,34},{7,35},{32,4},{33... | collective-permute-start | bytes 196616 | tf_op jit(solution)/shard_map/ppermute | solution.py:202
  40.9 1.3 %columns.1 = f32[64,128]{1,0:T(8,128)} custom-call(bf16[1024,2048]{1,0:T(8,128)(2,1)S(1)} %get-tuple-element.29.probs_ref, f32[2,1024]{1,0:T(2,128)S(1)} %get-tuple-element.32.mine_ref, f32[2,1024]{1,0:T(2,128)S(1)} %pair.1.pair_ref, f32[2,1024]{1,0:T(2,128)S(1)} %collective-permute-done.6.plane_ref, bf16[256,128]{1,0:T(8,128)(2,1)S(1)} %get-tuple-element.34.send_ref), custom_call_target="tpu_custom_call" | custom-call | flops 20000000000 | tf_op jit(solution)/shard_map/columns/pallas_call | solution.py:245
  42.2 4.7 %all-to-all-start.1 = ((f32[64,1,128]{2,1,0:T(1,128)}), f32[64,1,128]{2,1,0:T(1,128)S(1)}, u32[]{:S(2)}, u32[]{:S(2)}) async-start(f32[64,1,128]{2,1,0:T(1,128)} %bitcast.4), calls=%async_computation.1 | async-start | bytes 65536 | tf_op jit(solution)/shard_map/all_to_all | solution.py:248
  47.0 0.8 %merge.1 = bf16[256,128]{1,0:T(8,128)(2,1)} custom-call(f32[256,128]{1,0:T(8,128)S(1)} %get-tuple-element.33.keep_ref, bf16[256,128]{1,0:T(8,128)(2,1)S(1)} %collective-permute-done.5.got_ref, f32[2,1024]{1,0:T(2,128)S(1)} %pair.1.pair_ref, f32[2,1024]{1,0:T(2,128)S(1)} %collective-permute-done.6.plane_ref), custom_call_target="tpu_custom_call" | custom-call | flops 20000000000 | tf_op jit(solution)/shard_map/merge/pallas_call | solution.py:249
  47.7 7.9 %all-to-all-done.1 = f32[64,1,128]{2,1,0:T(1,128)S(1)} async-done(((f32[64,1,128]{2,1,0:T(1,128)}), f32[64,1,128]{2,1,0:T(1,128)S(1)}, u32[]{:S(2)}, u32[]{:S(2)}) %all-to-all-start.1) | async-done | bytes 32800 | tf_op jit(solution)/shard_map/all_to_all | solution.py:248
  55.6 0.1 reduce_sum.9
  55.7 0.1 div.10
  55.8 0.5 dynamic-slice_bitcast_fusion
  (10 shorter events, 0.0 us)
Async XLA Ops:
  2.6 23.6 %all-to-all-start = ((bf16[16,2,128,128]{3,2,1,0:T(8,128)(2,1)}), bf16[16,2,128,128]{3,2,1,0:T(8,128)(2,1)S(1)}, u32[]{:S(2)}, u32[]{:S(2)}) async-start(bf16[16,2,128,128]{3,2,1,0:T(8,128)(2,1)} %bitcast.8), calls=%async_computation | async-start | bytes 2097152 | tf_op jit(solution)/shard_map/all_to_all | solution.py:217
  10.2 8.3 %collective-permute-start.1 = (bf16[256,128]{1,0:T(8,128)(2,1)}, bf16[256,128]{1,0:T(8,128)(2,1)S(1)}, u32[]{:S(2)}, u32[]{:S(2)}) collective-permute-start(bf16[256,128]{1,0:T(8,128)(2,1)} %own_ref.1), channel_id=1, source_target_pairs={{0,36},{1,37},{2,38},{3,39},{4,32},{5,33},{6,34},{7,35},{32,4},{33... | collective-permute-start | bytes 196616 | tf_op jit(solution)/shard_map/ppermute | solution.py:202
  16.3 7.4 %collective-permute-start = (bf16[256,128]{1,0:T(8,128)(2,1)}, bf16[256,128]{1,0:T(8,128)(2,1)S(1)}, u32[]{:S(2)}, u32[]{:S(2)}) collective-permute-start(bf16[256,128]{1,0:T(8,128)(2,1)} %own_ref.1), channel_id=1, source_target_pairs={{0,1},{1,0},{2,3},{3,2},{4,5},{5,4},{6,7},{7,6},{8,9},{9,8},{10,11... | collective-permute-start | bytes 196616 | tf_op jit(solution)/shard_map/ppermute | solution.py:199
  18.4 5.2 %collective-permute-start.2 = (bf16[256,128]{1,0:T(8,128)(2,1)S(1)}, bf16[256,128]{1,0:T(8,128)(2,1)S(1)}, u32[]{:S(2)}, u32[]{:S(2)}) collective-permute-start(bf16[256,128]{1,0:T(8,128)(2,1)S(1)} %collective-permute-done.1.q2), channel_id=1, source_target_pairs={{0,1},{1,0},{2,3},{3,2},{4,5},{5,4},{6,7},{7,6},{8,9},{9,8},{10,11... | collective-permute-start | bytes 196616 | tf_op jit(solution)/shard_map/ppermute | solution.py:199
  20.3 0.8 %copy-start = (bf16[256,128]{1,0:T(8,128)(2,1)S(1)}, bf16[256,128]{1,0:T(8,128)(2,1)}, u32[]{:S(2)}) copy-start(bf16[256,128]{1,0:T(8,128)(2,1)} %own_ref.1) | copy-start | bytes 196612
  21.2 0.7 %copy-start.1 = (s32[4]{0:T(128)S(1)}, s32[4]{0:T(128)}, u32[]{:S(2)}) copy-start(s32[4]{0:T(128)} %docs_ref.1) | copy-start | bytes 52
  29.0 4.0 %collective-permute-start.4 = (f32[2,1024]{1,0:T(2,128)S(1)}, f32[2,1024]{1,0:T(2,128)S(1)}, u32[]{:S(2)}, u32[]{:S(2)}) collective-permute-start(f32[2,1024]{1,0:T(2,128)S(1)} %get-tuple-element.32.mine_ref), channel_id=1, source_target_pairs={{0,1},{1,0},{2,3},{3,2},{4,5},{5,4},{6,7},{7,6},{8,9},{9,8},{10,11... | collective-permute-start | bytes 24584 | tf_op jit(solution)/shard_map/ppermute | solution.py:199
  33.0 6.2 %collective-permute-start.3 = (f32[2,256,128]{2,1,0:T(8,128)S(1)}, f32[2,256,128]{2,1,0:T(8,128)S(1)}, u32[]{:S(2)}, u32[]{:S(2)}) collective-permute-start(f32[2,256,128]{2,1,0:T(8,128)S(1)} %get-tuple-element.31.send_ref), channel_id=1, source_target_pairs={{0,1},{1,0},{2,3},{3,2},{4,5},{5,4},{6,7},{7,6},{8,9},{9,8},{10,11... | collective-permute-start | bytes 786440 | tf_op jit(solution)/shard_map/ppermute | solution.py:199
  33.1 7.8 %collective-permute-start.6 = (f32[2,1024]{1,0:T(2,128)S(1)}, f32[2,1024]{1,0:T(2,128)S(1)}, u32[]{:S(2)}, u32[]{:S(2)}) collective-permute-start(f32[2,1024]{1,0:T(2,128)S(1)} %pair.1.pair_ref), channel_id=1, source_target_pairs={{0,36},{1,37},{2,38},{3,39},{4,32},{5,33},{6,34},{7,35},{32,4},{33... | collective-permute-start | bytes 24584 | tf_op jit(solution)/shard_map/ppermute | solution.py:202
  39.4 7.5 %collective-permute-start.5 = (bf16[256,128]{1,0:T(8,128)(2,1)S(1)}, bf16[256,128]{1,0:T(8,128)(2,1)S(1)}, u32[]{:S(2)}, u32[]{:S(2)}) collective-permute-start(bf16[256,128]{1,0:T(8,128)(2,1)S(1)} %get-tuple-element.34.send_ref), channel_id=1, source_target_pairs={{0,36},{1,37},{2,38},{3,39},{4,32},{5,33},{6,34},{7,35},{32,4},{33... | collective-permute-start | bytes 196616 | tf_op jit(solution)/shard_map/ppermute | solution.py:202
  42.2 13.4 %all-to-all-start.1 = ((f32[64,1,128]{2,1,0:T(1,128)}), f32[64,1,128]{2,1,0:T(1,128)S(1)}, u32[]{:S(2)}, u32[]{:S(2)}) async-start(f32[64,1,128]{2,1,0:T(1,128)} %bitcast.4), calls=%async_computation.1 | async-start | bytes 65536 | tf_op jit(solution)/shard_map/all_to_all | solution.py:248

commit v8 on v7

--- a/solution.py
+++ b/solution.py
@@ -1,3 +1,4 @@
+import functools
 import math
 
 import jax
@@ -117,11 +118,11 @@
     stats_ref[...] = jnp.where(first_lane, row_max, row_sum).T[0:2, :]
 
 
-def row_kernel(probs_ref, near_ref, keep_ref, send_ref):
-    acc = jnp.dot(probs_ref[...], near_ref[:, 1].reshape(KEYS, HD), preferred_element_type=jnp.float32)
+def row_kernel(first, probs_ref, near_ref, after_ref, out_ref):
+    values = near_ref[:, 1].reshape(KEYS, HD)
     for k in range(2):
-        keep_ref[k] = acc[2 * k * TOK : (2 * k + 1) * TOK]
-        send_ref[k] = acc[(2 * k + 1) * TOK : (2 * k + 2) * TOK]
+        rows = slice((2 * k + first) * TOK, (2 * k + first + 1) * TOK)
+        out_ref[k] = jnp.dot(probs_ref[rows, :], values, preferred_element_type=jnp.float32)
 
 
 def stat(ref, k):
@@ -235,12 +236,19 @@
         limit=24,
     )(near, own, q1, q2, q3, row_mask, key_mask)
     core = across(mine)
-    keep, send = kernel(row_kernel, "rows", (shape((2, TOK, HD), f32),) * 2, [VMEM] * 2, flops=LONG)(probs, near)
+    half = shape((2, TOK, HD), f32)
+    send = kernel(functools.partial(row_kernel, 1), "rows_out", half, [VMEM] * 2 + [ANY], flops=LONG)(
+        probs, near, mine
+    )
     pair = kernel(pair_kernel, "pair", shape((2, ROWS), f32), [VMEM] * 2 + [ANY], flops=LONG)(mine, core, send)
     plane = partner(pair)
+    joined = across(send)
+    keep = kernel(functools.partial(row_kernel, 0), "rows_kept", half, [VMEM] * 2 + [ANY], flops=LONG)(
+        probs, near, joined
+    )
     keep, send = kernel(
         join_kernel, "join", (shape((TOK, HD), f32), shape((TOK, HD), bf16)), [VMEM] * 4, flops=LONG
-    )(keep, across(send), mine, core)
+    )(keep, joined, mine, core)
     got = partner(send)
     cols = kernel(
         column_kernel, "columns", shape((BLOCKS * NZL, HALF), f32), [VMEM] * 4 + [ANY], flops=LONG
@@ -248,8 +256,8 @@
     parts = lax.all_to_all(cols.reshape(BLOCKS * NZL, 1, HALF), ("y", "x", "zl"), 0, 0, tiled=True)
     rows = kernel(merge_kernel, "merge", shape((TOK, HD), bf16), [VMEM] * 4, flops=LONG)(keep, got, pair, plane)
     parts, _ = lax.optimization_barrier((parts, rows))
-    totals = (jnp.sum(parts, axis=(0, 1)) / HEADS).reshape(NZL, CHUNK)
-    return rows, lax.dynamic_index_in_dim(totals, lax.axis_index("zl"), 0, keepdims=False)
+    piece = lax.dynamic_slice_in_dim(parts.reshape(BLOCKS * NZL, HALF), lax.axis_index("zl") * CHUNK, CHUNK, axis=1)
+    return rows, jnp.sum(piece, axis=0) / HEADS
 
 
 def solution(mesh):

time: 56.9 us -> 56.7 us (level)
  local copies, waits for them, and re-layouts: 2.1 us -> 1.49 us
  other arithmetic: 0.09 us -> 0.67 us
    pallas_call x1 -> x2, Pallas kernels: 1.24 us -> 1.39 us  [the longest x1 0.69 us: body(): kernel(functools.partial(row_kernel, 0), 'rows_kept', half, [VMEM] * 2 +...]
  transfers between devices with their start and end apart: 9 -> 9, of which waited for: 3 -> 3; matrix products, arithmetic and copies ran while one was open for 0% -> 0% of each run, Pallas kernels for 9% -> 10%
where the time goes in v8:
time: 56.7 us; the launch traced here: 56.4 us
  starting transfers between devices  31.9 us (56%)
  waiting for transfers between devices  11.3 us (20%)
  Pallas kernels  10.3 us (18%)
  local copies, waits for them, and re-layouts  1.49 us (3%)
  between operations  0.72 us (1%)
  other arithmetic  0.67 us (1%)
    ppermute x3, starting transfers between devices, partner(): return lax.ppermute(x, ('zh', 'zl', 'c'), [(i, i ^ 12) for i in range(16)])  13.7 us
    all_to_all x1, waiting for transfers between devices, body(): lax.all_to_all(cols.reshape(BLOCKS * NZL, 1, HALF), ('y', 'x', 'zl'), 0,...  7.86 us
    all_to_all x1, starting transfers between devices, body(): near = lax.all_to_all(copies, ('y', 'x'), 0, 0, tiled=True)  7.6 us
    ppermute x4, starting transfers between devices, across(): return lax.ppermute(x, 'c', [(0, 1), (1, 0)])  5.93 us
    all_to_all x1, starting transfers between devices, body(): lax.all_to_all(cols.reshape(BLOCKS * NZL, 1, HALF), ('y', 'x', 'zl'), 0,...  4.74 us
    pallas_call x1, Pallas kernels, body(): kernel(score_kernel, 'scores', (shape((ROWS, KEYS), bf16), shape((2, ROWS...  2.89 us
    all_to_all x1, waiting for transfers between devices, body(): near = lax.all_to_all(copies, ('y', 'x'), 0, 0, tiled=True)  2.49 us
    pallas_call x1, Pallas kernels, body(): kernel(spread_kernel, 'spread', shape((BLOCKS, 2, NZL, CHUNK, HD), bf16),...  1.91 us
  transfers between devices with their start and end apart: 9, of which 3 were waited for; matrix products, arithmetic and copies ran while one was open for 0% of the time, Pallas kernels for 10%

profile of v8, /device:TPU:1, one launch (start us, length us, event | category | flops | bytes accessed | tf_op | source)
XLA Modules:
  0.0 56.4 jit_solution(16812169756902941469)
XLA Ops:
  0.6 1.9 %spread.1 = bf16[16,2,4,32,128]{4,3,2,1,0:T(8,128)(2,1)} custom-call(bf16[4,2,32,128]{3,2,1,0:T(8,128)(2,1)} %bitcast.7, bf16[4,2,32,128]{3,2,1,0:T(8,128)(2,1)} %bitcast.8), custom_call_target="tpu_custom_call" | custom-call | tf_op jit(solution)/shard_map/spread/pallas_call | solution.py:205
  2.5 7.6 %all-to-all-start = ((bf16[16,2,128,128]{3,2,1,0:T(8,128)(2,1)}), bf16[16,2,128,128]{3,2,1,0:T(8,128)(2,1)S(1)}, u32[]{:S(2)}, u32[]{:S(2)}) async-start(bf16[16,2,128,128]{3,2,1,0:T(8,128)(2,1)} %bitcast.6), calls=%async_computation | async-start | bytes 2097152 | tf_op jit(solution)/shard_map/all_to_all | solution.py:218
  10.2 6.1 %collective-permute-start.1 = (bf16[256,128]{1,0:T(8,128)(2,1)}, bf16[256,128]{1,0:T(8,128)(2,1)S(1)}, u32[]{:S(2)}, u32[]{:S(2)}) collective-permute-start(bf16[256,128]{1,0:T(8,128)(2,1)} %own_ref.1), channel_id=1, source_target_pairs={{0,36},{1,37},{2,38},{3,39},{4,32},{5,33},{6,34},{7,35},{32,4},{33... | collective-permute-start | bytes 196616 | tf_op jit(solution)/shard_map/ppermute | solution.py:203
  16.3 1.2 %collective-permute-start = (bf16[256,128]{1,0:T(8,128)(2,1)}, bf16[256,128]{1,0:T(8,128)(2,1)S(1)}, u32[]{:S(2)}, u32[]{:S(2)}) collective-permute-start(bf16[256,128]{1,0:T(8,128)(2,1)} %own_ref.1), channel_id=1, source_target_pairs={{0,1},{1,0},{2,3},{3,2},{4,5},{5,4},{6,7},{7,6},{8,9},{9,8},{10,11... | collective-permute-start | bytes 196616 | tf_op jit(solution)/shard_map/ppermute | solution.py:200
  17.5 0.9 %collective-permute-done.1.q2 = bf16[256,128]{1,0:T(8,128)(2,1)S(1)} collective-permute-done((bf16[256,128]{1,0:T(8,128)(2,1)}, bf16[256,128]{1,0:T(8,128)(2,1)S(1)}, u32[]{:S(2)}, u32[]{:S(2)}) %collective-permute-start.1) | collective-permute-done | bytes 65568 | tf_op jit(solution)/shard_map/ppermute | solution.py:203
  18.4 1.9 %collective-permute-start.2 = (bf16[256,128]{1,0:T(8,128)(2,1)S(1)}, bf16[256,128]{1,0:T(8,128)(2,1)S(1)}, u32[]{:S(2)}, u32[]{:S(2)}) collective-permute-start(bf16[256,128]{1,0:T(8,128)(2,1)S(1)} %collective-permute-done.1.q2), channel_id=1, source_target_pairs={{0,1},{1,0},{2,3},{3,2},{4,5},{5,4},{6,7},{7,6},{8,9},{9,8},{10,11... | collective-permute-start | bytes 196616 | tf_op jit(solution)/shard_map/ppermute | solution.py:200
  20.3 0.8 %copy-done = bf16[256,128]{1,0:T(8,128)(2,1)S(1)} copy-done((bf16[256,128]{1,0:T(8,128)(2,1)S(1)}, bf16[256,128]{1,0:T(8,128)(2,1)}, u32[]{:S(2)}) %copy-start) | copy-done | bytes 65560
  21.2 0.7 %copy-done.1 = s32[4]{0:T(128)S(1)} copy-done((s32[4]{0:T(128)S(1)}, s32[4]{0:T(128)}, u32[]{:S(2)}) %copy-start.1) | copy-done | bytes 40
  21.8 1.8 %limits.1 = (bf16[256,128]{1,0:T(8,128)(2,1)S(1)}, bf16[1024,128]{1,0:T(8,128)(2,1)S(1)}, bf16[2048,128]{1,0:T(8,128)(2,1)S(1)}) custom-call(s32[4]{0:T(128)S(1)} %copy-done.1, bf16[256,128]{1,0:T(8,128)(2,1)S(1)} %copy-done), custom_call_target="tpu_custom_call" | custom-call | tf_op jit(solution)/shard_map/limits/pallas_call | solution.py:221
  23.7 2.5 %all-to-all-done.near_ref = bf16[16,2,128,128]{3,2,1,0:T(8,128)(2,1)S(1)} async-done(((bf16[16,2,128,128]{3,2,1,0:T(8,128)(2,1)}), bf16[16,2,128,128]{3,2,1,0:T(8,128)(2,1)S(1)}, u32[]{:S(2)}, u32[]{:S(2)}) %all-to-all-start) | async-done | bytes 1048608 | tf_op jit(solution)/shard_map/all_to_all | solution.py:218
  26.1 2.9 %scores.1 = (bf16[1024,2048]{1,0:T(8,128)(2,1)S(1)}, f32[2,1024]{1,0:T(2,128)S(1)}) custom-call(bf16[16,2,128,128]{3,2,1,0:T(8,128)(2,1)S(1)} %all-to-all-done.near_ref, bf16[256,128]{1,0:T(8,128)(2,1)S(1)} %get-tuple-element.21.q0, bf16[256,128]{1,0:T(8,128)(2,1)S(1)} %collective-permute-done.q1, bf16[256,128]{1,0:T(8,128)(2,1)S(1)} %collective-permute-done.1.q2, ...), custom_call_target="tpu_custom_call" | custom-call | tf_op jit(solution)/shard_map/scores/pallas_call | solution.py:230
  29.0 2.7 %collective-permute-start.4 = (f32[2,1024]{1,0:T(2,128)S(1)}, f32[2,1024]{1,0:T(2,128)S(1)}, u32[]{:S(2)}, u32[]{:S(2)}) collective-permute-start(f32[2,1024]{1,0:T(2,128)S(1)} %get-tuple-element.28.after_ref.mine_ref), channel_id=1, source_target_pairs={{0,1},{1,0},{2,3},{3,2},{4,5},{5,4},{6,7},{7,6},{8,9},{9,8},{10,11... | collective-permute-start | bytes 24584 | tf_op jit(solution)/shard_map/ppermute | solution.py:200
  31.7 0.7 %rows_out.1.send_ref = f32[2,256,128]{2,1,0:T(8,128)S(1)} custom-call(bf16[1024,2048]{1,0:T(8,128)(2,1)S(1)} %get-tuple-element.27.probs_ref, bf16[16,2,128,128]{3,2,1,0:T(8,128)(2,1)S(1)} %all-to-all-done.near_ref, f32[2,1024]{1,0:T(2,128)S(1)} %get-tuple-element.28.after_ref.mine_ref), custom_call_target="tpu_custom_call" | custom-call | flops 20000000000 | tf_op jit(solution)/shard_map/rows_out/pallas_call | solution.py:240
  32.4 0.1 collective-permute-start.3
  32.6 6.1 %collective-permute-start.6 = (f32[2,1024]{1,0:T(2,128)S(1)}, f32[2,1024]{1,0:T(2,128)S(1)}, u32[]{:S(2)}, u32[]{:S(2)}) collective-permute-start(f32[2,1024]{1,0:T(2,128)S(1)} %pair.1.pair_ref), channel_id=1, source_target_pairs={{0,36},{1,37},{2,38},{3,39},{4,32},{5,33},{6,34},{7,35},{32,4},{33... | collective-permute-start | bytes 24584 | tf_op jit(solution)/shard_map/ppermute | solution.py:203
  38.7 0.7 %rows_kept.1.keep_ref = f32[2,256,128]{2,1,0:T(8,128)S(1)} custom-call(bf16[1024,2048]{1,0:T(8,128)(2,1)S(1)} %get-tuple-element.27.probs_ref, bf16[16,2,128,128]{3,2,1,0:T(8,128)(2,1)S(1)} %all-to-all-done.near_ref, f32[2,256,128]{2,1,0:T(8,128)S(1)} %collective-permute-done.3.after_ref.got_ref), custom_call_target="tpu_custom_call" | custom-call | flops 20000000000 | tf_op jit(solution)/shard_map/rows_kept/pallas_call | solution.py:246
  39.4 0.2 join.1
  39.6 1.5 %collective-permute-start.5 = (bf16[256,128]{1,0:T(8,128)(2,1)S(1)}, bf16[256,128]{1,0:T(8,128)(2,1)S(1)}, u32[]{:S(2)}, u32[]{:S(2)}) collective-permute-start(bf16[256,128]{1,0:T(8,128)(2,1)S(1)} %get-tuple-element.30.send_ref), channel_id=1, source_target_pairs={{0,36},{1,37},{2,38},{3,39},{4,32},{5,33},{6,34},{7,35},{32,4},{33... | collective-permute-start | bytes 196616 | tf_op jit(solution)/shard_map/ppermute | solution.py:203
  41.1 1.3 %columns.1 = f32[64,128]{1,0:T(8,128)} custom-call(bf16[1024,2048]{1,0:T(8,128)(2,1)S(1)} %get-tuple-element.27.probs_ref, f32[2,1024]{1,0:T(2,128)S(1)} %get-tuple-element.28.after_ref.mine_ref, f32[2,1024]{1,0:T(2,128)S(1)} %pair.1.pair_ref, f32[2,1024]{1,0:T(2,128)S(1)} %collective-permute-done.6.plane_ref, bf16[256,128]{1,0:T(8,128)(2,1)S(1)} %get-tuple-element.30.send_ref), custom_call_target="tpu_custom_call" | custom-call | flops 20000000000 | tf_op jit(solution)/shard_map/columns/pallas_call | solution.py:253
  42.3 4.7 %all-to-all-start.1 = ((f32[64,1,128]{2,1,0:T(1,128)}), f32[64,1,128]{2,1,0:T(1,128)S(1)}, u32[]{:S(2)}, u32[]{:S(2)}) async-start(f32[64,1,128]{2,1,0:T(1,128)} %bitcast.4), calls=%async_computation.1 | async-start | bytes 65536 | tf_op jit(solution)/shard_map/all_to_all | solution.py:256
  47.1 0.8 %merge.1 = bf16[256,128]{1,0:T(8,128)(2,1)} custom-call(f32[256,128]{1,0:T(8,128)S(1)} %get-tuple-element.29.keep_ref, bf16[256,128]{1,0:T(8,128)(2,1)S(1)} %collective-permute-done.5.got_ref, f32[2,1024]{1,0:T(2,128)S(1)} %pair.1.pair_ref, f32[2,1024]{1,0:T(2,128)S(1)} %collective-permute-done.6.plane_ref), custom_call_target="tpu_custom_call" | custom-call | flops 20000000000 | tf_op jit(solution)/shard_map/merge/pallas_call | solution.py:257
  47.9 7.9 %all-to-all-done.1 = f32[64,1,128]{2,1,0:T(1,128)S(1)} async-done(((f32[64,1,128]{2,1,0:T(1,128)}), f32[64,1,128]{2,1,0:T(1,128)S(1)}, u32[]{:S(2)}, u32[]{:S(2)}) %all-to-all-start.1) | async-done | bytes 32800 | tf_op jit(solution)/shard_map/all_to_all | solution.py:256
  55.7 0.2 dynamic-slice_reduce_fusion
  55.9 0.5 broadcast_multiply_fusion
  (9 shorter events, 0.1 us)
Async XLA Ops:
  2.5 23.6 %all-to-all-start = ((bf16[16,2,128,128]{3,2,1,0:T(8,128)(2,1)}), bf16[16,2,128,128]{3,2,1,0:T(8,128)(2,1)S(1)}, u32[]{:S(2)}, u32[]{:S(2)}) async-start(bf16[16,2,128,128]{3,2,1,0:T(8,128)(2,1)} %bitcast.6), calls=%async_computation | async-start | bytes 2097152 | tf_op jit(solution)/shard_map/all_to_all | solution.py:218
  10.2 8.3 %collective-permute-start.1 = (bf16[256,128]{1,0:T(8,128)(2,1)}, bf16[256,128]{1,0:T(8,128)(2,1)S(1)}, u32[]{:S(2)}, u32[]{:S(2)}) collective-permute-start(bf16[256,128]{1,0:T(8,128)(2,1)} %own_ref.1), channel_id=1, source_target_pairs={{0,36},{1,37},{2,38},{3,39},{4,32},{5,33},{6,34},{7,35},{32,4},{33... | collective-permute-start | bytes 196616 | tf_op jit(solution)/shard_map/ppermute | solution.py:203
  16.3 7.4 %collective-permute-start = (bf16[256,128]{1,0:T(8,128)(2,1)}, bf16[256,128]{1,0:T(8,128)(2,1)S(1)}, u32[]{:S(2)}, u32[]{:S(2)}) collective-permute-start(bf16[256,128]{1,0:T(8,128)(2,1)} %own_ref.1), channel_id=1, source_target_pairs={{0,1},{1,0},{2,3},{3,2},{4,5},{5,4},{6,7},{7,6},{8,9},{9,8},{10,11... | collective-permute-start | bytes 196616 | tf_op jit(solution)/shard_map/ppermute | solution.py:200
  18.4 5.2 %collective-permute-start.2 = (bf16[256,128]{1,0:T(8,128)(2,1)S(1)}, bf16[256,128]{1,0:T(8,128)(2,1)S(1)}, u32[]{:S(2)}, u32[]{:S(2)}) collective-permute-start(bf16[256,128]{1,0:T(8,128)(2,1)S(1)} %collective-permute-done.1.q2), channel_id=1, source_target_pairs={{0,1},{1,0},{2,3},{3,2},{4,5},{5,4},{6,7},{7,6},{8,9},{9,8},{10,11... | collective-permute-start | bytes 196616 | tf_op jit(solution)/shard_map/ppermute | solution.py:200
  20.3 0.8 %copy-start = (bf16[256,128]{1,0:T(8,128)(2,1)S(1)}, bf16[256,128]{1,0:T(8,128)(2,1)}, u32[]{:S(2)}) copy-start(bf16[256,128]{1,0:T(8,128)(2,1)} %own_ref.1) | copy-start | bytes 196612
  21.2 0.7 %copy-start.1 = (s32[4]{0:T(128)S(1)}, s32[4]{0:T(128)}, u32[]{:S(2)}) copy-start(s32[4]{0:T(128)} %docs_ref.1) | copy-start | bytes 52
  29.0 3.5 %collective-permute-start.4 = (f32[2,1024]{1,0:T(2,128)S(1)}, f32[2,1024]{1,0:T(2,128)S(1)}, u32[]{:S(2)}, u32[]{:S(2)}) collective-permute-start(f32[2,1024]{1,0:T(2,128)S(1)} %get-tuple-element.28.after_ref.mine_ref), channel_id=1, source_target_pairs={{0,1},{1,0},{2,3},{3,2},{4,5},{5,4},{6,7},{7,6},{8,9},{9,8},{10,11... | collective-permute-start | bytes 24584 | tf_op jit(solution)/shard_map/ppermute | solution.py:200
  32.4 6.3 %collective-permute-start.3 = (f32[2,256,128]{2,1,0:T(8,128)S(1)}, f32[2,256,128]{2,1,0:T(8,128)S(1)}, u32[]{:S(2)}, u32[]{:S(2)}) collective-permute-start(f32[2,256,128]{2,1,0:T(8,128)S(1)} %rows_out.1.send_ref), channel_id=1, source_target_pairs={{0,1},{1,0},{2,3},{3,2},{4,5},{5,4},{6,7},{7,6},{8,9},{9,8},{10,11... | collective-permute-start | bytes 786440 | tf_op jit(solution)/shard_map/ppermute | solution.py:200
  32.6 8.5 %collective-permute-start.6 = (f32[2,1024]{1,0:T(2,128)S(1)}, f32[2,1024]{1,0:T(2,128)S(1)}, u32[]{:S(2)}, u32[]{:S(2)}) collective-permute-start(f32[2,1024]{1,0:T(2,128)S(1)} %pair.1.pair_ref), channel_id=1, source_target_pairs={{0,36},{1,37},{2,38},{3,39},{4,32},{5,33},{6,34},{7,35},{32,4},{33... | collective-permute-start | bytes 24584 | tf_op jit(solution)/shard_map/ppermute | solution.py:203
  39.6 7.5 %collective-permute-start.5 = (bf16[256,128]{1,0:T(8,128)(2,1)S(1)}, bf16[256,128]{1,0:T(8,128)(2,1)S(1)}, u32[]{:S(2)}, u32[]{:S(2)}) collective-permute-start(bf16[256,128]{1,0:T(8,128)(2,1)S(1)} %get-tuple-element.30.send_ref), channel_id=1, source_target_pairs={{0,36},{1,37},{2,38},{3,39},{4,32},{5,33},{6,34},{7,35},{32,4},{33... | collective-permute-start | bytes 196616 | tf_op jit(solution)/shard_map/ppermute | solution.py:203
  42.3 13.4 %all-to-all-start.1 = ((f32[64,1,128]{2,1,0:T(1,128)}), f32[64,1,128]{2,1,0:T(1,128)S(1)}, u32[]{:S(2)}, u32[]{:S(2)}) async-start(f32[64,1,128]{2,1,0:T(1,128)} %bitcast.4), calls=%async_computation.1 | async-start | bytes 65536 | tf_op jit(solution)/shard_map/all_to_all | solution.py:256

commit v9 on v7

--- a/solution.py
+++ b/solution.py
@@ -117,11 +117,14 @@
     stats_ref[...] = jnp.where(first_lane, row_max, row_sum).T[0:2, :]
 
 
-def row_kernel(probs_ref, near_ref, keep_ref, send_ref):
-    acc = jnp.dot(probs_ref[...], near_ref[:, 1].reshape(KEYS, HD), preferred_element_type=jnp.float32)
+def weighted(probs_ref, near_ref, k):
+    values = near_ref[:, 1].reshape(KEYS, HD)
+    return jnp.dot(probs_ref[k * TOK : (k + 1) * TOK, :], values, preferred_element_type=jnp.float32)
+
+
+def send_kernel(probs_ref, near_ref, send_ref):
     for k in range(2):
-        keep_ref[k] = acc[2 * k * TOK : (2 * k + 1) * TOK]
-        send_ref[k] = acc[(2 * k + 1) * TOK : (2 * k + 2) * TOK]
+        send_ref[k] = weighted(probs_ref, near_ref, 2 * k + 1)
 
 
 def stat(ref, k):
@@ -142,12 +145,12 @@
         pair_ref[1:2, cut] = l0 * jnp.exp2((m0 - top) * SCALE) + l1 * jnp.exp2((m1 - top) * SCALE)
 
 
-def join_kernel(keep_ref, got_ref, mine_ref, core_ref, keep_out_ref, send_ref):
-    for k, ref in ((0, keep_out_ref), (2, send_ref)):
+def join_kernel(probs_ref, near_ref, got_ref, mine_ref, core_ref, keep_ref, send_ref):
+    for k, ref in ((0, keep_ref), (2, send_ref)):
         m0, m1 = stat(mine_ref, k)[0], stat(core_ref, k ^ 1)[0]
         top = jnp.maximum(m0, m1)
         w0, w1 = jnp.exp2((m0 - top) * SCALE), jnp.exp2((m1 - top) * SCALE)
-        joined = keep_ref[k // 2] * as_column(w0) + got_ref[k // 2] * as_column(w1)
+        joined = weighted(probs_ref, near_ref, k) * as_column(w0) + got_ref[k // 2] * as_column(w1)
         ref[...] = joined.astype(ref.dtype)
 
 
@@ -235,12 +238,12 @@
         limit=24,
     )(near, own, q1, q2, q3, row_mask, key_mask)
     core = across(mine)
-    keep, send = kernel(row_kernel, "rows", (shape((2, TOK, HD), f32),) * 2, [VMEM] * 2, flops=LONG)(probs, near)
+    send = kernel(send_kernel, "rows_sent", shape((2, TOK, HD), f32), [VMEM] * 2, flops=LONG)(probs, near)
     pair = kernel(pair_kernel, "pair", shape((2, ROWS), f32), [VMEM] * 2 + [ANY], flops=LONG)(mine, core, send)
     plane = partner(pair)
     keep, send = kernel(
-        join_kernel, "join", (shape((TOK, HD), f32), shape((TOK, HD), bf16)), [VMEM] * 4, flops=LONG
-    )(keep, across(send), mine, core)
+        join_kernel, "rows_joined", (shape((TOK, HD), f32), shape((TOK, HD), bf16)), [VMEM] * 5, flops=LONG
+    )(probs, near, across(send), mine, core)
     got = partner(send)
     cols = kernel(
         column_kernel, "columns", shape((BLOCKS * NZL, HALF), f32), [VMEM] * 4 + [ANY], flops=LONG
@@ -248,8 +251,8 @@
     parts = lax.all_to_all(cols.reshape(BLOCKS * NZL, 1, HALF), ("y", "x", "zl"), 0, 0, tiled=True)
     rows = kernel(merge_kernel, "merge", shape((TOK, HD), bf16), [VMEM] * 4, flops=LONG)(keep, got, pair, plane)
     parts, _ = lax.optimization_barrier((parts, rows))
-    totals = (jnp.sum(parts, axis=(0, 1)) / HEADS).reshape(NZL, CHUNK)
-    return rows, lax.dynamic_index_in_dim(totals, lax.axis_index("zl"), 0, keepdims=False)
+    piece = lax.dynamic_slice_in_dim(parts.reshape(BLOCKS * NZL, HALF), lax.axis_index("zl") * CHUNK, CHUNK, axis=1)
+    return rows, jnp.sum(piece, axis=0) / HEADS
 
 
 def solution(mesh):

time: 56.9 us -> 56.5 us (level)
  local copies, waits for them, and re-layouts: 2.1 us -> 1.49 us
  other arithmetic: 0.09 us -> 0.67 us
where the time goes in v9:
time: 56.5 us; the launch traced here: 56.2 us
  starting transfers between devices  31.9 us (56%)
  waiting for transfers between devices  11.3 us (20%)
  Pallas kernels  10.1 us (18%)
  local copies, waits for them, and re-layouts  1.49 us (3%)
  between operations  0.71 us (1%)
  other arithmetic  0.67 us (1%)
    ppermute x3, starting transfers between devices, partner(): return lax.ppermute(x, ('zh', 'zl', 'c'), [(i, i ^ 12) for i in range(16)])  13.7 us
    all_to_all x1, waiting for transfers between devices, body(): lax.all_to_all(cols.reshape(BLOCKS * NZL, 1, HALF), ('y', 'x', 'zl'), 0,...  7.86 us
    all_to_all x1, starting transfers between devices, body(): near = lax.all_to_all(copies, ('y', 'x'), 0, 0, tiled=True)  7.6 us
    ppermute x4, starting transfers between devices, across(): return lax.ppermute(x, 'c', [(0, 1), (1, 0)])  5.93 us
    all_to_all x1, starting transfers between devices, body(): lax.all_to_all(cols.reshape(BLOCKS * NZL, 1, HALF), ('y', 'x', 'zl'), 0,...  4.74 us
    pallas_call x1, Pallas kernels, body(): kernel(score_kernel, 'scores', (shape((ROWS, KEYS), bf16), shape((2, ROWS...  2.89 us
    all_to_all x1, waiting for transfers between devices, body(): near = lax.all_to_all(copies, ('y', 'x'), 0, 0, tiled=True)  2.49 us
    pallas_call x1, Pallas kernels, body(): kernel(spread_kernel, 'spread', shape((BLOCKS, 2, NZL, CHUNK, HD), bf16),...  1.91 us
  transfers between devices with their start and end apart: 9, of which 3 were waited for; matrix products, arithmetic and copies ran while one was open for 0% of the time, Pallas kernels for 9%

profile of v9, /device:TPU:1, one launch (start us, length us, event | category | flops | bytes accessed | tf_op | source)
XLA Modules:
  0.0 56.2 jit_solution(12003005805654141755)
XLA Ops:
  0.6 1.9 %spread.1 = bf16[16,2,4,32,128]{4,3,2,1,0:T(8,128)(2,1)} custom-call(bf16[4,2,32,128]{3,2,1,0:T(8,128)(2,1)} %bitcast.7, bf16[4,2,32,128]{3,2,1,0:T(8,128)(2,1)} %bitcast.8), custom_call_target="tpu_custom_call" | custom-call | tf_op jit(solution)/shard_map/spread/pallas_call | solution.py:207
  2.5 7.6 %all-to-all-start = ((bf16[16,2,128,128]{3,2,1,0:T(8,128)(2,1)}), bf16[16,2,128,128]{3,2,1,0:T(8,128)(2,1)S(1)}, u32[]{:S(2)}, u32[]{:S(2)}) async-start(bf16[16,2,128,128]{3,2,1,0:T(8,128)(2,1)} %bitcast.6), calls=%async_computation | async-start | bytes 2097152 | tf_op jit(solution)/shard_map/all_to_all | solution.py:220
  10.2 6.1 %collective-permute-start.1 = (bf16[256,128]{1,0:T(8,128)(2,1)}, bf16[256,128]{1,0:T(8,128)(2,1)S(1)}, u32[]{:S(2)}, u32[]{:S(2)}) collective-permute-start(bf16[256,128]{1,0:T(8,128)(2,1)} %own_ref.1), channel_id=1, source_target_pairs={{0,36},{1,37},{2,38},{3,39},{4,32},{5,33},{6,34},{7,35},{32,4},{33... | collective-permute-start | bytes 196616 | tf_op jit(solution)/shard_map/ppermute | solution.py:205
  16.3 1.2 %collective-permute-start = (bf16[256,128]{1,0:T(8,128)(2,1)}, bf16[256,128]{1,0:T(8,128)(2,1)S(1)}, u32[]{:S(2)}, u32[]{:S(2)}) collective-permute-start(bf16[256,128]{1,0:T(8,128)(2,1)} %own_ref.1), channel_id=1, source_target_pairs={{0,1},{1,0},{2,3},{3,2},{4,5},{5,4},{6,7},{7,6},{8,9},{9,8},{10,11... | collective-permute-start | bytes 196616 | tf_op jit(solution)/shard_map/ppermute | solution.py:202
  17.5 0.9 %collective-permute-done.1.q2 = bf16[256,128]{1,0:T(8,128)(2,1)S(1)} collective-permute-done((bf16[256,128]{1,0:T(8,128)(2,1)}, bf16[256,128]{1,0:T(8,128)(2,1)S(1)}, u32[]{:S(2)}, u32[]{:S(2)}) %collective-permute-start.1) | collective-permute-done | bytes 65568 | tf_op jit(solution)/shard_map/ppermute | solution.py:205
  18.4 1.9 %collective-permute-start.2 = (bf16[256,128]{1,0:T(8,128)(2,1)S(1)}, bf16[256,128]{1,0:T(8,128)(2,1)S(1)}, u32[]{:S(2)}, u32[]{:S(2)}) collective-permute-start(bf16[256,128]{1,0:T(8,128)(2,1)S(1)} %collective-permute-done.1.q2), channel_id=1, source_target_pairs={{0,1},{1,0},{2,3},{3,2},{4,5},{5,4},{6,7},{7,6},{8,9},{9,8},{10,11... | collective-permute-start | bytes 196616 | tf_op jit(solution)/shard_map/ppermute | solution.py:202
  20.3 0.8 %copy-done = bf16[256,128]{1,0:T(8,128)(2,1)S(1)} copy-done((bf16[256,128]{1,0:T(8,128)(2,1)S(1)}, bf16[256,128]{1,0:T(8,128)(2,1)}, u32[]{:S(2)}) %copy-start) | copy-done | bytes 65560
  21.2 0.7 %copy-done.1 = s32[4]{0:T(128)S(1)} copy-done((s32[4]{0:T(128)S(1)}, s32[4]{0:T(128)}, u32[]{:S(2)}) %copy-start.1) | copy-done | bytes 40
  21.8 1.8 %limits.1 = (bf16[256,128]{1,0:T(8,128)(2,1)S(1)}, bf16[1024,128]{1,0:T(8,128)(2,1)S(1)}, bf16[2048,128]{1,0:T(8,128)(2,1)S(1)}) custom-call(s32[4]{0:T(128)S(1)} %copy-done.1, bf16[256,128]{1,0:T(8,128)(2,1)S(1)} %copy-done), custom_call_target="tpu_custom_call" | custom-call | tf_op jit(solution)/shard_map/limits/pallas_call | solution.py:223
  23.7 2.5 %all-to-all-done.near_ref = bf16[16,2,128,128]{3,2,1,0:T(8,128)(2,1)S(1)} async-done(((bf16[16,2,128,128]{3,2,1,0:T(8,128)(2,1)}), bf16[16,2,128,128]{3,2,1,0:T(8,128)(2,1)S(1)}, u32[]{:S(2)}, u32[]{:S(2)}) %all-to-all-start) | async-done | bytes 1048608 | tf_op jit(solution)/shard_map/all_to_all | solution.py:220
  26.1 2.9 %scores.1 = (bf16[1024,2048]{1,0:T(8,128)(2,1)S(1)}, f32[2,1024]{1,0:T(2,128)S(1)}) custom-call(bf16[16,2,128,128]{3,2,1,0:T(8,128)(2,1)S(1)} %all-to-all-done.near_ref, bf16[256,128]{1,0:T(8,128)(2,1)S(1)} %get-tuple-element.21.q0, bf16[256,128]{1,0:T(8,128)(2,1)S(1)} %collective-permute-done.q1, bf16[256,128]{1,0:T(8,128)(2,1)S(1)} %collective-permute-done.1.q2, ...), custom_call_target="tpu_custom_call" | custom-call | tf_op jit(solution)/shard_map/scores/pallas_call | solution.py:232
  29.0 2.7 %collective-permute-start.4 = (f32[2,1024]{1,0:T(2,128)S(1)}, f32[2,1024]{1,0:T(2,128)S(1)}, u32[]{:S(2)}, u32[]{:S(2)}) collective-permute-start(f32[2,1024]{1,0:T(2,128)S(1)} %get-tuple-element.28.mine_ref), channel_id=1, source_target_pairs={{0,1},{1,0},{2,3},{3,2},{4,5},{5,4},{6,7},{7,6},{8,9},{9,8},{10,11... | collective-permute-start | bytes 24584 | tf_op jit(solution)/shard_map/ppermute | solution.py:202
  31.7 0.7 %rows_sent.1.send_ref = f32[2,256,128]{2,1,0:T(8,128)S(1)} custom-call(bf16[1024,2048]{1,0:T(8,128)(2,1)S(1)} %get-tuple-element.27.probs_ref, bf16[16,2,128,128]{3,2,1,0:T(8,128)(2,1)S(1)} %all-to-all-done.near_ref), custom_call_target="tpu_custom_call" | custom-call | flops 20000000000 | tf_op jit(solution)/shard_map/rows_sent/pallas_call | solution.py:241
  32.4 0.1 collective-permute-start.3
  32.5 0.0 collective-permute-done.4.core_ref
  32.6 6.1 %collective-permute-start.6 = (f32[2,1024]{1,0:T(2,128)S(1)}, f32[2,1024]{1,0:T(2,128)S(1)}, u32[]{:S(2)}, u32[]{:S(2)}) collective-permute-start(f32[2,1024]{1,0:T(2,128)S(1)} %pair.1.pair_ref), channel_id=1, source_target_pairs={{0,36},{1,37},{2,38},{3,39},{4,32},{5,33},{6,34},{7,35},{32,4},{33... | collective-permute-start | bytes 24584 | tf_op jit(solution)/shard_map/ppermute | solution.py:205
  38.7 0.7 %rows_joined.1 = (f32[256,128]{1,0:T(8,128)S(1)}, bf16[256,128]{1,0:T(8,128)(2,1)S(1)}) custom-call(bf16[1024,2048]{1,0:T(8,128)(2,1)S(1)} %get-tuple-element.27.probs_ref, bf16[16,2,128,128]{3,2,1,0:T(8,128)(2,1)S(1)} %all-to-all-done.near_ref, f32[2,256,128]{2,1,0:T(8,128)S(1)} %collective-permute-done.3.got_ref, ...), custom_call_target="tpu_custom_call" | custom-call | flops 20000000000 | tf_op jit(solution)/shard_map/rows_joined/pallas_call | solution.py:244
  39.4 1.5 %collective-permute-start.5 = (bf16[256,128]{1,0:T(8,128)(2,1)S(1)}, bf16[256,128]{1,0:T(8,128)(2,1)S(1)}, u32[]{:S(2)}, u32[]{:S(2)}) collective-permute-start(bf16[256,128]{1,0:T(8,128)(2,1)S(1)} %get-tuple-element.30.send_ref), channel_id=1, source_target_pairs={{0,36},{1,37},{2,38},{3,39},{4,32},{5,33},{6,34},{7,35},{32,4},{33... | collective-permute-start | bytes 196616 | tf_op jit(solution)/shard_map/ppermute | solution.py:205
  40.9 1.3 %columns.1 = f32[64,128]{1,0:T(8,128)} custom-call(bf16[1024,2048]{1,0:T(8,128)(2,1)S(1)} %get-tuple-element.27.probs_ref, f32[2,1024]{1,0:T(2,128)S(1)} %get-tuple-element.28.mine_ref, f32[2,1024]{1,0:T(2,128)S(1)} %pair.1.pair_ref, f32[2,1024]{1,0:T(2,128)S(1)} %collective-permute-done.6.plane_ref, bf16[256,128]{1,0:T(8,128)(2,1)S(1)} %get-tuple-element.30.send_ref), custom_call_target="tpu_custom_call" | custom-call | flops 20000000000 | tf_op jit(solution)/shard_map/columns/pallas_call | solution.py:248
  42.1 4.7 %all-to-all-start.1 = ((f32[64,1,128]{2,1,0:T(1,128)}), f32[64,1,128]{2,1,0:T(1,128)S(1)}, u32[]{:S(2)}, u32[]{:S(2)}) async-start(f32[64,1,128]{2,1,0:T(1,128)} %bitcast.4), calls=%async_computation.1 | async-start | bytes 65536 | tf_op jit(solution)/shard_map/all_to_all | solution.py:251
  46.9 0.8 %merge.1 = bf16[256,128]{1,0:T(8,128)(2,1)} custom-call(f32[256,128]{1,0:T(8,128)S(1)} %get-tuple-element.29.keep_ref, bf16[256,128]{1,0:T(8,128)(2,1)S(1)} %collective-permute-done.5.got_ref, f32[2,1024]{1,0:T(2,128)S(1)} %pair.1.pair_ref, f32[2,1024]{1,0:T(2,128)S(1)} %collective-permute-done.6.plane_ref), custom_call_target="tpu_custom_call" | custom-call | flops 20000000000 | tf_op jit(solution)/shard_map/merge/pallas_call | solution.py:252
  47.7 7.9 %all-to-all-done.1 = f32[64,1,128]{2,1,0:T(1,128)S(1)} async-done(((f32[64,1,128]{2,1,0:T(1,128)}), f32[64,1,128]{2,1,0:T(1,128)S(1)}, u32[]{:S(2)}, u32[]{:S(2)}) %all-to-all-start.1) | async-done | bytes 32800 | tf_op jit(solution)/shard_map/all_to_all | solution.py:251
  55.5 0.2 dynamic-slice_reduce_fusion
  55.7 0.5 broadcast_multiply_fusion
  (8 shorter events, 0.0 us)
Async XLA Ops:
  2.5 23.6 %all-to-all-start = ((bf16[16,2,128,128]{3,2,1,0:T(8,128)(2,1)}), bf16[16,2,128,128]{3,2,1,0:T(8,128)(2,1)S(1)}, u32[]{:S(2)}, u32[]{:S(2)}) async-start(bf16[16,2,128,128]{3,2,1,0:T(8,128)(2,1)} %bitcast.6), calls=%async_computation | async-start | bytes 2097152 | tf_op jit(solution)/shard_map/all_to_all | solution.py:220
  10.2 8.3 %collective-permute-start.1 = (bf16[256,128]{1,0:T(8,128)(2,1)}, bf16[256,128]{1,0:T(8,128)(2,1)S(1)}, u32[]{:S(2)}, u32[]{:S(2)}) collective-permute-start(bf16[256,128]{1,0:T(8,128)(2,1)} %own_ref.1), channel_id=1, source_target_pairs={{0,36},{1,37},{2,38},{3,39},{4,32},{5,33},{6,34},{7,35},{32,4},{33... | collective-permute-start | bytes 196616 | tf_op jit(solution)/shard_map/ppermute | solution.py:205
  16.3 7.4 %collective-permute-start = (bf16[256,128]{1,0:T(8,128)(2,1)}, bf16[256,128]{1,0:T(8,128)(2,1)S(1)}, u32[]{:S(2)}, u32[]{:S(2)}) collective-permute-start(bf16[256,128]{1,0:T(8,128)(2,1)} %own_ref.1), channel_id=1, source_target_pairs={{0,1},{1,0},{2,3},{3,2},{4,5},{5,4},{6,7},{7,6},{8,9},{9,8},{10,11... | collective-permute-start | bytes 196616 | tf_op jit(solution)/shard_map/ppermute | solution.py:202
  18.4 5.2 %collective-permute-start.2 = (bf16[256,128]{1,0:T(8,128)(2,1)S(1)}, bf16[256,128]{1,0:T(8,128)(2,1)S(1)}, u32[]{:S(2)}, u32[]{:S(2)}) collective-permute-start(bf16[256,128]{1,0:T(8,128)(2,1)S(1)} %collective-permute-done.1.q2), channel_id=1, source_target_pairs={{0,1},{1,0},{2,3},{3,2},{4,5},{5,4},{6,7},{7,6},{8,9},{9,8},{10,11... | collective-permute-start | bytes 196616 | tf_op jit(solution)/shard_map/ppermute | solution.py:202
  20.3 0.8 %copy-start = (bf16[256,128]{1,0:T(8,128)(2,1)S(1)}, bf16[256,128]{1,0:T(8,128)(2,1)}, u32[]{:S(2)}) copy-start(bf16[256,128]{1,0:T(8,128)(2,1)} %own_ref.1) | copy-start | bytes 196612
  21.2 0.7 %copy-start.1 = (s32[4]{0:T(128)S(1)}, s32[4]{0:T(128)}, u32[]{:S(2)}) copy-start(s32[4]{0:T(128)} %docs_ref.1) | copy-start | bytes 52
  29.0 3.5 %collective-permute-start.4 = (f32[2,1024]{1,0:T(2,128)S(1)}, f32[2,1024]{1,0:T(2,128)S(1)}, u32[]{:S(2)}, u32[]{:S(2)}) collective-permute-start(f32[2,1024]{1,0:T(2,128)S(1)} %get-tuple-element.28.mine_ref), channel_id=1, source_target_pairs={{0,1},{1,0},{2,3},{3,2},{4,5},{5,4},{6,7},{7,6},{8,9},{9,8},{10,11... | collective-permute-start | bytes 24584 | tf_op jit(solution)/shard_map/ppermute | solution.py:202
  32.4 6.3 %collective-permute-start.3 = (f32[2,256,128]{2,1,0:T(8,128)S(1)}, f32[2,256,128]{2,1,0:T(8,128)S(1)}, u32[]{:S(2)}, u32[]{:S(2)}) collective-permute-start(f32[2,256,128]{2,1,0:T(8,128)S(1)} %rows_sent.1.send_ref), channel_id=1, source_target_pairs={{0,1},{1,0},{2,3},{3,2},{4,5},{5,4},{6,7},{7,6},{8,9},{9,8},{10,11... | collective-permute-start | bytes 786440 | tf_op jit(solution)/shard_map/ppermute | solution.py:202
  32.6 8.3 %collective-permute-start.6 = (f32[2,1024]{1,0:T(2,128)S(1)}, f32[2,1024]{1,0:T(2,128)S(1)}, u32[]{:S(2)}, u32[]{:S(2)}) collective-permute-start(f32[2,1024]{1,0:T(2,128)S(1)} %pair.1.pair_ref), channel_id=1, source_target_pairs={{0,36},{1,37},{2,38},{3,39},{4,32},{5,33},{6,34},{7,35},{32,4},{33... | collective-permute-start | bytes 24584 | tf_op jit(solution)/shard_map/ppermute | solution.py:205
  39.4 7.5 %collective-permute-start.5 = (bf16[256,128]{1,0:T(8,128)(2,1)S(1)}, bf16[256,128]{1,0:T(8,128)(2,1)S(1)}, u32[]{:S(2)}, u32[]{:S(2)}) collective-permute-start(bf16[256,128]{1,0:T(8,128)(2,1)S(1)} %get-tuple-element.30.send_ref), channel_id=1, source_target_pairs={{0,36},{1,37},{2,38},{3,39},{4,32},{5,33},{6,34},{7,35},{32,4},{33... | collective-permute-start | bytes 196616 | tf_op jit(solution)/shard_map/ppermute | solution.py:205
  42.1 13.4 %all-to-all-start.1 = ((f32[64,1,128]{2,1,0:T(1,128)}), f32[64,1,128]{2,1,0:T(1,128)S(1)}, u32[]{:S(2)}, u32[]{:S(2)}) async-start(f32[64,1,128]{2,1,0:T(1,128)} %bitcast.4), calls=%async_computation.1 | async-start | bytes 65536 | tf_op jit(solution)/shard_map/all_to_all | solution.py:251

commit v10 on v9

--- a/solution.py
+++ b/solution.py
@@ -124,7 +124,7 @@
 
 def send_kernel(probs_ref, near_ref, send_ref):
     for k in range(2):
-        send_ref[k] = weighted(probs_ref, near_ref, 2 * k + 1)
+        send_ref[k] = weighted(probs_ref, near_ref, 2 * k + 1).astype(jnp.bfloat16)
 
 
 def stat(ref, k):
@@ -150,7 +150,7 @@
         m0, m1 = stat(mine_ref, k)[0], stat(core_ref, k ^ 1)[0]
         top = jnp.maximum(m0, m1)
         w0, w1 = jnp.exp2((m0 - top) * SCALE), jnp.exp2((m1 - top) * SCALE)
-        joined = weighted(probs_ref, near_ref, k) * as_column(w0) + got_ref[k // 2] * as_column(w1)
+        joined = weighted(probs_ref, near_ref, k) * as_column(w0) + got_ref[k // 2].astype(jnp.float32) * as_column(w1)
         ref[...] = joined.astype(ref.dtype)
 
 
@@ -238,7 +238,7 @@
         limit=24,
     )(near, own, q1, q2, q3, row_mask, key_mask)
     core = across(mine)
-    send = kernel(send_kernel, "rows_sent", shape((2, TOK, HD), f32), [VMEM] * 2, flops=LONG)(probs, near)
+    send = kernel(send_kernel, "rows_sent", shape((2, TOK, HD), bf16), [VMEM] * 2, flops=LONG)(probs, near)
     pair = kernel(pair_kernel, "pair", shape((2, ROWS), f32), [VMEM] * 2 + [ANY], flops=LONG)(mine, core, send)
     plane = partner(pair)
     keep, send = kernel(

time: 56.5 us -> 56.3 us (level)
  no operation moved by 1% of the time
where the time goes in v10:
time: 56.3 us; the launch traced here: 56 us
  starting transfers between devices  31.8 us (56%)
  waiting for transfers between devices  11.3 us (20%)
  Pallas kernels  10.1 us (18%)
  local copies, waits for them, and re-layouts  1.49 us (3%)
  between operations  0.71 us (1%)
  other arithmetic  0.67 us (1%)
    ppermute x3, starting transfers between devices, partner(): return lax.ppermute(x, ('zh', 'zl', 'c'), [(i, i ^ 12) for i in range(16)])  13.5 us
    all_to_all x1, waiting for transfers between devices, body(): lax.all_to_all(cols.reshape(BLOCKS * NZL, 1, HALF), ('y', 'x', 'zl'), 0,...  7.86 us
    all_to_all x1, starting transfers between devices, body(): near = lax.all_to_all(copies, ('y', 'x'), 0, 0, tiled=True)  7.6 us
    ppermute x4, starting transfers between devices, across(): return lax.ppermute(x, 'c', [(0, 1), (1, 0)])  5.93 us
    all_to_all x1, starting transfers between devices, body(): lax.all_to_all(cols.reshape(BLOCKS * NZL, 1, HALF), ('y', 'x', 'zl'), 0,...  4.74 us
    pallas_call x1, Pallas kernels, body(): kernel(score_kernel, 'scores', (shape((ROWS, KEYS), bf16), shape((2, ROWS...  2.89 us
    all_to_all x1, waiting for transfers between devices, body(): near = lax.all_to_all(copies, ('y', 'x'), 0, 0, tiled=True)  2.49 us
    pallas_call x1, Pallas kernels, body(): kernel(spread_kernel, 'spread', shape((BLOCKS, 2, NZL, CHUNK, HD), bf16),...  1.91 us
  transfers between devices with their start and end apart: 9, of which 3 were waited for; matrix products, arithmetic and copies ran while one was open for 0% of the time, Pallas kernels for 9%

profile of v10, /device:TPU:1, one launch (start us, length us, event | category | flops | bytes accessed | tf_op | source)
XLA Modules:
  0.0 56.0 jit_solution(15109603423596679316)
XLA Ops:
  0.6 1.9 %spread.1 = bf16[16,2,4,32,128]{4,3,2,1,0:T(8,128)(2,1)} custom-call(bf16[4,2,32,128]{3,2,1,0:T(8,128)(2,1)} %bitcast.7, bf16[4,2,32,128]{3,2,1,0:T(8,128)(2,1)} %bitcast.8), custom_call_target="tpu_custom_call" | custom-call | tf_op jit(solution)/shard_map/spread/pallas_call | solution.py:207
  2.5 7.6 %all-to-all-start = ((bf16[16,2,128,128]{3,2,1,0:T(8,128)(2,1)}), bf16[16,2,128,128]{3,2,1,0:T(8,128)(2,1)S(1)}, u32[]{:S(2)}, u32[]{:S(2)}) async-start(bf16[16,2,128,128]{3,2,1,0:T(8,128)(2,1)} %bitcast.6), calls=%async_computation | async-start | bytes 2097152 | tf_op jit(solution)/shard_map/all_to_all | solution.py:220
  10.2 6.1 %collective-permute-start.1 = (bf16[256,128]{1,0:T(8,128)(2,1)}, bf16[256,128]{1,0:T(8,128)(2,1)S(1)}, u32[]{:S(2)}, u32[]{:S(2)}) collective-permute-start(bf16[256,128]{1,0:T(8,128)(2,1)} %own_ref.1), channel_id=1, source_target_pairs={{0,36},{1,37},{2,38},{3,39},{4,32},{5,33},{6,34},{7,35},{32,4},{33... | collective-permute-start | bytes 196616 | tf_op jit(solution)/shard_map/ppermute | solution.py:205
  16.3 1.2 %collective-permute-start = (bf16[256,128]{1,0:T(8,128)(2,1)}, bf16[256,128]{1,0:T(8,128)(2,1)S(1)}, u32[]{:S(2)}, u32[]{:S(2)}) collective-permute-start(bf16[256,128]{1,0:T(8,128)(2,1)} %own_ref.1), channel_id=1, source_target_pairs={{0,1},{1,0},{2,3},{3,2},{4,5},{5,4},{6,7},{7,6},{8,9},{9,8},{10,11... | collective-permute-start | bytes 196616 | tf_op jit(solution)/shard_map/ppermute | solution.py:202
  17.5 0.9 %collective-permute-done.1.q2 = bf16[256,128]{1,0:T(8,128)(2,1)S(1)} collective-permute-done((bf16[256,128]{1,0:T(8,128)(2,1)}, bf16[256,128]{1,0:T(8,128)(2,1)S(1)}, u32[]{:S(2)}, u32[]{:S(2)}) %collective-permute-start.1) | collective-permute-done | bytes 65568 | tf_op jit(solution)/shard_map/ppermute | solution.py:205
  18.4 1.9 %collective-permute-start.2 = (bf16[256,128]{1,0:T(8,128)(2,1)S(1)}, bf16[256,128]{1,0:T(8,128)(2,1)S(1)}, u32[]{:S(2)}, u32[]{:S(2)}) collective-permute-start(bf16[256,128]{1,0:T(8,128)(2,1)S(1)} %collective-permute-done.1.q2), channel_id=1, source_target_pairs={{0,1},{1,0},{2,3},{3,2},{4,5},{5,4},{6,7},{7,6},{8,9},{9,8},{10,11... | collective-permute-start | bytes 196616 | tf_op jit(solution)/shard_map/ppermute | solution.py:202
  20.3 0.8 %copy-done = bf16[256,128]{1,0:T(8,128)(2,1)S(1)} copy-done((bf16[256,128]{1,0:T(8,128)(2,1)S(1)}, bf16[256,128]{1,0:T(8,128)(2,1)}, u32[]{:S(2)}) %copy-start) | copy-done | bytes 65560
  21.2 0.7 %copy-done.1 = s32[4]{0:T(128)S(1)} copy-done((s32[4]{0:T(128)S(1)}, s32[4]{0:T(128)}, u32[]{:S(2)}) %copy-start.1) | copy-done | bytes 40
  21.8 1.8 %limits.1 = (bf16[256,128]{1,0:T(8,128)(2,1)S(1)}, bf16[1024,128]{1,0:T(8,128)(2,1)S(1)}, bf16[2048,128]{1,0:T(8,128)(2,1)S(1)}) custom-call(s32[4]{0:T(128)S(1)} %copy-done.1, bf16[256,128]{1,0:T(8,128)(2,1)S(1)} %copy-done), custom_call_target="tpu_custom_call" | custom-call | tf_op jit(solution)/shard_map/limits/pallas_call | solution.py:223
  23.7 2.5 %all-to-all-done.near_ref = bf16[16,2,128,128]{3,2,1,0:T(8,128)(2,1)S(1)} async-done(((bf16[16,2,128,128]{3,2,1,0:T(8,128)(2,1)}), bf16[16,2,128,128]{3,2,1,0:T(8,128)(2,1)S(1)}, u32[]{:S(2)}, u32[]{:S(2)}) %all-to-all-start) | async-done | bytes 1048608 | tf_op jit(solution)/shard_map/all_to_all | solution.py:220
  26.1 2.9 %scores.1 = (bf16[1024,2048]{1,0:T(8,128)(2,1)S(1)}, f32[2,1024]{1,0:T(2,128)S(1)}) custom-call(bf16[16,2,128,128]{3,2,1,0:T(8,128)(2,1)S(1)} %all-to-all-done.near_ref, bf16[256,128]{1,0:T(8,128)(2,1)S(1)} %get-tuple-element.21.q0, bf16[256,128]{1,0:T(8,128)(2,1)S(1)} %collective-permute-done.q1, bf16[256,128]{1,0:T(8,128)(2,1)S(1)} %collective-permute-done.1.q2, ...), custom_call_target="tpu_custom_call" | custom-call | tf_op jit(solution)/shard_map/scores/pallas_call | solution.py:232
  29.0 2.7 %collective-permute-start.4 = (f32[2,1024]{1,0:T(2,128)S(1)}, f32[2,1024]{1,0:T(2,128)S(1)}, u32[]{:S(2)}, u32[]{:S(2)}) collective-permute-start(f32[2,1024]{1,0:T(2,128)S(1)} %get-tuple-element.28.mine_ref), channel_id=1, source_target_pairs={{0,1},{1,0},{2,3},{3,2},{4,5},{5,4},{6,7},{7,6},{8,9},{9,8},{10,11... | collective-permute-start | bytes 24584 | tf_op jit(solution)/shard_map/ppermute | solution.py:202
  31.7 0.7 %rows_sent.1.send_ref = bf16[2,256,128]{2,1,0:T(8,128)(2,1)S(1)} custom-call(bf16[1024,2048]{1,0:T(8,128)(2,1)S(1)} %get-tuple-element.27.probs_ref, bf16[16,2,128,128]{3,2,1,0:T(8,128)(2,1)S(1)} %all-to-all-done.near_ref), custom_call_target="tpu_custom_call" | custom-call | flops 20000000000 | tf_op jit(solution)/shard_map/rows_sent/pallas_call | solution.py:241
  32.4 0.1 collective-permute-start.3
  32.5 0.0 collective-permute-done.4.core_ref
  32.6 6.1 %collective-permute-start.6 = (f32[2,1024]{1,0:T(2,128)S(1)}, f32[2,1024]{1,0:T(2,128)S(1)}, u32[]{:S(2)}, u32[]{:S(2)}) collective-permute-start(f32[2,1024]{1,0:T(2,128)S(1)} %pair.1.pair_ref), channel_id=1, source_target_pairs={{0,36},{1,37},{2,38},{3,39},{4,32},{5,33},{6,34},{7,35},{32,4},{33... | collective-permute-start | bytes 24584 | tf_op jit(solution)/shard_map/ppermute | solution.py:205
  38.7 0.7 %rows_joined.1 = (f32[256,128]{1,0:T(8,128)S(1)}, bf16[256,128]{1,0:T(8,128)(2,1)S(1)}) custom-call(bf16[1024,2048]{1,0:T(8,128)(2,1)S(1)} %get-tuple-element.27.probs_ref, bf16[16,2,128,128]{3,2,1,0:T(8,128)(2,1)S(1)} %all-to-all-done.near_ref, bf16[2,256,128]{2,1,0:T(8,128)(2,1)S(1)} %collective-permute-done.3.got_ref, ...), custom_call_target="tpu_custom_call" | custom-call | flops 20000000000 | tf_op jit(solution)/shard_map/rows_joined/pallas_call | solution.py:244
  39.4 1.3 %collective-permute-start.5 = (bf16[256,128]{1,0:T(8,128)(2,1)S(1)}, bf16[256,128]{1,0:T(8,128)(2,1)S(1)}, u32[]{:S(2)}, u32[]{:S(2)}) collective-permute-start(bf16[256,128]{1,0:T(8,128)(2,1)S(1)} %get-tuple-element.30.send_ref), channel_id=1, source_target_pairs={{0,36},{1,37},{2,38},{3,39},{4,32},{5,33},{6,34},{7,35},{32,4},{33... | collective-permute-start | bytes 196616 | tf_op jit(solution)/shard_map/ppermute | solution.py:205
  40.7 1.3 %columns.1 = f32[64,128]{1,0:T(8,128)} custom-call(bf16[1024,2048]{1,0:T(8,128)(2,1)S(1)} %get-tuple-element.27.probs_ref, f32[2,1024]{1,0:T(2,128)S(1)} %get-tuple-element.28.mine_ref, f32[2,1024]{1,0:T(2,128)S(1)} %pair.1.pair_ref, f32[2,1024]{1,0:T(2,128)S(1)} %collective-permute-done.6.plane_ref, bf16[256,128]{1,0:T(8,128)(2,1)S(1)} %get-tuple-element.30.send_ref), custom_call_target="tpu_custom_call" | custom-call | flops 20000000000 | tf_op jit(solution)/shard_map/columns/pallas_call | solution.py:248
  41.9 4.7 %all-to-all-start.1 = ((f32[64,1,128]{2,1,0:T(1,128)}), f32[64,1,128]{2,1,0:T(1,128)S(1)}, u32[]{:S(2)}, u32[]{:S(2)}) async-start(f32[64,1,128]{2,1,0:T(1,128)} %bitcast.4), calls=%async_computation.1 | async-start | bytes 65536 | tf_op jit(solution)/shard_map/all_to_all | solution.py:251
  46.7 0.8 %merge.1 = bf16[256,128]{1,0:T(8,128)(2,1)} custom-call(f32[256,128]{1,0:T(8,128)S(1)} %get-tuple-element.29.keep_ref, bf16[256,128]{1,0:T(8,128)(2,1)S(1)} %collective-permute-done.5.got_ref, f32[2,1024]{1,0:T(2,128)S(1)} %pair.1.pair_ref, f32[2,1024]{1,0:T(2,128)S(1)} %collective-permute-done.6.plane_ref), custom_call_target="tpu_custom_call" | custom-call | flops 20000000000 | tf_op jit(solution)/shard_map/merge/pallas_call | solution.py:252
  47.5 7.9 %all-to-all-done.1 = f32[64,1,128]{2,1,0:T(1,128)S(1)} async-done(((f32[64,1,128]{2,1,0:T(1,128)}), f32[64,1,128]{2,1,0:T(1,128)S(1)}, u32[]{:S(2)}, u32[]{:S(2)}) %all-to-all-start.1) | async-done | bytes 32800 | tf_op jit(solution)/shard_map/all_to_all | solution.py:251
  55.3 0.2 dynamic-slice_reduce_fusion
  55.5 0.5 broadcast_multiply_fusion
  (8 shorter events, 0.0 us)
Async XLA Ops:
  2.5 23.6 %all-to-all-start = ((bf16[16,2,128,128]{3,2,1,0:T(8,128)(2,1)}), bf16[16,2,128,128]{3,2,1,0:T(8,128)(2,1)S(1)}, u32[]{:S(2)}, u32[]{:S(2)}) async-start(bf16[16,2,128,128]{3,2,1,0:T(8,128)(2,1)} %bitcast.6), calls=%async_computation | async-start | bytes 2097152 | tf_op jit(solution)/shard_map/all_to_all | solution.py:220
  10.2 8.3 %collective-permute-start.1 = (bf16[256,128]{1,0:T(8,128)(2,1)}, bf16[256,128]{1,0:T(8,128)(2,1)S(1)}, u32[]{:S(2)}, u32[]{:S(2)}) collective-permute-start(bf16[256,128]{1,0:T(8,128)(2,1)} %own_ref.1), channel_id=1, source_target_pairs={{0,36},{1,37},{2,38},{3,39},{4,32},{5,33},{6,34},{7,35},{32,4},{33... | collective-permute-start | bytes 196616 | tf_op jit(solution)/shard_map/ppermute | solution.py:205
  16.3 7.4 %collective-permute-start = (bf16[256,128]{1,0:T(8,128)(2,1)}, bf16[256,128]{1,0:T(8,128)(2,1)S(1)}, u32[]{:S(2)}, u32[]{:S(2)}) collective-permute-start(bf16[256,128]{1,0:T(8,128)(2,1)} %own_ref.1), channel_id=1, source_target_pairs={{0,1},{1,0},{2,3},{3,2},{4,5},{5,4},{6,7},{7,6},{8,9},{9,8},{10,11... | collective-permute-start | bytes 196616 | tf_op jit(solution)/shard_map/ppermute | solution.py:202
  18.4 5.2 %collective-permute-start.2 = (bf16[256,128]{1,0:T(8,128)(2,1)S(1)}, bf16[256,128]{1,0:T(8,128)(2,1)S(1)}, u32[]{:S(2)}, u32[]{:S(2)}) collective-permute-start(bf16[256,128]{1,0:T(8,128)(2,1)S(1)} %collective-permute-done.1.q2), channel_id=1, source_target_pairs={{0,1},{1,0},{2,3},{3,2},{4,5},{5,4},{6,7},{7,6},{8,9},{9,8},{10,11... | collective-permute-start | bytes 196616 | tf_op jit(solution)/shard_map/ppermute | solution.py:202
  20.3 0.8 %copy-start = (bf16[256,128]{1,0:T(8,128)(2,1)S(1)}, bf16[256,128]{1,0:T(8,128)(2,1)}, u32[]{:S(2)}) copy-start(bf16[256,128]{1,0:T(8,128)(2,1)} %own_ref.1) | copy-start | bytes 196612
  21.2 0.7 %copy-start.1 = (s32[4]{0:T(128)S(1)}, s32[4]{0:T(128)}, u32[]{:S(2)}) copy-start(s32[4]{0:T(128)} %docs_ref.1) | copy-start | bytes 52
  29.0 3.5 %collective-permute-start.4 = (f32[2,1024]{1,0:T(2,128)S(1)}, f32[2,1024]{1,0:T(2,128)S(1)}, u32[]{:S(2)}, u32[]{:S(2)}) collective-permute-start(f32[2,1024]{1,0:T(2,128)S(1)} %get-tuple-element.28.mine_ref), channel_id=1, source_target_pairs={{0,1},{1,0},{2,3},{3,2},{4,5},{5,4},{6,7},{7,6},{8,9},{9,8},{10,11... | collective-permute-start | bytes 24584 | tf_op jit(solution)/shard_map/ppermute | solution.py:202
  32.4 6.3 %collective-permute-start.3 = (bf16[2,256,128]{2,1,0:T(8,128)(2,1)S(1)}, bf16[2,256,128]{2,1,0:T(8,128)(2,1)S(1)}, u32[]{:S(2)}, u32[]{:S(2)}) collective-permute-start(bf16[2,256,128]{2,1,0:T(8,128)(2,1)S(1)} %rows_sent.1.send_ref), channel_id=1, source_target_pairs={{0,1},{1,0},{2,3},{3,2},{4,5},{5,4},{6,7},{7,6},{8,9},{9,8},{10,11... | collective-permute-start | bytes 393224 | tf_op jit(solution)/shard_map/ppermute | solution.py:202
  32.6 8.1 %collective-permute-start.6 = (f32[2,1024]{1,0:T(2,128)S(1)}, f32[2,1024]{1,0:T(2,128)S(1)}, u32[]{:S(2)}, u32[]{:S(2)}) collective-permute-start(f32[2,1024]{1,0:T(2,128)S(1)} %pair.1.pair_ref), channel_id=1, source_target_pairs={{0,36},{1,37},{2,38},{3,39},{4,32},{5,33},{6,34},{7,35},{32,4},{33... | collective-permute-start | bytes 24584 | tf_op jit(solution)/shard_map/ppermute | solution.py:205
  39.4 7.3 %collective-permute-start.5 = (bf16[256,128]{1,0:T(8,128)(2,1)S(1)}, bf16[256,128]{1,0:T(8,128)(2,1)S(1)}, u32[]{:S(2)}, u32[]{:S(2)}) collective-permute-start(bf16[256,128]{1,0:T(8,128)(2,1)S(1)} %get-tuple-element.30.send_ref), channel_id=1, source_target_pairs={{0,36},{1,37},{2,38},{3,39},{4,32},{5,33},{6,34},{7,35},{32,4},{33... | collective-permute-start | bytes 196616 | tf_op jit(solution)/shard_map/ppermute | solution.py:205
  41.9 13.4 %all-to-all-start.1 = ((f32[64,1,128]{2,1,0:T(1,128)}), f32[64,1,128]{2,1,0:T(1,128)S(1)}, u32[]{:S(2)}, u32[]{:S(2)}) async-start(f32[64,1,128]{2,1,0:T(1,128)} %bitcast.4), calls=%async_computation.1 | async-start | bytes 65536 | tf_op jit(solution)/shard_map/all_to_all | solution.py:251

commit v11 on v10

--- a/solution.py
+++ b/solution.py
@@ -16,6 +16,7 @@
 CHUNK = TOK // HEADS
 HALF = TOK // 2
 BLOCKS = AXES["y"] * NX
+ORDER = [y * NX + x for y in (0, 2, 1, 3) for x in range(NX)]
 KEYS = BLOCKS * HALF
 FLIPS = 4
 ROWS = FLIPS * TOK
@@ -47,6 +48,10 @@
         copy.wait()
 
 
+def swapped(major):
+    return major % 2 * 2 + major // 2
+
+
 def inside_block(index):
     return (index // CHUNK * 2 + lax.axis_index("c")) * CHUNK + index % CHUNK
 
@@ -72,7 +77,7 @@
     key = lax.broadcasted_iota(jnp.int32, (KEYS, HD), 0)
     lane = lax.broadcasted_iota(jnp.int32, (KEYS, HD), 1)
     slot = key // HALF
-    block = slot // NX * 8 + zh * 4 + slot % NX
+    block = swapped(slot // NX) * 8 + zh * 4 + slot % NX
     doc = document(block * TOK + inside_block(key % HALF))
     barred = (lane < OWN) & (lane != doc)
     barred = barred | ((lane == OWN) & (block >= own)) | ((lane == OTHER) & (block > other))
@@ -84,7 +89,7 @@
     queries = jnp.concatenate([q[...] for q in (q0, q1, q2, q3)], axis=0)
     queries = jnp.concatenate([queries, row_mask_ref[...]], axis=1)
     own = 2 * TOK
-    slot = lax.axis_index("y") * NX + lax.axis_index("x")
+    slot = swapped(lax.axis_index("y")) * NX + lax.axis_index("x")
     mask = key_mask_ref[pl.ds(pl.multiple_of(slot * HALF, HALF), HALF), :]
     feature = lax.broadcasted_iota(jnp.int32, (HALF, HD), 1)
     mask = jnp.where(feature == OWN, 0.0, mask.astype(jnp.float32)).astype(jnp.bfloat16)
@@ -170,7 +175,8 @@
         sums = jnp.dot(both, probs_ref[:, first : first + 2 * HALF], preferred_element_type=jnp.float32)
         line = jnp.sum(sums, axis=0, keepdims=True)
         pair = [jnp.broadcast_to(line[:, i * HALF : (i + 1) * HALF], (NZL, HALF)) for i in range(2)]
-        cols_ref[b * NZL : (b + 2) * NZL, :] = jnp.concatenate(pair, axis=0)
+        source = swapped(b // NX) * NX + b % NX
+        cols_ref[source * NZL : (source + 2) * NZL, :] = jnp.concatenate(pair, axis=0)
 
 
 def merge_kernel(keep_ref, got_ref, pair_ref, plane_ref, out_ref):
@@ -217,7 +223,7 @@
         limit=60,
         space=ANY,
     )(keys.reshape(NZL, 2, CHUNK, HD), values.reshape(NZL, 2, CHUNK, HD)).reshape(BLOCKS, 2, HALF, HD)
-    near = lax.all_to_all(copies, ("y", "x"), 0, 0, tiled=True)
+    near = lax.all_to_all(copies, ("y", "x"), 0, 0, axis_index_groups=[ORDER], tiled=True)
     q1, q2 = across(queries), partner(queries)
     q3 = across(q2)
     own, row_mask, key_mask = kernel(

time: 56.3 us -> 56.2 us (level)
  starting transfers between devices: 31.8 us -> 31 us
    ppermute x4, starting transfers between devices: 5.93 us -> 5.34 us  [across(): return lax.ppermute(x, 'c', [(0, 1), (1, 0)])]
  transfers between devices with their start and end apart: 9 -> 9, of which waited for: 3 -> 3; matrix products, arithmetic and copies ran while one was open for 0% -> 0% of each run, Pallas kernels for 9% -> 10%
where the time goes in v11:
time: 56.2 us; the launch traced here: 55.8 us
  starting transfers between devices  31 us (55%)
  waiting for transfers between devices  11.6 us (21%)
  Pallas kernels  10.4 us (19%)
  local copies, waits for them, and re-layouts  1.49 us (3%)
  between operations  0.71 us (1%)
  other arithmetic  0.67 us (1%)
    ppermute x3, starting transfers between devices, partner(): return lax.ppermute(x, ('zh', 'zl', 'c'), [(i, i ^ 12) for i in range(16)])  13.5 us
    all_to_all x1, waiting for transfers between devices, body(): lax.all_to_all(cols.reshape(BLOCKS * NZL, 1, HALF), ('y', 'x', 'zl'), 0,...  7.86 us
    all_to_all x1, starting transfers between devices, body(): lax.all_to_all(copies, ('y', 'x'), 0, 0, axis_index_groups=[ORDER], tiled...  7.6 us
    ppermute x4, starting transfers between devices, across(): return lax.ppermute(x, 'c', [(0, 1), (1, 0)])  5.34 us
    all_to_all x1, starting transfers between devices, body(): lax.all_to_all(cols.reshape(BLOCKS * NZL, 1, HALF), ('y', 'x', 'zl'), 0,...  4.54 us
    pallas_call x1, Pallas kernels, body(): kernel(score_kernel, 'scores', (shape((ROWS, KEYS), bf16), shape((2, ROWS...  2.9 us
    all_to_all x1, waiting for transfers between devices, body(): lax.all_to_all(copies, ('y', 'x'), 0, 0, axis_index_groups=[ORDER], tiled...  2.73 us
    pallas_call x1, Pallas kernels, body(): kernel(limit_kernel, 'limits', (shape((TOK, HD), bf16), shape((ROWS, HD),...  2.14 us
  transfers between devices with their start and end apart: 9, of which 3 were waited for; matrix products, arithmetic and copies ran while one was open for 0% of the time, Pallas kernels for 10%

profile of v11, /device:TPU:1, one launch (start us, length us, event | category | flops | bytes accessed | tf_op | source)
XLA Modules:
  0.0 55.8 jit_solution(6391027008141780117)
XLA Ops:
  0.6 1.9 %spread.1 = bf16[16,2,4,32,128]{4,3,2,1,0:T(8,128)(2,1)} custom-call(bf16[4,2,32,128]{3,2,1,0:T(8,128)(2,1)} %bitcast.7, bf16[4,2,32,128]{3,2,1,0:T(8,128)(2,1)} %bitcast.8), custom_call_target="tpu_custom_call" | custom-call | tf_op jit(solution)/shard_map/spread/pallas_call | solution.py:213
  2.5 7.6 %all-to-all-start = ((bf16[16,2,128,128]{3,2,1,0:T(8,128)(2,1)}), bf16[16,2,128,128]{3,2,1,0:T(8,128)(2,1)S(1)}, u32[]{:S(2)}, u32[]{:S(2)}) async-start(bf16[16,2,128,128]{3,2,1,0:T(8,128)(2,1)} %bitcast.6), calls=%async_computation | async-start | bytes 2097152 | tf_op jit(solution)/shard_map/all_to_all | solution.py:226
  10.2 6.1 %collective-permute-start.1 = (bf16[256,128]{1,0:T(8,128)(2,1)}, bf16[256,128]{1,0:T(8,128)(2,1)S(1)}, u32[]{:S(2)}, u32[]{:S(2)}) collective-permute-start(bf16[256,128]{1,0:T(8,128)(2,1)} %own_ref.1), channel_id=1, source_target_pairs={{0,36},{1,37},{2,38},{3,39},{4,32},{5,33},{6,34},{7,35},{32,4},{33... | collective-permute-start | bytes 196616 | tf_op jit(solution)/shard_map/ppermute | solution.py:211
  16.3 1.2 %collective-permute-start = (bf16[256,128]{1,0:T(8,128)(2,1)}, bf16[256,128]{1,0:T(8,128)(2,1)S(1)}, u32[]{:S(2)}, u32[]{:S(2)}) collective-permute-start(bf16[256,128]{1,0:T(8,128)(2,1)} %own_ref.1), channel_id=1, source_target_pairs={{0,1},{1,0},{2,3},{3,2},{4,5},{5,4},{6,7},{7,6},{8,9},{9,8},{10,11... | collective-permute-start | bytes 196616 | tf_op jit(solution)/shard_map/ppermute | solution.py:208
  17.5 0.9 %collective-permute-done.1.q2 = bf16[256,128]{1,0:T(8,128)(2,1)S(1)} collective-permute-done((bf16[256,128]{1,0:T(8,128)(2,1)}, bf16[256,128]{1,0:T(8,128)(2,1)S(1)}, u32[]{:S(2)}, u32[]{:S(2)}) %collective-permute-start.1) | collective-permute-done | bytes 65568 | tf_op jit(solution)/shard_map/ppermute | solution.py:211
  18.4 1.9 %collective-permute-start.2 = (bf16[256,128]{1,0:T(8,128)(2,1)S(1)}, bf16[256,128]{1,0:T(8,128)(2,1)S(1)}, u32[]{:S(2)}, u32[]{:S(2)}) collective-permute-start(bf16[256,128]{1,0:T(8,128)(2,1)S(1)} %collective-permute-done.1.q2), channel_id=1, source_target_pairs={{0,1},{1,0},{2,3},{3,2},{4,5},{5,4},{6,7},{7,6},{8,9},{9,8},{10,11... | collective-permute-start | bytes 196616 | tf_op jit(solution)/shard_map/ppermute | solution.py:208
  20.3 0.8 %copy-done = bf16[256,128]{1,0:T(8,128)(2,1)S(1)} copy-done((bf16[256,128]{1,0:T(8,128)(2,1)S(1)}, bf16[256,128]{1,0:T(8,128)(2,1)}, u32[]{:S(2)}) %copy-start) | copy-done | bytes 65560
  21.2 0.7 %copy-done.1 = s32[4]{0:T(128)S(1)} copy-done((s32[4]{0:T(128)S(1)}, s32[4]{0:T(128)}, u32[]{:S(2)}) %copy-start.1) | copy-done | bytes 40
  21.8 2.1 %limits.1 = (bf16[256,128]{1,0:T(8,128)(2,1)S(1)}, bf16[1024,128]{1,0:T(8,128)(2,1)S(1)}, bf16[2048,128]{1,0:T(8,128)(2,1)S(1)}) custom-call(s32[4]{0:T(128)S(1)} %copy-done.1, bf16[256,128]{1,0:T(8,128)(2,1)S(1)} %copy-done), custom_call_target="tpu_custom_call" | custom-call | tf_op jit(solution)/shard_map/limits/pallas_call | solution.py:229
  24.0 2.7 %all-to-all-done.near_ref = bf16[16,2,128,128]{3,2,1,0:T(8,128)(2,1)S(1)} async-done(((bf16[16,2,128,128]{3,2,1,0:T(8,128)(2,1)}), bf16[16,2,128,128]{3,2,1,0:T(8,128)(2,1)S(1)}, u32[]{:S(2)}, u32[]{:S(2)}) %all-to-all-start) | async-done | bytes 1048608 | tf_op jit(solution)/shard_map/all_to_all | solution.py:226
  26.7 2.9 %scores.1 = (bf16[1024,2048]{1,0:T(8,128)(2,1)S(1)}, f32[2,1024]{1,0:T(2,128)S(1)}) custom-call(bf16[16,2,128,128]{3,2,1,0:T(8,128)(2,1)S(1)} %all-to-all-done.near_ref, bf16[256,128]{1,0:T(8,128)(2,1)S(1)} %get-tuple-element.21.q0, bf16[256,128]{1,0:T(8,128)(2,1)S(1)} %collective-permute-done.q1, bf16[256,128]{1,0:T(8,128)(2,1)S(1)} %collective-permute-done.1.q2, ...), custom_call_target="tpu_custom_call" | custom-call | tf_op jit(solution)/shard_map/scores/pallas_call | solution.py:238
  29.6 2.1 %collective-permute-start.4 = (f32[2,1024]{1,0:T(2,128)S(1)}, f32[2,1024]{1,0:T(2,128)S(1)}, u32[]{:S(2)}, u32[]{:S(2)}) collective-permute-start(f32[2,1024]{1,0:T(2,128)S(1)} %get-tuple-element.28.mine_ref), channel_id=1, source_target_pairs={{0,1},{1,0},{2,3},{3,2},{4,5},{5,4},{6,7},{7,6},{8,9},{9,8},{10,11... | collective-permute-start | bytes 24584 | tf_op jit(solution)/shard_map/ppermute | solution.py:208
  31.7 0.7 %rows_sent.1.send_ref = bf16[2,256,128]{2,1,0:T(8,128)(2,1)S(1)} custom-call(bf16[1024,2048]{1,0:T(8,128)(2,1)S(1)} %get-tuple-element.27.probs_ref, bf16[16,2,128,128]{3,2,1,0:T(8,128)(2,1)S(1)} %all-to-all-done.near_ref), custom_call_target="tpu_custom_call" | custom-call | flops 20000000000 | tf_op jit(solution)/shard_map/rows_sent/pallas_call | solution.py:247
  32.4 0.1 collective-permute-start.3
  32.5 0.0 collective-permute-done.4.core_ref
  32.6 6.1 %collective-permute-start.6 = (f32[2,1024]{1,0:T(2,128)S(1)}, f32[2,1024]{1,0:T(2,128)S(1)}, u32[]{:S(2)}, u32[]{:S(2)}) collective-permute-start(f32[2,1024]{1,0:T(2,128)S(1)} %pair.1.pair_ref), channel_id=1, source_target_pairs={{0,36},{1,37},{2,38},{3,39},{4,32},{5,33},{6,34},{7,35},{32,4},{33... | collective-permute-start | bytes 24584 | tf_op jit(solution)/shard_map/ppermute | solution.py:211
  38.7 0.7 %rows_joined.1 = (f32[256,128]{1,0:T(8,128)S(1)}, bf16[256,128]{1,0:T(8,128)(2,1)S(1)}) custom-call(bf16[1024,2048]{1,0:T(8,128)(2,1)S(1)} %get-tuple-element.27.probs_ref, bf16[16,2,128,128]{3,2,1,0:T(8,128)(2,1)S(1)} %all-to-all-done.near_ref, bf16[2,256,128]{2,1,0:T(8,128)(2,1)S(1)} %collective-permute-done.3.got_ref, ...), custom_call_target="tpu_custom_call" | custom-call | flops 20000000000 | tf_op jit(solution)/shard_map/rows_joined/pallas_call | solution.py:250
  39.4 1.3 %collective-permute-start.5 = (bf16[256,128]{1,0:T(8,128)(2,1)S(1)}, bf16[256,128]{1,0:T(8,128)(2,1)S(1)}, u32[]{:S(2)}, u32[]{:S(2)}) collective-permute-start(bf16[256,128]{1,0:T(8,128)(2,1)S(1)} %get-tuple-element.30.send_ref), channel_id=1, source_target_pairs={{0,36},{1,37},{2,38},{3,39},{4,32},{5,33},{6,34},{7,35},{32,4},{33... | collective-permute-start | bytes 196616 | tf_op jit(solution)/shard_map/ppermute | solution.py:211
  40.7 1.3 %columns.1 = f32[64,128]{1,0:T(8,128)} custom-call(bf16[1024,2048]{1,0:T(8,128)(2,1)S(1)} %get-tuple-element.27.probs_ref, f32[2,1024]{1,0:T(2,128)S(1)} %get-tuple-element.28.mine_ref, f32[2,1024]{1,0:T(2,128)S(1)} %pair.1.pair_ref, f32[2,1024]{1,0:T(2,128)S(1)} %collective-permute-done.6.plane_ref, bf16[256,128]{1,0:T(8,128)(2,1)S(1)} %get-tuple-element.30.send_ref), custom_call_target="tpu_custom_call" | custom-call | flops 20000000000 | tf_op jit(solution)/shard_map/columns/pallas_call | solution.py:254
  41.9 4.5 %all-to-all-start.1 = ((f32[64,1,128]{2,1,0:T(1,128)}), f32[64,1,128]{2,1,0:T(1,128)S(1)}, u32[]{:S(2)}, u32[]{:S(2)}) async-start(f32[64,1,128]{2,1,0:T(1,128)} %bitcast.4), calls=%async_computation.1 | async-start | bytes 65536 | tf_op jit(solution)/shard_map/all_to_all | solution.py:257
  46.5 0.8 %merge.1 = bf16[256,128]{1,0:T(8,128)(2,1)} custom-call(f32[256,128]{1,0:T(8,128)S(1)} %get-tuple-element.29.keep_ref, bf16[256,128]{1,0:T(8,128)(2,1)S(1)} %collective-permute-done.5.got_ref, f32[2,1024]{1,0:T(2,128)S(1)} %pair.1.pair_ref, f32[2,1024]{1,0:T(2,128)S(1)} %collective-permute-done.6.plane_ref), custom_call_target="tpu_custom_call" | custom-call | flops 20000000000 | tf_op jit(solution)/shard_map/merge/pallas_call | solution.py:258
  47.3 7.9 %all-to-all-done.1 = f32[64,1,128]{2,1,0:T(1,128)S(1)} async-done(((f32[64,1,128]{2,1,0:T(1,128)}), f32[64,1,128]{2,1,0:T(1,128)S(1)}, u32[]{:S(2)}, u32[]{:S(2)}) %all-to-all-start.1) | async-done | bytes 32800 | tf_op jit(solution)/shard_map/all_to_all | solution.py:257
  55.2 0.2 dynamic-slice_reduce_fusion
  55.3 0.5 broadcast_multiply_fusion
  (8 shorter events, 0.0 us)
Async XLA Ops:
  2.5 24.2 %all-to-all-start = ((bf16[16,2,128,128]{3,2,1,0:T(8,128)(2,1)}), bf16[16,2,128,128]{3,2,1,0:T(8,128)(2,1)S(1)}, u32[]{:S(2)}, u32[]{:S(2)}) async-start(bf16[16,2,128,128]{3,2,1,0:T(8,128)(2,1)} %bitcast.6), calls=%async_computation | async-start | bytes 2097152 | tf_op jit(solution)/shard_map/all_to_all | solution.py:226
  10.2 8.3 %collective-permute-start.1 = (bf16[256,128]{1,0:T(8,128)(2,1)}, bf16[256,128]{1,0:T(8,128)(2,1)S(1)}, u32[]{:S(2)}, u32[]{:S(2)}) collective-permute-start(bf16[256,128]{1,0:T(8,128)(2,1)} %own_ref.1), channel_id=1, source_target_pairs={{0,36},{1,37},{2,38},{3,39},{4,32},{5,33},{6,34},{7,35},{32,4},{33... | collective-permute-start | bytes 196616 | tf_op jit(solution)/shard_map/ppermute | solution.py:211
  16.3 7.7 %collective-permute-start = (bf16[256,128]{1,0:T(8,128)(2,1)}, bf16[256,128]{1,0:T(8,128)(2,1)S(1)}, u32[]{:S(2)}, u32[]{:S(2)}) collective-permute-start(bf16[256,128]{1,0:T(8,128)(2,1)} %own_ref.1), channel_id=1, source_target_pairs={{0,1},{1,0},{2,3},{3,2},{4,5},{5,4},{6,7},{7,6},{8,9},{9,8},{10,11... | collective-permute-start | bytes 196616 | tf_op jit(solution)/shard_map/ppermute | solution.py:208
  18.4 5.6 %collective-permute-start.2 = (bf16[256,128]{1,0:T(8,128)(2,1)S(1)}, bf16[256,128]{1,0:T(8,128)(2,1)S(1)}, u32[]{:S(2)}, u32[]{:S(2)}) collective-permute-start(bf16[256,128]{1,0:T(8,128)(2,1)S(1)} %collective-permute-done.1.q2), channel_id=1, source_target_pairs={{0,1},{1,0},{2,3},{3,2},{4,5},{5,4},{6,7},{7,6},{8,9},{9,8},{10,11... | collective-permute-start | bytes 196616 | tf_op jit(solution)/shard_map/ppermute | solution.py:208
  20.3 0.8 %copy-start = (bf16[256,128]{1,0:T(8,128)(2,1)S(1)}, bf16[256,128]{1,0:T(8,128)(2,1)}, u32[]{:S(2)}) copy-start(bf16[256,128]{1,0:T(8,128)(2,1)} %own_ref.1) | copy-start | bytes 196612
  21.2 0.7 %copy-start.1 = (s32[4]{0:T(128)S(1)}, s32[4]{0:T(128)}, u32[]{:S(2)}) copy-start(s32[4]{0:T(128)} %docs_ref.1) | copy-start | bytes 52
  29.6 2.9 %collective-permute-start.4 = (f32[2,1024]{1,0:T(2,128)S(1)}, f32[2,1024]{1,0:T(2,128)S(1)}, u32[]{:S(2)}, u32[]{:S(2)}) collective-permute-start(f32[2,1024]{1,0:T(2,128)S(1)} %get-tuple-element.28.mine_ref), channel_id=1, source_target_pairs={{0,1},{1,0},{2,3},{3,2},{4,5},{5,4},{6,7},{7,6},{8,9},{9,8},{10,11... | collective-permute-start | bytes 24584 | tf_op jit(solution)/shard_map/ppermute | solution.py:208
  32.4 6.3 %collective-permute-start.3 = (bf16[2,256,128]{2,1,0:T(8,128)(2,1)S(1)}, bf16[2,256,128]{2,1,0:T(8,128)(2,1)S(1)}, u32[]{:S(2)}, u32[]{:S(2)}) collective-permute-start(bf16[2,256,128]{2,1,0:T(8,128)(2,1)S(1)} %rows_sent.1.send_ref), channel_id=1, source_target_pairs={{0,1},{1,0},{2,3},{3,2},{4,5},{5,4},{6,7},{7,6},{8,9},{9,8},{10,11... | collective-permute-start | bytes 393224 | tf_op jit(solution)/shard_map/ppermute | solution.py:208
  32.6 8.1 %collective-permute-start.6 = (f32[2,1024]{1,0:T(2,128)S(1)}, f32[2,1024]{1,0:T(2,128)S(1)}, u32[]{:S(2)}, u32[]{:S(2)}) collective-permute-start(f32[2,1024]{1,0:T(2,128)S(1)} %pair.1.pair_ref), channel_id=1, source_target_pairs={{0,36},{1,37},{2,38},{3,39},{4,32},{5,33},{6,34},{7,35},{32,4},{33... | collective-permute-start | bytes 24584 | tf_op jit(solution)/shard_map/ppermute | solution.py:211
  39.4 7.1 %collective-permute-start.5 = (bf16[256,128]{1,0:T(8,128)(2,1)S(1)}, bf16[256,128]{1,0:T(8,128)(2,1)S(1)}, u32[]{:S(2)}, u32[]{:S(2)}) collective-permute-start(bf16[256,128]{1,0:T(8,128)(2,1)S(1)} %get-tuple-element.30.send_ref), channel_id=1, source_target_pairs={{0,36},{1,37},{2,38},{3,39},{4,32},{5,33},{6,34},{7,35},{32,4},{33... | collective-permute-start | bytes 196616 | tf_op jit(solution)/shard_map/ppermute | solution.py:211
  41.9 13.2 %all-to-all-start.1 = ((f32[64,1,128]{2,1,0:T(1,128)}), f32[64,1,128]{2,1,0:T(1,128)S(1)}, u32[]{:S(2)}, u32[]{:S(2)}) async-start(f32[64,1,128]{2,1,0:T(1,128)} %bitcast.4), calls=%async_computation.1 | async-start | bytes 65536 | tf_op jit(solution)/shard_map/all_to_all | solution.py:257

commit v12 on v10

--- a/solution.py
+++ b/solution.py
@@ -19,7 +19,7 @@
 KEYS = BLOCKS * HALF
 FLIPS = 4
 ROWS = FLIPS * TOK
-TILE = 512
+TILE = 1024
 SCALE = math.log2(math.e) / math.sqrt(HD)
 OWN, OTHER = 4, 5
 BARRED = 32768.0

time: 56.3 us -> 56.3 us (level)
  no operation moved by 1% of the time
where the time goes in v12:
time: 56.3 us; the launch traced here: 56 us
  starting transfers between devices  31.8 us (56%)
  waiting for transfers between devices  11.3 us (20%)
  Pallas kernels  10.1 us (18%)
  local copies, waits for them, and re-layouts  1.49 us (3%)
  between operations  0.71 us (1%)
  other arithmetic  0.67 us (1%)
    ppermute x3, starting transfers between devices, partner(): return lax.ppermute(x, ('zh', 'zl', 'c'), [(i, i ^ 12) for i in range(16)])  13.5 us
    all_to_all x1, waiting for transfers between devices, body(): lax.all_to_all(cols.reshape(BLOCKS * NZL, 1, HALF), ('y', 'x', 'zl'), 0,...  7.86 us
    all_to_all x1, starting transfers between devices, body(): near = lax.all_to_all(copies, ('y', 'x'), 0, 0, tiled=True)  7.6 us
    ppermute x4, starting transfers between devices, across(): return lax.ppermute(x, 'c', [(0, 1), (1, 0)])  5.93 us
    all_to_all x1, starting transfers between devices, body(): lax.all_to_all(cols.reshape(BLOCKS * NZL, 1, HALF), ('y', 'x', 'zl'), 0,...  4.74 us
    pallas_call x1, Pallas kernels, body(): kernel(score_kernel, 'scores', (shape((ROWS, KEYS), bf16), shape((2, ROWS...  2.89 us
    all_to_all x1, waiting for transfers between devices, body(): near = lax.all_to_all(copies, ('y', 'x'), 0, 0, tiled=True)  2.49 us
    pallas_call x1, Pallas kernels, body(): kernel(spread_kernel, 'spread', shape((BLOCKS, 2, NZL, CHUNK, HD), bf16),...  1.91 us
  transfers between devices with their start and end apart: 9, of which 3 were waited for; matrix products, arithmetic and copies ran while one was open for 0% of the time, Pallas kernels for 9%

profile of v12, /device:TPU:1, one launch (start us, length us, event | category | flops | bytes accessed | tf_op | source)
XLA Modules:
  0.0 56.0 jit_solution(15109603423596679316)
XLA Ops:
  0.6 1.9 %spread.1 = bf16[16,2,4,32,128]{4,3,2,1,0:T(8,128)(2,1)} custom-call(bf16[4,2,32,128]{3,2,1,0:T(8,128)(2,1)} %bitcast.7, bf16[4,2,32,128]{3,2,1,0:T(8,128)(2,1)} %bitcast.8), custom_call_target="tpu_custom_call" | custom-call | tf_op jit(solution)/shard_map/spread/pallas_call | solution.py:207
  2.5 7.6 %all-to-all-start = ((bf16[16,2,128,128]{3,2,1,0:T(8,128)(2,1)}), bf16[16,2,128,128]{3,2,1,0:T(8,128)(2,1)S(1)}, u32[]{:S(2)}, u32[]{:S(2)}) async-start(bf16[16,2,128,128]{3,2,1,0:T(8,128)(2,1)} %bitcast.6), calls=%async_computation | async-start | bytes 2097152 | tf_op jit(solution)/shard_map/all_to_all | solution.py:220
  10.2 6.1 %collective-permute-start.1 = (bf16[256,128]{1,0:T(8,128)(2,1)}, bf16[256,128]{1,0:T(8,128)(2,1)S(1)}, u32[]{:S(2)}, u32[]{:S(2)}) collective-permute-start(bf16[256,128]{1,0:T(8,128)(2,1)} %own_ref.1), channel_id=1, source_target_pairs={{0,36},{1,37},{2,38},{3,39},{4,32},{5,33},{6,34},{7,35},{32,4},{33... | collective-permute-start | bytes 196616 | tf_op jit(solution)/shard_map/ppermute | solution.py:205
  16.3 1.2 %collective-permute-start = (bf16[256,128]{1,0:T(8,128)(2,1)}, bf16[256,128]{1,0:T(8,128)(2,1)S(1)}, u32[]{:S(2)}, u32[]{:S(2)}) collective-permute-start(bf16[256,128]{1,0:T(8,128)(2,1)} %own_ref.1), channel_id=1, source_target_pairs={{0,1},{1,0},{2,3},{3,2},{4,5},{5,4},{6,7},{7,6},{8,9},{9,8},{10,11... | collective-permute-start | bytes 196616 | tf_op jit(solution)/shard_map/ppermute | solution.py:202
  17.5 0.9 %collective-permute-done.1.q2 = bf16[256,128]{1,0:T(8,128)(2,1)S(1)} collective-permute-done((bf16[256,128]{1,0:T(8,128)(2,1)}, bf16[256,128]{1,0:T(8,128)(2,1)S(1)}, u32[]{:S(2)}, u32[]{:S(2)}) %collective-permute-start.1) | collective-permute-done | bytes 65568 | tf_op jit(solution)/shard_map/ppermute | solution.py:205
  18.4 1.9 %collective-permute-start.2 = (bf16[256,128]{1,0:T(8,128)(2,1)S(1)}, bf16[256,128]{1,0:T(8,128)(2,1)S(1)}, u32[]{:S(2)}, u32[]{:S(2)}) collective-permute-start(bf16[256,128]{1,0:T(8,128)(2,1)S(1)} %collective-permute-done.1.q2), channel_id=1, source_target_pairs={{0,1},{1,0},{2,3},{3,2},{4,5},{5,4},{6,7},{7,6},{8,9},{9,8},{10,11... | collective-permute-start | bytes 196616 | tf_op jit(solution)/shard_map/ppermute | solution.py:202
  20.3 0.8 %copy-done = bf16[256,128]{1,0:T(8,128)(2,1)S(1)} copy-done((bf16[256,128]{1,0:T(8,128)(2,1)S(1)}, bf16[256,128]{1,0:T(8,128)(2,1)}, u32[]{:S(2)}) %copy-start) | copy-done | bytes 65560
  21.2 0.7 %copy-done.1 = s32[4]{0:T(128)S(1)} copy-done((s32[4]{0:T(128)S(1)}, s32[4]{0:T(128)}, u32[]{:S(2)}) %copy-start.1) | copy-done | bytes 40
  21.8 1.8 %limits.1 = (bf16[256,128]{1,0:T(8,128)(2,1)S(1)}, bf16[1024,128]{1,0:T(8,128)(2,1)S(1)}, bf16[2048,128]{1,0:T(8,128)(2,1)S(1)}) custom-call(s32[4]{0:T(128)S(1)} %copy-done.1, bf16[256,128]{1,0:T(8,128)(2,1)S(1)} %copy-done), custom_call_target="tpu_custom_call" | custom-call | tf_op jit(solution)/shard_map/limits/pallas_call | solution.py:223
  23.7 2.5 %all-to-all-done.near_ref = bf16[16,2,128,128]{3,2,1,0:T(8,128)(2,1)S(1)} async-done(((bf16[16,2,128,128]{3,2,1,0:T(8,128)(2,1)}), bf16[16,2,128,128]{3,2,1,0:T(8,128)(2,1)S(1)}, u32[]{:S(2)}, u32[]{:S(2)}) %all-to-all-start) | async-done | bytes 1048608 | tf_op jit(solution)/shard_map/all_to_all | solution.py:220
  26.1 2.9 %scores.1 = (bf16[1024,2048]{1,0:T(8,128)(2,1)S(1)}, f32[2,1024]{1,0:T(2,128)S(1)}) custom-call(bf16[16,2,128,128]{3,2,1,0:T(8,128)(2,1)S(1)} %all-to-all-done.near_ref, bf16[256,128]{1,0:T(8,128)(2,1)S(1)} %get-tuple-element.21.q0, bf16[256,128]{1,0:T(8,128)(2,1)S(1)} %collective-permute-done.q1, bf16[256,128]{1,0:T(8,128)(2,1)S(1)} %collective-permute-done.1.q2, ...), custom_call_target="tpu_custom_call" | custom-call | tf_op jit(solution)/shard_map/scores/pallas_call | solution.py:232
  29.0 2.7 %collective-permute-start.4 = (f32[2,1024]{1,0:T(2,128)S(1)}, f32[2,1024]{1,0:T(2,128)S(1)}, u32[]{:S(2)}, u32[]{:S(2)}) collective-permute-start(f32[2,1024]{1,0:T(2,128)S(1)} %get-tuple-element.28.mine_ref), channel_id=1, source_target_pairs={{0,1},{1,0},{2,3},{3,2},{4,5},{5,4},{6,7},{7,6},{8,9},{9,8},{10,11... | collective-permute-start | bytes 24584 | tf_op jit(solution)/shard_map/ppermute | solution.py:202
  31.7 0.7 %rows_sent.1.send_ref = bf16[2,256,128]{2,1,0:T(8,128)(2,1)S(1)} custom-call(bf16[1024,2048]{1,0:T(8,128)(2,1)S(1)} %get-tuple-element.27.probs_ref, bf16[16,2,128,128]{3,2,1,0:T(8,128)(2,1)S(1)} %all-to-all-done.near_ref), custom_call_target="tpu_custom_call" | custom-call | flops 20000000000 | tf_op jit(solution)/shard_map/rows_sent/pallas_call | solution.py:241
  32.4 0.1 collective-permute-start.3
  32.5 0.0 collective-permute-done.4.core_ref
  32.6 6.1 %collective-permute-start.6 = (f32[2,1024]{1,0:T(2,128)S(1)}, f32[2,1024]{1,0:T(2,128)S(1)}, u32[]{:S(2)}, u32[]{:S(2)}) collective-permute-start(f32[2,1024]{1,0:T(2,128)S(1)} %pair.1.pair_ref), channel_id=1, source_target_pairs={{0,36},{1,37},{2,38},{3,39},{4,32},{5,33},{6,34},{7,35},{32,4},{33... | collective-permute-start | bytes 24584 | tf_op jit(solution)/shard_map/ppermute | solution.py:205
  38.7 0.7 %rows_joined.1 = (f32[256,128]{1,0:T(8,128)S(1)}, bf16[256,128]{1,0:T(8,128)(2,1)S(1)}) custom-call(bf16[1024,2048]{1,0:T(8,128)(2,1)S(1)} %get-tuple-element.27.probs_ref, bf16[16,2,128,128]{3,2,1,0:T(8,128)(2,1)S(1)} %all-to-all-done.near_ref, bf16[2,256,128]{2,1,0:T(8,128)(2,1)S(1)} %collective-permute-done.3.got_ref, ...), custom_call_target="tpu_custom_call" | custom-call | flops 20000000000 | tf_op jit(solution)/shard_map/rows_joined/pallas_call | solution.py:244
  39.4 1.3 %collective-permute-start.5 = (bf16[256,128]{1,0:T(8,128)(2,1)S(1)}, bf16[256,128]{1,0:T(8,128)(2,1)S(1)}, u32[]{:S(2)}, u32[]{:S(2)}) collective-permute-start(bf16[256,128]{1,0:T(8,128)(2,1)S(1)} %get-tuple-element.30.send_ref), channel_id=1, source_target_pairs={{0,36},{1,37},{2,38},{3,39},{4,32},{5,33},{6,34},{7,35},{32,4},{33... | collective-permute-start | bytes 196616 | tf_op jit(solution)/shard_map/ppermute | solution.py:205
  40.7 1.3 %columns.1 = f32[64,128]{1,0:T(8,128)} custom-call(bf16[1024,2048]{1,0:T(8,128)(2,1)S(1)} %get-tuple-element.27.probs_ref, f32[2,1024]{1,0:T(2,128)S(1)} %get-tuple-element.28.mine_ref, f32[2,1024]{1,0:T(2,128)S(1)} %pair.1.pair_ref, f32[2,1024]{1,0:T(2,128)S(1)} %collective-permute-done.6.plane_ref, bf16[256,128]{1,0:T(8,128)(2,1)S(1)} %get-tuple-element.30.send_ref), custom_call_target="tpu_custom_call" | custom-call | flops 20000000000 | tf_op jit(solution)/shard_map/columns/pallas_call | solution.py:248
  41.9 4.7 %all-to-all-start.1 = ((f32[64,1,128]{2,1,0:T(1,128)}), f32[64,1,128]{2,1,0:T(1,128)S(1)}, u32[]{:S(2)}, u32[]{:S(2)}) async-start(f32[64,1,128]{2,1,0:T(1,128)} %bitcast.4), calls=%async_computation.1 | async-start | bytes 65536 | tf_op jit(solution)/shard_map/all_to_all | solution.py:251
  46.7 0.8 %merge.1 = bf16[256,128]{1,0:T(8,128)(2,1)} custom-call(f32[256,128]{1,0:T(8,128)S(1)} %get-tuple-element.29.keep_ref, bf16[256,128]{1,0:T(8,128)(2,1)S(1)} %collective-permute-done.5.got_ref, f32[2,1024]{1,0:T(2,128)S(1)} %pair.1.pair_ref, f32[2,1024]{1,0:T(2,128)S(1)} %collective-permute-done.6.plane_ref), custom_call_target="tpu_custom_call" | custom-call | flops 20000000000 | tf_op jit(solution)/shard_map/merge/pallas_call | solution.py:252
  47.5 7.9 %all-to-all-done.1 = f32[64,1,128]{2,1,0:T(1,128)S(1)} async-done(((f32[64,1,128]{2,1,0:T(1,128)}), f32[64,1,128]{2,1,0:T(1,128)S(1)}, u32[]{:S(2)}, u32[]{:S(2)}) %all-to-all-start.1) | async-done | bytes 32800 | tf_op jit(solution)/shard_map/all_to_all | solution.py:251
  55.3 0.2 dynamic-slice_reduce_fusion
  55.5 0.5 broadcast_multiply_fusion
  (8 shorter events, 0.0 us)
Async XLA Ops:
  2.5 23.6 %all-to-all-start = ((bf16[16,2,128,128]{3,2,1,0:T(8,128)(2,1)}), bf16[16,2,128,128]{3,2,1,0:T(8,128)(2,1)S(1)}, u32[]{:S(2)}, u32[]{:S(2)}) async-start(bf16[16,2,128,128]{3,2,1,0:T(8,128)(2,1)} %bitcast.6), calls=%async_computation | async-start | bytes 2097152 | tf_op jit(solution)/shard_map/all_to_all | solution.py:220
  10.2 8.3 %collective-permute-start.1 = (bf16[256,128]{1,0:T(8,128)(2,1)}, bf16[256,128]{1,0:T(8,128)(2,1)S(1)}, u32[]{:S(2)}, u32[]{:S(2)}) collective-permute-start(bf16[256,128]{1,0:T(8,128)(2,1)} %own_ref.1), channel_id=1, source_target_pairs={{0,36},{1,37},{2,38},{3,39},{4,32},{5,33},{6,34},{7,35},{32,4},{33... | collective-permute-start | bytes 196616 | tf_op jit(solution)/shard_map/ppermute | solution.py:205
  16.3 7.4 %collective-permute-start = (bf16[256,128]{1,0:T(8,128)(2,1)}, bf16[256,128]{1,0:T(8,128)(2,1)S(1)}, u32[]{:S(2)}, u32[]{:S(2)}) collective-permute-start(bf16[256,128]{1,0:T(8,128)(2,1)} %own_ref.1), channel_id=1, source_target_pairs={{0,1},{1,0},{2,3},{3,2},{4,5},{5,4},{6,7},{7,6},{8,9},{9,8},{10,11... | collective-permute-start | bytes 196616 | tf_op jit(solution)/shard_map/ppermute | solution.py:202
  18.4 5.2 %collective-permute-start.2 = (bf16[256,128]{1,0:T(8,128)(2,1)S(1)}, bf16[256,128]{1,0:T(8,128)(2,1)S(1)}, u32[]{:S(2)}, u32[]{:S(2)}) collective-permute-start(bf16[256,128]{1,0:T(8,128)(2,1)S(1)} %collective-permute-done.1.q2), channel_id=1, source_target_pairs={{0,1},{1,0},{2,3},{3,2},{4,5},{5,4},{6,7},{7,6},{8,9},{9,8},{10,11... | collective-permute-start | bytes 196616 | tf_op jit(solution)/shard_map/ppermute | solution.py:202
  20.3 0.8 %copy-start = (bf16[256,128]{1,0:T(8,128)(2,1)S(1)}, bf16[256,128]{1,0:T(8,128)(2,1)}, u32[]{:S(2)}) copy-start(bf16[256,128]{1,0:T(8,128)(2,1)} %own_ref.1) | copy-start | bytes 196612
  21.2 0.7 %copy-start.1 = (s32[4]{0:T(128)S(1)}, s32[4]{0:T(128)}, u32[]{:S(2)}) copy-start(s32[4]{0:T(128)} %docs_ref.1) | copy-start | bytes 52
  29.0 3.5 %collective-permute-start.4 = (f32[2,1024]{1,0:T(2,128)S(1)}, f32[2,1024]{1,0:T(2,128)S(1)}, u32[]{:S(2)}, u32[]{:S(2)}) collective-permute-start(f32[2,1024]{1,0:T(2,128)S(1)} %get-tuple-element.28.mine_ref), channel_id=1, source_target_pairs={{0,1},{1,0},{2,3},{3,2},{4,5},{5,4},{6,7},{7,6},{8,9},{9,8},{10,11... | collective-permute-start | bytes 24584 | tf_op jit(solution)/shard_map/ppermute | solution.py:202
  32.4 6.3 %collective-permute-start.3 = (bf16[2,256,128]{2,1,0:T(8,128)(2,1)S(1)}, bf16[2,256,128]{2,1,0:T(8,128)(2,1)S(1)}, u32[]{:S(2)}, u32[]{:S(2)}) collective-permute-start(bf16[2,256,128]{2,1,0:T(8,128)(2,1)S(1)} %rows_sent.1.send_ref), channel_id=1, source_target_pairs={{0,1},{1,0},{2,3},{3,2},{4,5},{5,4},{6,7},{7,6},{8,9},{9,8},{10,11... | collective-permute-start | bytes 393224 | tf_op jit(solution)/shard_map/ppermute | solution.py:202
  32.6 8.1 %collective-permute-start.6 = (f32[2,1024]{1,0:T(2,128)S(1)}, f32[2,1024]{1,0:T(2,128)S(1)}, u32[]{:S(2)}, u32[]{:S(2)}) collective-permute-start(f32[2,1024]{1,0:T(2,128)S(1)} %pair.1.pair_ref), channel_id=1, source_target_pairs={{0,36},{1,37},{2,38},{3,39},{4,32},{5,33},{6,34},{7,35},{32,4},{33... | collective-permute-start | bytes 24584 | tf_op jit(solution)/shard_map/ppermute | solution.py:205
  39.4 7.3 %collective-permute-start.5 = (bf16[256,128]{1,0:T(8,128)(2,1)S(1)}, bf16[256,128]{1,0:T(8,128)(2,1)S(1)}, u32[]{:S(2)}, u32[]{:S(2)}) collective-permute-start(bf16[256,128]{1,0:T(8,128)(2,1)S(1)} %get-tuple-element.30.send_ref), channel_id=1, source_target_pairs={{0,36},{1,37},{2,38},{3,39},{4,32},{5,33},{6,34},{7,35},{32,4},{33... | collective-permute-start | bytes 196616 | tf_op jit(solution)/shard_map/ppermute | solution.py:205
  41.9 13.4 %all-to-all-start.1 = ((f32[64,1,128]{2,1,0:T(1,128)}), f32[64,1,128]{2,1,0:T(1,128)S(1)}, u32[]{:S(2)}, u32[]{:S(2)}) async-start(f32[64,1,128]{2,1,0:T(1,128)} %bitcast.4), calls=%async_computation.1 | async-start | bytes 65536 | tf_op jit(solution)/shard_map/all_to_all | solution.py:251
